TPU v7x, 128 devices: a whole 4x4x4 slice. The times are simulated.
128 devices in a mesh: replica: 4 (over z_lo, core), fsdp: 32 (over y, x, z_hi).
Axes of the slice: x: 4, y: 4, z: 4 (z_hi: 2, z_lo: 2; z = z_hi * 2 + z_lo), core: 2. Of those that a mesh axis runs over, the one named last changes fastest.
Arguments:
- tokens: bfloat16 [131072, 8192], P(('replica', 'fsdp')), may hold values from -24 to 24
- out_grad: bfloat16 [131072, 512], P(('replica', 'fsdp')), may hold values from -6 to 6
- inner_weights: float32 [4, 8192, 512], P('replica', 'fsdp'), may hold values from -6 to 6
- first_moment: float32 [4, 8192, 512], P('replica', 'fsdp'), may hold values from -4 to 4
- second_moment: float32 [4, 8192, 512], P('replica', 'fsdp'), may hold values from 0.25 to 4
- global_weights: float32 [8192, 512], P('fsdp'), may hold values from -6 to 6
- outer_momentum: float32 [8192, 512], P('fsdp'), may hold values from -6 to 6
Outputs:
- new_first: float32 [4, 8192, 512], P('replica', 'fsdp')
- new_second: float32 [4, 8192, 512], P('replica', 'fsdp')
- new_global: float32 [8192, 512], P('fsdp')
- new_momentum: float32 [8192, 512], P('fsdp')
- projected: bfloat16 [131072, 512], P(('replica', 'fsdp'))
All inputs are finite; a program needn't handle non-finite values.
Results may differ from a plain program's by a relative error of at most 0.0049.
Values may be sent and summed in bfloat16 or wider, within the bound.
No kernel may reach another device: no remote copies, remote signals or barrier semaphores. Data moves between devices by JAX's collectives and lax.ppermute only.
A program may use at most 128 MiB of HBM per device.

v0:
```python
import jax
import jax.numpy as jnp
from jax import lax
from jax.sharding import PartitionSpec as P


def body(
    tokens, out_grad, inner_weights, first_moment, second_moment, global_weights, outer_momentum
):
    width = tokens.shape[1]
    inv_root = 1.0 / width**0.5
    tok_cols = tokens
    grad = (
        lax.psum_scatter(
            lax.dot_general(
                tok_cols, out_grad, (((0,), (0,)), ((), ())), preferred_element_type=jnp.float32
            ),
            "fsdp",
            scatter_dimension=0,
            tiled=True,
        )
        * inv_root
    )
    first = 0.9 * first_moment[0] + 0.1 * grad
    second = 0.95 * second_moment[0] + 0.05 * grad * grad
    inner = inner_weights[0]
    stepped = inner - 0.25 * (first / (jnp.sqrt(second) + 1e-08) + 0.1 * inner)
    drift = global_weights - stepped
    n_replica = lax.axis_size("replica")
    pseudo = lax.psum(drift, "replica") / n_replica
    new_momentum = 0.9 * outer_momentum + pseudo
    new_global = global_weights - 0.7 * (pseudo + 0.9 * new_momentum)
    synced = new_global.astype(jnp.bfloat16)
    tok_cols = tokens
    summed = jnp.dot(
        tok_cols,
        lax.all_gather(synced, "fsdp", axis=0, tiled=True),
        preferred_element_type=jnp.float32,
    )
    projected = (summed * inv_root).astype(jnp.bfloat16)
    return (first[None], second[None], new_global, new_momentum, projected)


def solution(mesh):
    placed = (
        P(("replica", "fsdp"), None),
        P(("replica", "fsdp"), None),
        P("replica", "fsdp", None),
        P("replica", "fsdp", None),
        P("replica", "fsdp", None),
        P("fsdp", None),
        P("fsdp", None),
    )
    return jax.shard_map(
        body,
        mesh=mesh,
        in_specs=placed,
        out_specs=(
            P("replica", "fsdp", None),
            P("replica", "fsdp", None),
            P("fsdp", None),
            P("fsdp", None),
            P(("replica", "fsdp"), None),
        ),
        check_vma=False,
    )
```

profile of v0, /device:TPU:1, one launch (start us, length us, event | category | flops | bytes accessed | tf_op | source)
XLA Modules:
  0.0 563.4 jit_solution(17338934756618022745)
XLA Ops:
  7.2 0.0 copy-start
  7.2 0.0 reduce-scatter.2.cloned.1.call-start
  7.2 1.2 copy-done
  8.4 15.8 %fusion.7 = f32[8192,512]{1,0:T(8,128)} fusion(bf16[1024,8192]{1,0:T(8,128)(2,1)} %param.7, bf16[1024,512]{1,0:T(8,128)(2,1)S(1)} %copy-done), kind=kOutput, calls=%fused_computation.14 | convolution fusion | flops 8589934592 | bytes 34603008 | tf_op jit(solution)/shard_map/dot_general | solution.py:15
  24.2 0.0 copy-start.1
  24.2 0.0 copy-start.3
  24.2 0.0 copy-start.4
  24.2 0.0 copy-start.2
  24.2 0.0 reduce-scatter.2.cloned.1.call-update
  24.2 0.0 all-reduce.2.cloned.1.call-start
  24.3 364.2 %reduce-scatter.2.cloned.1.call-done = f32[256,512]{1,0:T(8,128)} async-done(((f32[8192,512]{1,0:T(8,128)}), f32[256,512]{1,0:T(8,128)}) %reduce-scatter.2.cloned.1.call-update) | async-done | bytes 524304 | tf_op jit(solution)/shard_map/reduce_scatter | solution.py:14
  388.5 0.0 copy-done.1
  388.5 0.0 copy-done.3
  388.5 0.0 copy-done.4
  388.5 2.6 fusion.3
  391.1 0.0 all-reduce.2.cloned.1.call-update
  391.1 0.0 all-gather.2.cloned.1.call-start
  391.1 40.7 %all-reduce.2.cloned.1.call-done = f32[256,512]{1,0:T(8,128)} async-done(((f32[256,512]{1,0:T(8,128)}), f32[256,512]{1,0:T(8,128)}) %all-reduce.2.cloned.1.call-update) | async-done | bytes 524304 | tf_op jit(solution)/shard_map/psum | solution.py:30
  431.8 0.0 copy-done.2
  431.8 2.3 fusion.6
  434.1 0.0 all-gather.2.cloned.1.call-update
  434.1 106.5 %all-gather.2.cloned.1.call-done = bf16[8192,512]{1,0:T(8,128)(2,1)} async-done(((bf16[256,512]{1,0:T(8,128)(2,1)}), bf16[8192,512]{1,0:T(8,128)(2,1)}) %all-gather.2.cloned.1.call-update) | async-done | bytes 8388624 | tf_op jit(solution)/shard_map/all_gather | solution.py:37
  540.7 14.9 %fusion = bf16[1024,512]{0,1:T(8,128)(2,1)S(1)} fusion(bf16[8192,512]{1,0:T(8,128)(2,1)} %all-gather.2.cloned.1.call-done, bf16[1024,8192]{1,0:T(8,128)(2,1)} %param.7), kind=kOutput, calls=%fused_computation.1 | convolution fusion | flops 8590983168 | bytes 26214400 | tf_op jit(solution)/shard_map/dot_general | solution.py:35
  555.5 1.3 copy.12
Async XLA Ops:
  7.2 1.2 copy-start
  7.2 381.3 %reduce-scatter.2.cloned.1.call-start = ((), (), s32[]{:S(2)}) async-start(), calls=%async_computation.1 | async-start | bytes 17301504 | tf_op jit(solution)/shard_map/reduce_scatter | solution.py:14
  24.2 364.3 %copy-start.1 = (f32[256,512]{1,0:T(8,128)S(1)}, f32[256,512]{1,0:T(8,128)}, u32[]{:S(2)}) copy-start(f32[256,512]{1,0:T(8,128)} %param.12) | copy-start | bytes 1572868
  24.2 364.3 %copy-start.3 = (f32[1,256,512]{2,1,0:T(8,128)S(1)}, f32[1,256,512]{2,1,0:T(8,128)}, u32[]{:S(2)}) copy-start(f32[1,256,512]{2,1,0:T(8,128)} %param.9) | copy-start | bytes 1572868
  24.2 364.3 %copy-start.4 = (f32[1,256,512]{2,1,0:T(8,128)S(1)}, f32[1,256,512]{2,1,0:T(8,128)}, u32[]{:S(2)}) copy-start(f32[1,256,512]{2,1,0:T(8,128)} %param.10) | copy-start | bytes 1572868
  24.2 407.7 %copy-start.2 = (f32[256,512]{1,0:T(8,128)S(1)}, f32[256,512]{1,0:T(8,128)}, u32[]{:S(2)}) copy-start(f32[256,512]{1,0:T(8,128)} %param.13) | copy-start | bytes 1572868
  24.2 407.6 %all-reduce.2.cloned.1.call-start = ((), (), s32[]{:S(2)}) async-start(), calls=%async_computation.2 | async-start | bytes 1048576 | tf_op jit(solution)/shard_map/psum | solution.py:30
  391.1 149.6 %all-gather.2.cloned.1.call-start = ((), (), s32[]{:S(2)}) async-start(), calls=%async_computation.3 | async-start | bytes 8650752 | tf_op jit(solution)/shard_map/all_gather | solution.py:37
Sparse Core Ops, SparseCore 0:
  24.3 364.0 reduce-scatter.1
  391.5 40.2 all-reduce.1
  435.4 105.1 all-gather.1
where the time goes:
time: 564 us; the launch traced here: 563 us
  waiting for transfers between devices  511 us (91%)
  matrix products  30.6 us (5%)
  between operations  13.8 us (2%)
    reduce_scatter x1, waiting for transfers between devices, body(): lax.psum_scatter(lax.dot_general(tok_cols, out_grad, (((0,), (0,)), ((),...  364 us
    all_gather x1, waiting for transfers between devices, body(): lax.all_gather(synced, 'fsdp', axis=0, tiled=True)  107 us
    psum x1, waiting for transfers between devices, body(): pseudo = lax.psum(drift, 'replica') / n_replica  40.7 us
    dot_general x1, matrix products, body(): lax.dot_general(tok_cols, out_grad, (((0,), (0,)), ((), ())), preferred_e...  15.8 us
    dot_general x1, matrix products, body(): jnp.dot(tok_cols, lax.all_gather(synced, 'fsdp', axis=0, tiled=True), pre...  14.9 us
  transfers between devices with their start and end apart: 3, of which 3 were waited for; matrix products, arithmetic and copies ran while one was open for 0% of the time, Pallas kernels for 0%

commit v1 on v0

v1 whole, which is shorter than its diff:
```python
import functools

import jax
import jax.numpy as jnp
from jax import lax
from jax.experimental import pallas as pl
from jax.experimental.pallas import tpu as pltpu
from jax.sharding import PartitionSpec as P

BOTH = ("replica", "fsdp")
BF16, F32 = jnp.bfloat16, jnp.float32
H1, H2 = (2, 1), (3, 0)


def flat(x, y, z, c):
    x, y, z = x % 4, y % 4, z % 4
    return ((z % 2) * 2 + c) * 32 + (y * 4 + x) * 2 + z // 2


def permute(array, move):
    pairs = [
        (flat(x, y, z, c), flat(*move(x, y, z, c)))
        for x in range(4)
        for y in range(4)
        for z in range(4)
        for c in range(2)
    ]
    return lax.ppermute(array, BOTH, pairs)


def along(axis, step):
    if axis == "x":
        return lambda x, y, z, c: (x + step, y, z, c)
    return lambda x, y, z, c: (x, y + step, z, c)


def other_core(x, y, z, c):
    return x, y, z, 1 - c


def pair_lo(x, y, z, c):
    return x, y, z ^ 1, c


def pair_hi(x, y, z, c):
    return x, y, 3 - z, c


def across(x, y, z, c):
    return x, y, z + 2, c


AXES = (("x", "y"), ("y", "x"))


def place():
    f = lax.axis_index("fsdp")
    return f // 8, (f // 2) % 4, f % 2


def numbers(blocks):
    y, x, _ = place()
    found = []
    for kind, k1, k2 in blocks:
        dx, dy = (k1, k2) if kind == 0 else (k2, k1)
        found.append((((y + dy) % 4) * 4 + (x + dx) % 4) * 2 + kind)
    return jnp.stack(found).astype(jnp.int32)


def grad_kernel(groups, size, n_recv, idx_ref, tok_ref, g_ref, *refs):
    recv, outs = refs[:n_recv], refs[n_recv:]
    step = pl.program_id(0)
    term = lax.dot_general(
        tok_ref[...], g_ref[...], (((0,), (0,)), ((), ())), preferred_element_type=F32
    )
    for group in range(groups):

        @pl.when(step // size == group)
        def _(group=group):
            total = term
            if n_recv:
                total = total + recv[group][0].astype(F32)
            outs[group][0] = total.astype(outs[group].dtype)


def grad_blocks(blocks, groups, tokens, out_grad, recv=(), dtype=BF16):
    size = len(blocks) // groups
    rows = tokens.shape[1] // 32
    cols = out_grad.shape[1]
    toks = tokens.shape[0]

    def part(group):
        return pl.BlockSpec(
            (1, rows, cols), lambda i, idx: (jnp.clip(i - group * size, 0, size - 1), 0, 0)
        )

    return pl.pallas_call(
        functools.partial(grad_kernel, groups, size, len(recv)),
        grid_spec=pltpu.PrefetchScalarGridSpec(
            num_scalar_prefetch=1,
            grid=(len(blocks),),
            in_specs=[
                pl.BlockSpec((toks, rows), lambda i, idx: (0, idx[i])),
                pl.BlockSpec((toks, cols), lambda i, idx: (0, 0)),
                *[part(group) for group in range(len(recv))],
            ],
            out_specs=[part(group) for group in range(groups)],
        ),
        out_shape=[jax.ShapeDtypeStruct((size, rows, cols), dtype) for _ in range(groups)],
        compiler_params=pltpu.CompilerParams(vmem_limit_bytes=50 << 20),
        cost_estimate=pl.CostEstimate(
            flops=2 * toks * rows * cols * len(blocks),
            bytes_accessed=2 * toks * rows * len(blocks),
            transcendentals=0,
        ),
    )(numbers(blocks), tokens, out_grad, *recv)


def project_kernel(sizes, has_acc, last, scale, idx_ref, core_ref, tok_ref, *refs):
    n = len(sizes)
    mine, theirs = refs[:n], refs[n : 2 * n]
    refs = refs[2 * n :]
    if has_acc:
        acc_in, refs = refs[0], refs[1:]
    out_ref = refs[0]
    acc = refs[1] if last else out_ref
    step = pl.program_id(0)

    @pl.when(step == 0)
    def _():
        if has_acc:
            acc[...] = acc_in[...]
        else:
            acc[...] = jnp.zeros_like(acc)

    start = 0
    for group, size in enumerate(sizes):

        @pl.when((step >= start) & (step < start + size))
        def _(group=group):
            acc[0] += jnp.dot(tok_ref[...], mine[group][0], preferred_element_type=F32)
            acc[1] += jnp.dot(tok_ref[...], theirs[group][0], preferred_element_type=F32)

        start += size
    if last:
        half = acc.shape[2]
        for core in range(2):

            @pl.when((step == start - 1) & (core_ref[0] == core))
            def _(core=core):
                out_ref[:, core * half : (core + 1) * half] = (acc[0] * scale).astype(BF16)
                out_ref[:, (1 - core) * half : (2 - core) * half] = (acc[1] * scale).astype(BF16)


def project_blocks(blocks, mine, theirs, acc, last, tokens, core, scale):
    sizes = [array.shape[0] for array in mine]
    toks = tokens.shape[0]
    rows, half = mine[0].shape[1:]

    def part(group):
        start, size = sum(sizes[:group]), sizes[group]
        return pl.BlockSpec(
            (1, rows, half), lambda i, idx, core: (jnp.clip(i - start, 0, size - 1), 0, 0)
        )

    parts = [part(group) for group in range(len(sizes))]
    whole = pl.BlockSpec((2, toks, half), lambda i, idx, core: (0, 0, 0))
    if last:
        out_shape = jax.ShapeDtypeStruct((toks, 2 * half), BF16)
        out_spec = pl.BlockSpec((toks, 2 * half), lambda i, idx, core: (0, 0))
    else:
        out_shape = jax.ShapeDtypeStruct((2, toks, half), F32)
        out_spec = whole
    carried = [] if acc is None else [acc]
    return pl.pallas_call(
        functools.partial(project_kernel, sizes, bool(carried), last, scale),
        grid_spec=pltpu.PrefetchScalarGridSpec(
            num_scalar_prefetch=2,
            grid=(sum(sizes),),
            in_specs=[
                pl.BlockSpec((toks, rows), lambda i, idx, core: (0, idx[i])),
                *parts,
                *parts,
                *[whole for _ in carried],
            ],
            out_specs=out_spec,
            scratch_shapes=[pltpu.VMEM((2, toks, half), F32)] if last else [],
        ),
        out_shape=out_shape,
        compiler_params=pltpu.CompilerParams(vmem_limit_bytes=50 << 20),
        cost_estimate=pl.CostEstimate(
            flops=4 * toks * rows * half * sum(sizes),
            bytes_accessed=2 * toks * rows * sum(sizes),
            transcendentals=0,
        ),
    )(numbers(blocks), core[None], tokens, *mine, *theirs, *carried)


def pick(k1, half):
    return [[(kind, k1, k2) for k2 in half] for kind in range(2)]


def reduce_scatter(tokens, out_grad):
    kinds = range(2)
    blocks = functools.partial(grad_blocks, tokens=tokens, out_grad=out_grad)

    def lay(forward, backward):
        order = []
        for kind in kinds:
            for k1, half in (forward, backward):
                order += [(kind, k1, k2) for k2 in half]
        return order

    def send(four):
        got = []
        for kind in kinds:
            axis = AXES[kind][0]
            got.append(permute(four[2 * kind], along(axis, 1)))
            got.append(permute(four[2 * kind + 1], along(axis, -1)))
        return got

    first = send(blocks(lay((2, H1), (2, H2)), 4))
    second = send(blocks(lay((1, H2), (3, H1)), 4))
    third = send(blocks(lay((1, H1), (3, H2)), 4, recv=first))
    own = blocks([(kind, 0, k2) for kind in kinds for k2 in H1 + H2], 2, dtype=F32)
    finals = []
    for kind in kinds:
        axis = AXES[kind][1]
        up2, down2 = second[2 * kind : 2 * kind + 2]
        up3, down3 = third[2 * kind : 2 * kind + 2]
        sums = {}
        for place_in, k2 in enumerate(H1):
            sums[k2] = (
                own[kind][place_in] + up3[place_in].astype(F32) + down2[place_in].astype(F32)
            )
        for place_in, k2 in enumerate(H2):
            sums[k2] = (
                own[kind][2 + place_in] + up2[place_in].astype(F32) + down3[place_in].astype(F32)
            )
        cut = sums[2].shape[0] // 2
        far = sums[2].astype(BF16)
        up = permute(far[:cut], along(axis, 1)).astype(F32)
        down = permute(far[cut:], along(axis, -1)).astype(F32)
        near = jnp.concatenate([sums[1][:cut] + up, sums[1][cut:]]).astype(BF16)
        back = jnp.concatenate([sums[3][:cut], sums[3][cut:] + down]).astype(BF16)
        finals.append(
            sums[0]
            + permute(near, along(axis, 1)).astype(F32)
            + permute(back, along(axis, -1)).astype(F32)
        )
    even = place()[2] == 0
    keep = jnp.where(even, finals[0], finals[1])
    give = jnp.where(even, finals[1], finals[0]).astype(BF16)
    return keep + permute(give, across).astype(F32)


def ring_gather(block, axis):
    behind = permute(block, along(axis, 1))
    ahead = permute(block, along(axis, -1))
    return behind, ahead


def gather_project(synced, tokens, core, scale):
    received = permute(synced, pair_hi)
    even = place()[2] == 0
    own = [jnp.where(even, synced, received), jnp.where(even, received, synced)]
    cut = synced.shape[0] // 2
    stacks = []
    for kind in range(2):
        axis = AXES[kind][0]
        behind, ahead = ring_gather(own[kind], axis)
        low = permute(behind[:cut], along(axis, 1))
        high = permute(ahead[cut:], along(axis, -1))
        stacks.append(jnp.stack([own[kind], behind, ahead, jnp.concatenate([low, high])]))
    order = (0, 3, 1, 2)

    def swap(arrays):
        return [permute(array, other_core) for array in arrays]

    run = functools.partial(project_blocks, tokens=tokens, core=core, scale=scale)
    acc = run(
        [(kind, k1, 0) for kind in range(2) for k1 in order], stacks, swap(stacks), None, False
    )
    behinds, aheads, near = [], [], []
    for kind in range(2):
        behind, ahead = ring_gather(stacks[kind], AXES[kind][1])
        behinds.append(behind)
        aheads.append(ahead)
        near += [behind, ahead]
    acc = run(
        [(kind, k1, k2) for kind in range(2) for k2 in (3, 1) for k1 in order],
        near,
        swap(near),
        acc,
        False,
    )
    far = []
    for kind in range(2):
        axis = AXES[kind][1]
        far.append(permute(behinds[kind][:2], along(axis, 1)))
        far.append(permute(aheads[kind][2:], along(axis, -1)))
    return run(
        [(kind, k1, 2) for kind in range(2) for k1 in order], far, swap(far), acc, True
    )


def body(
    tokens, out_grad, inner_weights, first_moment, second_moment, global_weights, outer_momentum
):
    scale = 1.0 / tokens.shape[1] ** 0.5
    core = (lax.axis_index("replica") % 2).astype(jnp.int32)
    grad = reduce_scatter(tokens, out_grad) * scale
    first = 0.9 * first_moment[0] + 0.1 * grad
    second = 0.95 * second_moment[0] + 0.05 * grad * grad
    inner = inner_weights[0]
    stepped = inner - 0.25 * (first / (jnp.sqrt(second) + 1e-08) + 0.1 * inner)
    drift = global_weights - stepped
    n_replica = lax.axis_size("replica")
    half = drift.shape[1] // 2

    def outer(total, weights, momentum):
        pseudo = total / n_replica
        new_momentum = 0.9 * momentum + pseudo
        return weights - 0.7 * (pseudo + 0.9 * new_momentum), new_momentum

    def columns(array, which):
        return lax.dynamic_slice_in_dim(array, which * half, half, axis=1)

    mine = columns(drift, core) + permute(columns(drift, 1 - core), other_core)
    mine = mine + permute(mine, pair_lo)
    synced = outer(mine, columns(global_weights, core), columns(outer_momentum, core))[0]
    theirs = permute(mine, other_core)
    total = jnp.where(
        core == 0,
        jnp.concatenate([mine, theirs], axis=1),
        jnp.concatenate([theirs, mine], axis=1),
    )
    new_global, new_momentum = outer(total, global_weights, outer_momentum)
    projected = gather_project(synced.astype(BF16), tokens, core, scale)
    return (first[None], second[None], new_global, new_momentum, projected)


def solution(mesh):
    placed = (
        P(("replica", "fsdp"), None),
        P(("replica", "fsdp"), None),
        P("replica", "fsdp", None),
        P("replica", "fsdp", None),
        P("replica", "fsdp", None),
        P("fsdp", None),
        P("fsdp", None),
    )
    return jax.shard_map(
        body,
        mesh=mesh,
        in_specs=placed,
        out_specs=(
            P("replica", "fsdp", None),
            P("replica", "fsdp", None),
            P("fsdp", None),
            P("fsdp", None),
            P(("replica", "fsdp"), None),
        ),
        check_vma=False,
    )
```

time: 564 us -> 196 us (0.35)
  waiting for transfers between devices: 511 us -> 25.7 us
  starting transfers between devices: 0.12 us -> 75.9 us
  Pallas kernels: 0 us -> 68.7 us
  matrix products: 30.6 us -> 0 us
  other arithmetic: 4.88 us -> 18 us
  between operations: 13.8 us -> 1.21 us
    reduce_scatter x1 -> x0, waiting for transfers between devices: 364 us -> none  [body(): lax.psum_scatter(lax.dot_general(tok_cols, out_grad, (((0,), (0,)), ((),...]
    all_gather x1 -> x0, waiting for transfers between devices: 107 us -> none  [body(): lax.all_gather(synced, 'fsdp', axis=0, tiled=True)]
    ppermute x0 -> x51, starting transfers between devices: none -> 75.9 us  [permute(): return lax.ppermute(array, BOTH, pairs)]
    pallas_call x0 -> x7, Pallas kernels: none -> 68.7 us  [the longest x4 35 us: grad_blocks(): pl.pallas_call(functools.partial(grad_kernel, groups, size, len(recv)), g...]
    psum x1 -> x0, waiting for transfers between devices: 40.7 us -> none  [body(): pseudo = lax.psum(drift, 'replica') / n_replica]
    dot_general x2 -> x0, matrix products: 30.6 us -> none  [the longest x1 15.8 us: body(): lax.dot_general(tok_cols, out_grad, (((0,), (0,)), ((), ())), preferred_e...]
    ppermute x0 -> x51, waiting for transfers between devices: none -> 25.7 us  [permute(): return lax.ppermute(array, BOTH, pairs)]
  transfers between devices with their start and end apart: 3 -> 51, of which waited for: 3 -> 10; matrix products, arithmetic and copies ran while one was open for 0% -> 5% of each run, Pallas kernels for 0% -> 26%
where the time goes in v1:
time: 196 us; the launch traced here: 195 us
  starting transfers between devices  75.9 us (39%)
  Pallas kernels  68.7 us (35%)
  waiting for transfers between devices  25.7 us (13%)
  other arithmetic  18 us (9%)
  local copies, waits for them, and re-layouts  5.26 us (3%)
    ppermute x51, starting transfers between devices, permute(): return lax.ppermute(array, BOTH, pairs)  75.9 us
    pallas_call x4, Pallas kernels, grad_blocks(): pl.pallas_call(functools.partial(grad_kernel, groups, size, len(recv)), g...  35 us
    pallas_call x3, Pallas kernels, project_blocks(): pl.pallas_call(functools.partial(project_kernel, sizes, bool(carried), la...  33.8 us
    ppermute x51, waiting for transfers between devices, permute(): return lax.ppermute(array, BOTH, pairs)  25.7 us
  transfers between devices with their start and end apart: 51, of which 10 were waited for; matrix products, arithmetic and copies ran while one was open for 5% of the time, Pallas kernels for 26%

profile of v1, /device:TPU:1, one launch (start us, length us, event | category | flops | bytes accessed | tf_op | source)
XLA Modules:
  0.0 194.8 jit_solution(9069360617677409372)
XLA Ops:
  0.9 1.2 copy-done
  2.1 8.6 %shard_map.112 = (bf16[2,256,512]{2,1,0:T(8,128)(2,1)}, bf16[2,256,512]{2,1,0:T(8,128)(2,1)}, bf16[2,256,512]{2,1,0:T(8,128)(2,1)}, bf16[2,256,512]{2,1,0:T(8,128)(2,1)S(1)}) custom-call(s32[8]{0:T(128)S(1)} %stack.214.idx_ref, bf16[1024,8192]{1,0:T(8,128)(2,1)} %tok_ref.13, bf16[1024,512]{1,0:T(8,128)(2,1)S(1)} %copy-done), custom_call_target="tpu_custom_call" | custom-call | flops 2147483648 | bytes 4194304 | tf_op jit(solution)/shard_map/pallas_call | solution.py:97
  10.7 2.0 %collective-permute-start.1 = (bf16[2,256,512]{2,1,0:T(8,128)(2,1)}, bf16[2,256,512]{2,1,0:T(8,128)(2,1)S(1)}, u32[]{:S(2)}, u32[]{:S(2)}) collective-permute-start(bf16[2,256,512]{2,1,0:T(8,128)(2,1)} %get-tuple-element.21), channel_id=1, source_target_pairs={{0,2},{32,34},{64,66},{96,98},{1,3},{33,35},{65,67},{97,99},{8,10}... | collective-permute-start | bytes 1572872 | tf_op jit(solution)/shard_map/ppermute | solution.py:28
  12.8 1.3 collective-permute-start.2
  14.0 1.5 collective-permute-start.3
  15.5 1.4 collective-permute-start.4
  17.0 8.7 %shard_map.111 = (bf16[2,256,512]{2,1,0:T(8,128)(2,1)}, bf16[2,256,512]{2,1,0:T(8,128)(2,1)}, bf16[2,256,512]{2,1,0:T(8,128)(2,1)}, bf16[2,256,512]{2,1,0:T(8,128)(2,1)}) custom-call(s32[8]{0:T(128)S(1)} %stack.196.idx_ref, bf16[1024,8192]{1,0:T(8,128)(2,1)} %tok_ref.13, bf16[1024,512]{1,0:T(8,128)(2,1)S(1)} %copy-done.1), custom_call_target="tpu_custom_call" | custom-call | flops 2147483648 | bytes 4194304 | tf_op jit(solution)/shard_map/pallas_call | solution.py:97
  25.7 1.3 collective-permute-start.12
  27.1 1.5 collective-permute-start.15
  28.7 2.5 %collective-permute-start.7 = (bf16[2,256,512]{2,1,0:T(8,128)(2,1)}, bf16[2,256,512]{2,1,0:T(8,128)(2,1)}, u32[]{:S(2)}, u32[]{:S(2)}) collective-permute-start(bf16[2,256,512]{2,1,0:T(8,128)(2,1)} %get-tuple-element.27), channel_id=1, source_target_pairs={{0,6},{32,38},{64,70},{96,102},{1,7},{33,39},{65,71},{97,103},{8,1... | collective-permute-start | bytes 1572872 | tf_op jit(solution)/shard_map/ppermute | solution.py:28
  31.3 9.3 %shard_map.113 = (bf16[2,256,512]{2,1,0:T(8,128)(2,1)}, bf16[2,256,512]{2,1,0:T(8,128)(2,1)}, bf16[2,256,512]{2,1,0:T(8,128)(2,1)}, bf16[2,256,512]{2,1,0:T(8,128)(2,1)}) custom-call(s32[8]{0:T(128)S(1)} %stack.205.idx_ref, bf16[1024,8192]{1,0:T(8,128)(2,1)} %tok_ref.13, bf16[1024,512]{1,0:T(8,128)(2,1)} %g_ref.7, ...), custom_call_target="tpu_custom_call" | custom-call | flops 2147483648 | bytes 4194304 | tf_op jit(solution)/shard_map/pallas_call | solution.py:97
  40.8 1.2 collective-permute-start.14
  42.1 1.4 collective-permute-start.6
  43.6 8.4 %shard_map.110 = (f32[4,256,512]{2,1,0:T(8,128)S(1)}, f32[4,256,512]{2,1,0:T(8,128)}) custom-call(s32[8]{0:T(128)S(1)} %stack.187.idx_ref, bf16[1024,8192]{1,0:T(8,128)(2,1)} %tok_ref.13, bf16[1024,512]{1,0:T(8,128)(2,1)S(1)} %copy-done.2), custom_call_target="tpu_custom_call" | custom-call | flops 2147483648 | bytes 4194304 | tf_op jit(solution)/shard_map/pallas_call | solution.py:97
  52.0 0.6 collective-permute-done.14
  52.6 0.8 collective-permute-done.6
  53.4 3.0 %convert_add_fusion.2 = (f32[1,256,512]{2,1,0:T(8,128)S(1)}, bf16[1,256,512]{2,1,0:T(8,128)(2,1)S(1)}, f32[1,256,512]{2,1,0:T(8,128)S(1)}, f32[1,256,512]{2,1,0:...) fusion(f32[4,256,512]{2,1,0:T(8,128)} %get-tuple-element.28, ...), kind=kLoop, calls=%fused_computation.21 | loop fusion | flops 3407872 | bytes 8912896 | tf_op jit(solution)/shard_map/add | solution.py:234
  56.4 0.3 collective-permute-start.16
  56.7 2.5 %collective-permute-start.18 = (bf16[128,512]{1,0:T(8,128)(2,1)S(1)}, bf16[128,512]{1,0:T(8,128)(2,1)S(1)}, u32[]{:S(2)}, u32[]{:S(2)}) collective-permute-start(bf16[128,512]{1,0:T(8,128)(2,1)S(1)} %get-tuple-element.50), channel_id=1, source_target_pairs={{0,6},{32,38},{64,70},{96,102},{1,7},{33,39},{65,71},{97,103},{8,1... | collective-permute-start | bytes 393224 | tf_op jit(solution)/shard_map/ppermute | solution.py:28
  59.3 0.5 collective-permute-start.8
  59.7 2.4 %collective-permute-start.10 = (bf16[128,512]{1,0:T(8,128)(2,1)S(1)}, bf16[128,512]{1,0:T(8,128)(2,1)S(1)}, u32[]{:S(2)}, u32[]{:S(2)}) collective-permute-start(bf16[128,512]{1,0:T(8,128)(2,1)S(1)} %get-tuple-element.52), channel_id=1, source_target_pairs={{0,24},{32,56},{64,88},{96,120},{1,25},{33,57},{65,89},{97,121},{8... | collective-permute-start | bytes 393224 | tf_op jit(solution)/shard_map/ppermute | solution.py:28
  62.2 0.7 pad_maximum_fusion.4
  62.9 0.7 pad_maximum_fusion.5
  63.7 2.7 %collective-permute-start.19 = (bf16[256,512]{1,0:T(8,128)(2,1)}, bf16[256,512]{1,0:T(8,128)(2,1)}, u32[]{:S(2)}, u32[]{:S(2)}) collective-permute-start(bf16[256,512]{1,0:T(8,128)(2,1)} %pad_maximum_fusion.5), channel_id=1, source_target_pairs={{0,6},{32,38},{64,70},{96,102},{1,7},{33,39},{65,71},{97,103},{8,1... | collective-permute-start | bytes 786440 | tf_op jit(solution)/shard_map/ppermute | solution.py:28
  66.4 0.7 pad_maximum_fusion.2
  67.1 0.7 pad_maximum_fusion.3
  67.9 2.7 %collective-permute-start.11 = (bf16[256,512]{1,0:T(8,128)(2,1)}, bf16[256,512]{1,0:T(8,128)(2,1)}, u32[]{:S(2)}, u32[]{:S(2)}) collective-permute-start(bf16[256,512]{1,0:T(8,128)(2,1)} %pad_maximum_fusion.3), channel_id=1, source_target_pairs={{0,24},{32,56},{64,88},{96,120},{1,25},{33,57},{65,89},{97,121},{8... | collective-permute-start | bytes 786440 | tf_op jit(solution)/shard_map/ppermute | solution.py:28
  70.5 3.5 %collective-permute-done.9 = bf16[256,512]{1,0:T(8,128)(2,1)} collective-permute-done((bf16[256,512]{1,0:T(8,128)(2,1)}, bf16[256,512]{1,0:T(8,128)(2,1)}, u32[]{:S(2)}, u32[]{:S(2)}) %collective-permute-start.9) | collective-permute-done | bytes 262176 | tf_op jit(solution)/shard_map/ppermute | solution.py:28
  74.2 2.7 %select_convert_fusion = bf16[256,512]{1,0:T(8,128)(2,1)} fusion(pred[]{:T(512)S(6)} %eq.146, bf16[256,512]{1,0:T(8,128)(2,1)} %collective-permute-done.11, bf16[256,512]{1,0:T(8,128)(2,1)} %collective-permute-done.9, bf16[2,256,512]{2,1,0:T(8,128)(2,1)} %collective-permute-done.5, bf16[2,256,512]{2,1,0:T(8,128)(2,1)} %collective-permute-done, ...), kind=kLoop, calls=%fused_computation.18 | loop fusion | flops 2359296 | bytes 3407873 | tf_op jit(solution)/shard_map/convert_element_type | solution.py:253
  76.8 3.6 %collective-permute-start.20 = (bf16[256,512]{1,0:T(8,128)(2,1)}, bf16[256,512]{1,0:T(8,128)(2,1)}, u32[]{:S(2)}, u32[]{:S(2)}) collective-permute-start(bf16[256,512]{1,0:T(8,128)(2,1)} %select_convert_fusion), channel_id=1, source_target_pairs={{0,1},{32,33},{64,65},{96,97},{1,0},{33,32},{65,64},{97,96},{8,9},... | collective-permute-start | bytes 786440 | tf_op jit(solution)/shard_map/ppermute | solution.py:28
  80.5 4.1 %collective-permute-done.20 = bf16[256,512]{1,0:T(8,128)(2,1)} collective-permute-done((bf16[256,512]{1,0:T(8,128)(2,1)}, bf16[256,512]{1,0:T(8,128)(2,1)}, u32[]{:S(2)}, u32[]{:S(2)}) %collective-permute-start.20) | collective-permute-done | bytes 262176 | tf_op jit(solution)/shard_map/ppermute | solution.py:28
  84.5 3.5 %fusion.3 = (f32[256,512]{1,0:T(8,128)S(1)}, f32[256,512]{1,0:T(8,128)}) fusion(f32[256,512]{1,0:T(8,128)S(1)} %copy-done.3, f32[1,256,512]{2,1,0:T(8,128)} %param.9, f32[1,256,512]{2,1,0:T(8,128)S(1)} %copy-done.5, f32[1,256,512]{2,1,0:T(8,128)} %param.11, bf16[256,512]{1,0:T(8,128)(2,1)} %collective-permute-done.20, ...), kind=kLoop, calls=%fused_computation.8 | loop fusion | flops 4456448 | bytes 6553601 | tf_op jit(solution)/shard_map/sub | solution.py:317
  88.0 0.8 copy-done.6
  88.8 8.4 %collective-permute-start.21 = (f32[256,256]{1,0:T(8,128)S(1)}, f32[256,256]{1,0:T(8,128)S(1)}, u32[]{:S(2)}, u32[]{:S(2)}) collective-permute-start(f32[256,256]{1,0:T(8,128)S(1)} %constant_dynamic-slice_fusion), channel_id=1, source_target_pairs={{0,32},{32,0},{64,96},{96,64},{1,33},{33,1},{65,97},{97,65},{8,40}... | collective-permute-start | bytes 786440 | tf_op jit(solution)/shard_map/ppermute | solution.py:28
  97.2 1.2 collective-permute-done.21
  98.3 1.0 dynamic-slice_add_fusion
  99.3 1.3 collective-permute-start.22
  100.7 6.3 %collective-permute-done.22 = f32[256,256]{1,0:T(8,128)S(1)} collective-permute-done((f32[256,256]{1,0:T(8,128)S(1)}, f32[256,256]{1,0:T(8,128)S(1)}, u32[]{:S(2)}, u32[]{:S(2)}) %collective-permute-start.22) | collective-permute-done | bytes 262176 | tf_op jit(solution)/shard_map/ppermute | solution.py:28
  106.9 1.0 subtract_convert_fusion
  108.0 3.5 %collective-permute-start.24 = (bf16[256,256]{1,0:T(8,128)(2,1)S(1)}, bf16[256,256]{1,0:T(8,128)(2,1)S(1)}, u32[]{:S(2)}, u32[]{:S(2)}) collective-permute-start(bf16[256,256]{1,0:T(8,128)(2,1)S(1)} %get-tuple-element.33), channel_id=1, source_target_pairs={{0,65},{32,97},{64,1},{96,33},{1,64},{33,96},{65,0},{97,32},{8,73}... | collective-permute-start | bytes 393224 | tf_op jit(solution)/shard_map/ppermute | solution.py:28
  111.5 2.4 %collective-permute-done.24 = bf16[256,256]{1,0:T(8,128)(2,1)S(1)} collective-permute-done((bf16[256,256]{1,0:T(8,128)(2,1)S(1)}, bf16[256,256]{1,0:T(8,128)(2,1)S(1)}, u32[]{:S(2)}, u32[]{:S(2)}) %collective-permute-start.24) | collective-permute-done | bytes 131104 | tf_op jit(solution)/shard_map/ppermute | solution.py:28
  113.9 3.5 %collective-permute-start.34 = (bf16[256,256]{1,0:T(8,128)(2,1)S(1)}, bf16[256,256]{1,0:T(8,128)(2,1)S(1)}, u32[]{:S(2)}, u32[]{:S(2)}) collective-permute-start(bf16[256,256]{1,0:T(8,128)(2,1)S(1)} %get-tuple-element.47), channel_id=1, source_target_pairs={{0,24},{32,56},{64,88},{96,120},{1,25},{33,57},{65,89},{97,121},{8... | collective-permute-start | bytes 393224 | tf_op jit(solution)/shard_map/ppermute | solution.py:28
  117.4 2.7 %collective-permute-start.26 = (bf16[256,256]{1,0:T(8,128)(2,1)S(1)}, bf16[256,256]{1,0:T(8,128)(2,1)S(1)}, u32[]{:S(2)}, u32[]{:S(2)}) collective-permute-start(bf16[256,256]{1,0:T(8,128)(2,1)S(1)} %get-tuple-element.48), channel_id=1, source_target_pairs={{0,6},{32,38},{64,70},{96,102},{1,7},{33,39},{65,71},{97,103},{8,1... | collective-permute-start | bytes 393224 | tf_op jit(solution)/shard_map/ppermute | solution.py:28
  120.2 2.7 %collective-permute-start.36 = (bf16[128,256]{1,0:T(8,128)(2,1)S(1)}, bf16[128,256]{1,0:T(8,128)(2,1)S(1)}, u32[]{:S(2)}, u32[]{:S(2)}) collective-permute-start(bf16[128,256]{1,0:T(8,128)(2,1)S(1)} %slice.261), channel_id=1, source_target_pairs={{0,24},{32,56},{64,88},{96,120},{1,25},{33,57},{65,89},{97,121},{8... | collective-permute-start | bytes 196616 | tf_op jit(solution)/shard_map/ppermute | solution.py:28
  123.0 2.7 %collective-permute-start.28 = (bf16[128,256]{1,0:T(8,128)(2,1)S(1)}, bf16[128,256]{1,0:T(8,128)(2,1)S(1)}, u32[]{:S(2)}, u32[]{:S(2)}) collective-permute-start(bf16[128,256]{1,0:T(8,128)(2,1)S(1)} %slice.257), channel_id=1, source_target_pairs={{0,6},{32,38},{64,70},{96,102},{1,7},{33,39},{65,71},{97,103},{8,1... | collective-permute-start | bytes 196616 | tf_op jit(solution)/shard_map/ppermute | solution.py:28
  125.9 2.7 %collective-permute-start.39 = (bf16[4,256,256]{2,1,0:T(8,128)(2,1)S(1)}, bf16[4,256,256]{2,1,0:T(8,128)(2,1)S(1)}, u32[]{:S(2)}, u32[]{:S(2)}) collective-permute-start(bf16[4,256,256]{2,1,0:T(8,128)(2,1)S(1)} %pad_maximum_fusion.1.refs_1_), channel_id=1, source_target_pairs={{0,6},{32,38},{64,70},{96,102},{1,7},{33,39},{65,71},{97,103},{8,1... | collective-permute-start | bytes 1572872 | tf_op jit(solution)/shard_map/ppermute | solution.py:28
  128.8 4.7 %collective-permute-start.50 = (bf16[4,256,256]{2,1,0:T(8,128)(2,1)S(1)}, bf16[4,256,256]{2,1,0:T(8,128)(2,1)}, u32[]{:S(2)}, u32[]{:S(2)}) collective-permute-start(bf16[4,256,256]{2,1,0:T(8,128)(2,1)S(1)} %pad_maximum_fusion.1.refs_1_), channel_id=1, source_target_pairs={{0,32},{32,0},{64,96},{96,64},{1,33},{33,1},{65,97},{97,65},{8,40}... | collective-permute-start | bytes 1572872 | tf_op jit(solution)/shard_map/ppermute | solution.py:28
  133.6 4.3 %collective-permute-done.37.refs_2_ = bf16[4,256,256]{2,1,0:T(8,128)(2,1)S(1)} collective-permute-done((bf16[4,256,256]{2,1,0:T(8,128)(2,1)S(1)}, bf16[4,256,256]{2,1,0:T(8,128)(2,1)S(1)}, u32[]{:S(2)}, u32[]{:S(2)}) %collective-permute-start.37) | collective-permute-done | bytes 524320 | tf_op jit(solution)/shard_map/ppermute | solution.py:28
  137.9 1.2 collective-permute-start.31
  139.1 4.9 %collective-permute-start.23 = (f32[256,256]{1,0:T(8,128)S(1)}, f32[256,256]{1,0:T(8,128)S(1)}, u32[]{:S(2)}, u32[]{:S(2)}) collective-permute-start(f32[256,256]{1,0:T(8,128)S(1)} %get-tuple-element.34), channel_id=1, source_target_pairs={{0,32},{32,0},{64,96},{96,64},{1,33},{33,1},{65,97},{97,65},{8,40}... | collective-permute-start | bytes 786440 | tf_op jit(solution)/shard_map/ppermute | solution.py:28
  143.9 0.7 slice.262
  144.7 0.7 slice.263
  145.4 0.7 copy-done.11
  146.1 2.0 %collective-permute-start.40 = (bf16[2,256,256]{2,1,0:T(8,128)(2,1)}, bf16[2,256,256]{2,1,0:T(8,128)(2,1)}, u32[]{:S(2)}, u32[]{:S(2)}) collective-permute-start(bf16[2,256,256]{2,1,0:T(8,128)(2,1)} %slice.263), channel_id=1, source_target_pairs={{0,6},{32,38},{64,70},{96,102},{1,7},{33,39},{65,71},{97,103},{8,1... | collective-permute-start | bytes 786440 | tf_op jit(solution)/shard_map/ppermute | solution.py:28
  148.5 0.9 collective-permute-start.47
  149.4 2.8 %collective-permute-start.48 = (bf16[4,256,256]{2,1,0:T(8,128)(2,1)S(1)}, bf16[4,256,256]{2,1,0:T(8,128)(2,1)S(1)}, u32[]{:S(2)}, u32[]{:S(2)}) collective-permute-start(bf16[4,256,256]{2,1,0:T(8,128)(2,1)S(1)} %collective-permute-done.39.refs_3_), channel_id=1, source_target_pairs={{0,32},{32,0},{64,96},{96,64},{1,33},{33,1},{65,97},{97,65},{8,40}... | collective-permute-start | bytes 1572872 | tf_op jit(solution)/shard_map/ppermute | solution.py:28
  152.2 2.4 %collective-permute-done.38.refs_2_ = bf16[2,256,256]{2,1,0:T(8,128)(2,1)S(1)} collective-permute-done((bf16[2,256,256]{2,1,0:T(8,128)(2,1)}, bf16[2,256,256]{2,1,0:T(8,128)(2,1)S(1)}, u32[]{:S(2)}, u32[]{:S(2)}) %collective-permute-start.38) | collective-permute-done | bytes 262176 | tf_op jit(solution)/shard_map/ppermute | solution.py:28
  154.7 0.9 collective-permute-start.45
  155.6 2.5 %fusion.19 = (f32[1,256,512]{2,1,0:T(8,128)}, f32[1,256,512]{2,1,0:T(8,128)}) fusion(f32[256,512]{1,0:T(8,128)} %get-tuple-element.38, f32[1,256,512]{2,1,0:T(8,128)} %param.11, f32[1,256,512]{2,1,0:T(8,128)} %param.10), kind=kLoop, calls=%fused_computation.60 | loop fusion | flops 1048576 | bytes 2621440 | tf_op jit(solution)/shard_map/broadcast_in_dim | solution.py:340
  158.2 1.2 multiply_subtract_fusion
  159.4 8.8 %shard_map.114.refs_8_ = f32[2,1024,256]{2,1,0:T(8,128)} custom-call(s32[8]{0:T(128)S(1)} %stack.227.idx_ref, s32[1]{0:T(128)} %bitcast.51.core_ref, bf16[1024,8192]{1,0:T(8,128)(2,1)} %tok_ref.13, bf16[4,256,256]{2,1,0:T(8,128)(2,1)S(1)} %pad_maximum_fusion.refs_0_, bf16[4,256,256]{2,1,0:T(8,128)(2,1)S(1)} %pad_maximum_fusion.1.refs_1_, ...), custom_call_target="tpu_custom_call" | custom-call | flops 2147483648 | bytes 4194304 | tf_op jit(solution)/shard_map/pallas_call | solution.py:175
  168.2 0.5 collective-permute-start.43
  169.8 15.7 %shard_map.115.refs_8_ = f32[2,1024,256]{2,1,0:T(8,128)} custom-call(s32[16]{0:T(128)S(1)} %stack.226.idx_ref, s32[1]{0:T(128)} %bitcast.51.core_ref, bf16[1024,8192]{1,0:T(8,128)(2,1)} %tok_ref.13, bf16[4,256,256]{2,1,0:T(8,128)(2,1)S(1)} %collective-permute-done.29.refs_0_, bf16[4,256,256]{2,1,0:T(8,128)(2,1)S(1)} %collective-permute-done.31.refs_1_, ...), custom_call_target="tpu_custom_call" | custom-call | flops 4294967296 | bytes 8388608 | tf_op jit(solution)/shard_map/pallas_call | solution.py:175
  185.5 9.3 %shard_map.116 = bf16[1024,512]{1,0:T(8,128)(2,1)} custom-call(s32[8]{0:T(128)S(1)} %stack.215.idx_ref, s32[1]{0:T(128)} %bitcast.51.core_ref, bf16[1024,8192]{1,0:T(8,128)(2,1)} %tok_ref.13, bf16[2,256,256]{2,1,0:T(8,128)(2,1)S(1)} %collective-permute-done.30.refs_0_, bf16[2,256,256]{2,1,0:T(8,128)(2,1)S(1)} %collective-permute-done.32.refs_1_, ...), custom_call_target="tpu_custom_call" | custom-call | flops 2147483648 | bytes 4194304 | tf_op jit(solution)/shard_map/pallas_call | solution.py:175
  (113 shorter events, 3.5 us)
Async XLA Ops:
  0.9 1.2 copy-start
  2.1 14.9 %copy-start.1 = (bf16[1024,512]{1,0:T(8,128)(2,1)S(1)}, bf16[1024,512]{1,0:T(8,128)(2,1)}, u32[]{:S(2)}) copy-start(bf16[1024,512]{1,0:T(8,128)(2,1)} %g_ref.7) | copy-start | bytes 3145732
  10.7 15.0 %collective-permute-start.1 = (bf16[2,256,512]{2,1,0:T(8,128)(2,1)}, bf16[2,256,512]{2,1,0:T(8,128)(2,1)S(1)}, u32[]{:S(2)}, u32[]{:S(2)}) collective-permute-start(bf16[2,256,512]{2,1,0:T(8,128)(2,1)} %get-tuple-element.21), channel_id=1, source_target_pairs={{0,2},{32,34},{64,66},{96,98},{1,3},{33,35},{65,67},{97,99},{8,10}... | collective-permute-start | bytes 1572872 | tf_op jit(solution)/shard_map/ppermute | solution.py:28
  12.8 14.3 %collective-permute-start.2 = (bf16[2,256,512]{2,1,0:T(8,128)(2,1)}, bf16[2,256,512]{2,1,0:T(8,128)(2,1)S(1)}, u32[]{:S(2)}, u32[]{:S(2)}) collective-permute-start(bf16[2,256,512]{2,1,0:T(8,128)(2,1)} %get-tuple-element.22), channel_id=1, source_target_pairs={{0,6},{32,38},{64,70},{96,102},{1,7},{33,39},{65,71},{97,103},{8,1... | collective-permute-start | bytes 1572872 | tf_op jit(solution)/shard_map/ppermute | solution.py:28
  14.0 14.7 %collective-permute-start.3 = (bf16[2,256,512]{2,1,0:T(8,128)(2,1)}, bf16[2,256,512]{2,1,0:T(8,128)(2,1)S(1)}, u32[]{:S(2)}, u32[]{:S(2)}) collective-permute-start(bf16[2,256,512]{2,1,0:T(8,128)(2,1)} %get-tuple-element.23), channel_id=1, source_target_pairs={{0,8},{32,40},{64,72},{96,104},{1,9},{33,41},{65,73},{97,105},{8,1... | collective-permute-start | bytes 1572872 | tf_op jit(solution)/shard_map/ppermute | solution.py:28
  15.5 15.7 %collective-permute-start.4 = (bf16[2,256,512]{2,1,0:T(8,128)(2,1)S(1)}, bf16[2,256,512]{2,1,0:T(8,128)(2,1)}, u32[]{:S(2)}, u32[]{:S(2)}) collective-permute-start(bf16[2,256,512]{2,1,0:T(8,128)(2,1)S(1)} %get-tuple-element.24), channel_id=1, source_target_pairs={{0,24},{32,56},{64,88},{96,120},{1,25},{33,57},{65,89},{97,121},{8... | collective-permute-start | bytes 1572872 | tf_op jit(solution)/shard_map/ppermute | solution.py:28
  25.7 15.1 %collective-permute-start = (bf16[2,256,512]{2,1,0:T(8,128)(2,1)}, bf16[2,256,512]{2,1,0:T(8,128)(2,1)}, u32[]{:S(2)}, u32[]{:S(2)}) collective-permute-start(bf16[2,256,512]{2,1,0:T(8,128)(2,1)} %get-tuple-element.20), channel_id=1, source_target_pairs={{0,2},{32,34},{64,66},{96,98},{1,3},{33,35},{65,67},{97,99},{8,10}... | collective-permute-start | bytes 1572872 | tf_op jit(solution)/shard_map/ppermute | solution.py:28
  25.7 16.3 %collective-permute-start.12 = (bf16[2,256,512]{2,1,0:T(8,128)(2,1)}, bf16[2,256,512]{2,1,0:T(8,128)(2,1)}, u32[]{:S(2)}, u32[]{:S(2)}) collective-permute-start(bf16[2,256,512]{2,1,0:T(8,128)(2,1)} %get-tuple-element.29), channel_id=1, source_target_pairs={{0,8},{32,40},{64,72},{96,104},{1,9},{33,41},{65,73},{97,105},{8,1... | collective-permute-start | bytes 1572872 | tf_op jit(solution)/shard_map/ppermute | solution.py:28
  27.1 15.0 %collective-permute-start.15 = (bf16[2,256,512]{2,1,0:T(8,128)(2,1)}, bf16[2,256,512]{2,1,0:T(8,128)(2,1)}, u32[]{:S(2)}, u32[]{:S(2)}) collective-permute-start(bf16[2,256,512]{2,1,0:T(8,128)(2,1)} %get-tuple-element.32), channel_id=1, source_target_pairs={{0,24},{32,56},{64,88},{96,120},{1,25},{33,57},{65,89},{97,121},{8... | collective-permute-start | bytes 1572872 | tf_op jit(solution)/shard_map/ppermute | solution.py:28
  28.7 14.9 %copy-start.2 = (bf16[1024,512]{1,0:T(8,128)(2,1)S(1)}, bf16[1024,512]{1,0:T(8,128)(2,1)}, u32[]{:S(2)}) copy-start(bf16[1024,512]{1,0:T(8,128)(2,1)} %g_ref.7) | copy-start | bytes 3145732
  28.7 23.3 %collective-permute-start.7 = (bf16[2,256,512]{2,1,0:T(8,128)(2,1)}, bf16[2,256,512]{2,1,0:T(8,128)(2,1)}, u32[]{:S(2)}, u32[]{:S(2)}) collective-permute-start(bf16[2,256,512]{2,1,0:T(8,128)(2,1)} %get-tuple-element.27), channel_id=1, source_target_pairs={{0,6},{32,38},{64,70},{96,102},{1,7},{33,39},{65,71},{97,103},{8,1... | collective-permute-start | bytes 1572872 | tf_op jit(solution)/shard_map/ppermute | solution.py:28
  40.5 11.4 %collective-permute-start.13 = (bf16[2,256,512]{2,1,0:T(8,128)(2,1)}, bf16[2,256,512]{2,1,0:T(8,128)(2,1)}, u32[]{:S(2)}, u32[]{:S(2)}) collective-permute-start(bf16[2,256,512]{2,1,0:T(8,128)(2,1)} %get-tuple-element.30), channel_id=1, source_target_pairs={{0,24},{32,56},{64,88},{96,120},{1,25},{33,57},{65,89},{97,121},{8... | collective-permute-start | bytes 1572872 | tf_op jit(solution)/shard_map/ppermute | solution.py:28
  40.8 11.8 %collective-permute-start.14 = (bf16[2,256,512]{2,1,0:T(8,128)(2,1)}, bf16[2,256,512]{2,1,0:T(8,128)(2,1)}, u32[]{:S(2)}, u32[]{:S(2)}) collective-permute-start(bf16[2,256,512]{2,1,0:T(8,128)(2,1)} %get-tuple-element.31), channel_id=1, source_target_pairs={{0,8},{32,40},{64,72},{96,104},{1,9},{33,41},{65,73},{97,105},{8,1... | collective-permute-start | bytes 1572872 | tf_op jit(solution)/shard_map/ppermute | solution.py:28
  42.0 10.5 %collective-permute-start.5 = (bf16[2,256,512]{2,1,0:T(8,128)(2,1)}, bf16[2,256,512]{2,1,0:T(8,128)(2,1)}, u32[]{:S(2)}, u32[]{:S(2)}) collective-permute-start(bf16[2,256,512]{2,1,0:T(8,128)(2,1)} %get-tuple-element.25), channel_id=1, source_target_pairs={{0,6},{32,38},{64,70},{96,102},{1,7},{33,39},{65,71},{97,103},{8,1... | collective-permute-start | bytes 1572872 | tf_op jit(solution)/shard_map/ppermute | solution.py:28
  42.1 11.3 %collective-permute-start.6 = (bf16[2,256,512]{2,1,0:T(8,128)(2,1)}, bf16[2,256,512]{2,1,0:T(8,128)(2,1)}, u32[]{:S(2)}, u32[]{:S(2)}) collective-permute-start(bf16[2,256,512]{2,1,0:T(8,128)(2,1)} %get-tuple-element.26), channel_id=1, source_target_pairs={{0,2},{32,34},{64,66},{96,98},{1,3},{33,35},{65,67},{97,99},{8,10}... | collective-permute-start | bytes 1572872 | tf_op jit(solution)/shard_map/ppermute | solution.py:28
  56.4 5.7 %collective-permute-start.16 = (bf16[128,512]{1,0:T(8,128)(2,1)S(1)}, bf16[128,512]{1,0:T(8,128)(2,1)S(1)}, u32[]{:S(2)}, u32[]{:S(2)}) collective-permute-start(bf16[128,512]{1,0:T(8,128)(2,1)S(1)} %get-tuple-element.49), channel_id=1, source_target_pairs={{0,2},{32,34},{64,66},{96,98},{1,3},{33,35},{65,67},{97,99},{8,10}... | collective-permute-start | bytes 393224 | tf_op jit(solution)/shard_map/ppermute | solution.py:28
  56.7 6.2 %collective-permute-start.18 = (bf16[128,512]{1,0:T(8,128)(2,1)S(1)}, bf16[128,512]{1,0:T(8,128)(2,1)S(1)}, u32[]{:S(2)}, u32[]{:S(2)}) collective-permute-start(bf16[128,512]{1,0:T(8,128)(2,1)S(1)} %get-tuple-element.50), channel_id=1, source_target_pairs={{0,6},{32,38},{64,70},{96,102},{1,7},{33,39},{65,71},{97,103},{8,1... | collective-permute-start | bytes 393224 | tf_op jit(solution)/shard_map/ppermute | solution.py:28
  59.3 7.1 %collective-permute-start.8 = (bf16[128,512]{1,0:T(8,128)(2,1)S(1)}, bf16[128,512]{1,0:T(8,128)(2,1)S(1)}, u32[]{:S(2)}, u32[]{:S(2)}) collective-permute-start(bf16[128,512]{1,0:T(8,128)(2,1)S(1)} %get-tuple-element.51), channel_id=1, source_target_pairs={{0,8},{32,40},{64,72},{96,104},{1,9},{33,41},{65,73},{97,105},{8,1... | collective-permute-start | bytes 393224 | tf_op jit(solution)/shard_map/ppermute | solution.py:28
  59.7 7.3 %collective-permute-start.10 = (bf16[128,512]{1,0:T(8,128)(2,1)S(1)}, bf16[128,512]{1,0:T(8,128)(2,1)S(1)}, u32[]{:S(2)}, u32[]{:S(2)}) collective-permute-start(bf16[128,512]{1,0:T(8,128)(2,1)S(1)} %get-tuple-element.52), channel_id=1, source_target_pairs={{0,24},{32,56},{64,88},{96,120},{1,25},{33,57},{65,89},{97,121},{8... | collective-permute-start | bytes 393224 | tf_op jit(solution)/shard_map/ppermute | solution.py:28
  62.9 7.6 %collective-permute-start.17 = (bf16[256,512]{1,0:T(8,128)(2,1)}, bf16[256,512]{1,0:T(8,128)(2,1)S(1)}, u32[]{:S(2)}, u32[]{:S(2)}) collective-permute-start(bf16[256,512]{1,0:T(8,128)(2,1)} %pad_maximum_fusion.4), channel_id=1, source_target_pairs={{0,2},{32,34},{64,66},{96,98},{1,3},{33,35},{65,67},{97,99},{8,10}... | collective-permute-start | bytes 786440 | tf_op jit(solution)/shard_map/ppermute | solution.py:28
  63.7 6.9 %collective-permute-start.19 = (bf16[256,512]{1,0:T(8,128)(2,1)}, bf16[256,512]{1,0:T(8,128)(2,1)}, u32[]{:S(2)}, u32[]{:S(2)}) collective-permute-start(bf16[256,512]{1,0:T(8,128)(2,1)} %pad_maximum_fusion.5), channel_id=1, source_target_pairs={{0,6},{32,38},{64,70},{96,102},{1,7},{33,39},{65,71},{97,103},{8,1... | collective-permute-start | bytes 786440 | tf_op jit(solution)/shard_map/ppermute | solution.py:28
  67.1 6.9 %collective-permute-start.9 = (bf16[256,512]{1,0:T(8,128)(2,1)}, bf16[256,512]{1,0:T(8,128)(2,1)}, u32[]{:S(2)}, u32[]{:S(2)}) collective-permute-start(bf16[256,512]{1,0:T(8,128)(2,1)} %pad_maximum_fusion.2), channel_id=1, source_target_pairs={{0,8},{32,40},{64,72},{96,104},{1,9},{33,41},{65,73},{97,105},{8,1... | collective-permute-start | bytes 786440 | tf_op jit(solution)/shard_map/ppermute | solution.py:28
  67.1 17.4 %copy-start.3 = (f32[256,512]{1,0:T(8,128)S(1)}, f32[256,512]{1,0:T(8,128)}, u32[]{:S(2)}) copy-start(f32[256,512]{1,0:T(8,128)} %param.12) | copy-start | bytes 1572868
  67.1 17.4 %copy-start.5 = (f32[1,256,512]{2,1,0:T(8,128)S(1)}, f32[1,256,512]{2,1,0:T(8,128)}, u32[]{:S(2)}) copy-start(f32[1,256,512]{2,1,0:T(8,128)} %param.10) | copy-start | bytes 1572868
  67.9 6.3 %collective-permute-start.11 = (bf16[256,512]{1,0:T(8,128)(2,1)}, bf16[256,512]{1,0:T(8,128)(2,1)}, u32[]{:S(2)}, u32[]{:S(2)}) collective-permute-start(bf16[256,512]{1,0:T(8,128)(2,1)} %pad_maximum_fusion.3), channel_id=1, source_target_pairs={{0,24},{32,56},{64,88},{96,120},{1,25},{33,57},{65,89},{97,121},{8... | collective-permute-start | bytes 786440 | tf_op jit(solution)/shard_map/ppermute | solution.py:28
  76.8 7.7 %collective-permute-start.20 = (bf16[256,512]{1,0:T(8,128)(2,1)}, bf16[256,512]{1,0:T(8,128)(2,1)}, u32[]{:S(2)}, u32[]{:S(2)}) collective-permute-start(bf16[256,512]{1,0:T(8,128)(2,1)} %select_convert_fusion), channel_id=1, source_target_pairs={{0,1},{32,33},{64,65},{96,97},{1,0},{33,32},{65,64},{97,96},{8,9},... | collective-permute-start | bytes 786440 | tf_op jit(solution)/shard_map/ppermute | solution.py:28
  88.0 0.8 copy-start.6
  88.8 9.5 %collective-permute-start.21 = (f32[256,256]{1,0:T(8,128)S(1)}, f32[256,256]{1,0:T(8,128)S(1)}, u32[]{:S(2)}, u32[]{:S(2)}) collective-permute-start(f32[256,256]{1,0:T(8,128)S(1)} %constant_dynamic-slice_fusion), channel_id=1, source_target_pairs={{0,32},{32,0},{64,96},{96,64},{1,33},{33,1},{65,97},{97,65},{8,40}... | collective-permute-start | bytes 786440 | tf_op jit(solution)/shard_map/ppermute | solution.py:28
  99.3 7.6 %collective-permute-start.22 = (f32[256,256]{1,0:T(8,128)S(1)}, f32[256,256]{1,0:T(8,128)S(1)}, u32[]{:S(2)}, u32[]{:S(2)}) collective-permute-start(f32[256,256]{1,0:T(8,128)S(1)} %dynamic-slice_add_fusion), channel_id=1, source_target_pairs={{0,64},{32,96},{64,0},{96,32},{1,65},{33,97},{65,1},{97,33},{8,72}... | collective-permute-start | bytes 786440 | tf_op jit(solution)/shard_map/ppermute | solution.py:28
  108.0 36.7 %copy-start.8 = (f32[256,256]{1,0:T(8,128)}, f32[256,256]{1,0:T(8,128)S(1)}, u32[]{:S(2)}) copy-start(f32[256,256]{1,0:T(8,128)S(1)} %get-tuple-element.34) | copy-start | bytes 786436
  108.0 5.8 %collective-permute-start.24 = (bf16[256,256]{1,0:T(8,128)(2,1)S(1)}, bf16[256,256]{1,0:T(8,128)(2,1)S(1)}, u32[]{:S(2)}, u32[]{:S(2)}) collective-permute-start(bf16[256,256]{1,0:T(8,128)(2,1)S(1)} %get-tuple-element.33), channel_id=1, source_target_pairs={{0,65},{32,97},{64,1},{96,33},{1,64},{33,96},{65,0},{97,32},{8,73}... | collective-permute-start | bytes 393224 | tf_op jit(solution)/shard_map/ppermute | solution.py:28
  113.8 6.2 %collective-permute-start.33 = (bf16[256,256]{1,0:T(8,128)(2,1)S(1)}, bf16[256,256]{1,0:T(8,128)(2,1)S(1)}, u32[]{:S(2)}, u32[]{:S(2)}) collective-permute-start(bf16[256,256]{1,0:T(8,128)(2,1)S(1)} %get-tuple-element.47), channel_id=1, source_target_pairs={{0,8},{32,40},{64,72},{96,104},{1,9},{33,41},{65,73},{97,105},{8,1... | collective-permute-start | bytes 393224 | tf_op jit(solution)/shard_map/ppermute | solution.py:28
  113.9 6.3 %collective-permute-start.34 = (bf16[256,256]{1,0:T(8,128)(2,1)S(1)}, bf16[256,256]{1,0:T(8,128)(2,1)S(1)}, u32[]{:S(2)}, u32[]{:S(2)}) collective-permute-start(bf16[256,256]{1,0:T(8,128)(2,1)S(1)} %get-tuple-element.47), channel_id=1, source_target_pairs={{0,24},{32,56},{64,88},{96,120},{1,25},{33,57},{65,89},{97,121},{8... | collective-permute-start | bytes 393224 | tf_op jit(solution)/shard_map/ppermute | solution.py:28
  117.4 5.5 %collective-permute-start.25 = (bf16[256,256]{1,0:T(8,128)(2,1)S(1)}, bf16[256,256]{1,0:T(8,128)(2,1)S(1)}, u32[]{:S(2)}, u32[]{:S(2)}) collective-permute-start(bf16[256,256]{1,0:T(8,128)(2,1)S(1)} %get-tuple-element.48), channel_id=1, source_target_pairs={{0,2},{32,34},{64,66},{96,98},{1,3},{33,35},{65,67},{97,99},{8,10}... | collective-permute-start | bytes 393224 | tf_op jit(solution)/shard_map/ppermute | solution.py:28
  117.4 5.6 %collective-permute-start.26 = (bf16[256,256]{1,0:T(8,128)(2,1)S(1)}, bf16[256,256]{1,0:T(8,128)(2,1)S(1)}, u32[]{:S(2)}, u32[]{:S(2)}) collective-permute-start(bf16[256,256]{1,0:T(8,128)(2,1)S(1)} %get-tuple-element.48), channel_id=1, source_target_pairs={{0,6},{32,38},{64,70},{96,102},{1,7},{33,39},{65,71},{97,103},{8,1... | collective-permute-start | bytes 393224 | tf_op jit(solution)/shard_map/ppermute | solution.py:28
  120.1 5.7 %collective-permute-start.35 = (bf16[128,256]{1,0:T(8,128)(2,1)S(1)}, bf16[128,256]{1,0:T(8,128)(2,1)S(1)}, u32[]{:S(2)}, u32[]{:S(2)}) collective-permute-start(bf16[128,256]{1,0:T(8,128)(2,1)S(1)} %slice.260), channel_id=1, source_target_pairs={{0,8},{32,40},{64,72},{96,104},{1,9},{33,41},{65,73},{97,105},{8,1... | collective-permute-start | bytes 196616 | tf_op jit(solution)/shard_map/ppermute | solution.py:28
  120.2 5.6 %collective-permute-start.36 = (bf16[128,256]{1,0:T(8,128)(2,1)S(1)}, bf16[128,256]{1,0:T(8,128)(2,1)S(1)}, u32[]{:S(2)}, u32[]{:S(2)}) collective-permute-start(bf16[128,256]{1,0:T(8,128)(2,1)S(1)} %slice.261), channel_id=1, source_target_pairs={{0,24},{32,56},{64,88},{96,120},{1,25},{33,57},{65,89},{97,121},{8... | collective-permute-start | bytes 196616 | tf_op jit(solution)/shard_map/ppermute | solution.py:28
  122.9 5.7 %collective-permute-start.27 = (bf16[128,256]{1,0:T(8,128)(2,1)S(1)}, bf16[128,256]{1,0:T(8,128)(2,1)S(1)}, u32[]{:S(2)}, u32[]{:S(2)}) collective-permute-start(bf16[128,256]{1,0:T(8,128)(2,1)S(1)} %slice.256), channel_id=1, source_target_pairs={{0,2},{32,34},{64,66},{96,98},{1,3},{33,35},{65,67},{97,99},{8,10}... | collective-permute-start | bytes 196616 | tf_op jit(solution)/shard_map/ppermute | solution.py:28
  123.0 5.6 %collective-permute-start.28 = (bf16[128,256]{1,0:T(8,128)(2,1)S(1)}, bf16[128,256]{1,0:T(8,128)(2,1)S(1)}, u32[]{:S(2)}, u32[]{:S(2)}) collective-permute-start(bf16[128,256]{1,0:T(8,128)(2,1)S(1)} %slice.257), channel_id=1, source_target_pairs={{0,6},{32,38},{64,70},{96,102},{1,7},{33,39},{65,71},{97,103},{8,1... | collective-permute-start | bytes 196616 | tf_op jit(solution)/shard_map/ppermute | solution.py:28
  125.9 12.0 %collective-permute-start.37 = (bf16[4,256,256]{2,1,0:T(8,128)(2,1)S(1)}, bf16[4,256,256]{2,1,0:T(8,128)(2,1)S(1)}, u32[]{:S(2)}, u32[]{:S(2)}) collective-permute-start(bf16[4,256,256]{2,1,0:T(8,128)(2,1)S(1)} %pad_maximum_fusion.1.refs_1_), channel_id=1, source_target_pairs={{0,2},{32,34},{64,66},{96,98},{1,3},{33,35},{65,67},{97,99},{8,10}... | collective-permute-start | bytes 1572872 | tf_op jit(solution)/shard_map/ppermute | solution.py:28
  125.9 13.1 %collective-permute-start.39 = (bf16[4,256,256]{2,1,0:T(8,128)(2,1)S(1)}, bf16[4,256,256]{2,1,0:T(8,128)(2,1)S(1)}, u32[]{:S(2)}, u32[]{:S(2)}) collective-permute-start(bf16[4,256,256]{2,1,0:T(8,128)(2,1)S(1)} %pad_maximum_fusion.1.refs_1_), channel_id=1, source_target_pairs={{0,6},{32,38},{64,70},{96,102},{1,7},{33,39},{65,71},{97,103},{8,1... | collective-permute-start | bytes 1572872 | tf_op jit(solution)/shard_map/ppermute | solution.py:28
  128.7 16.7 %collective-permute-start.29 = (bf16[4,256,256]{2,1,0:T(8,128)(2,1)S(1)}, bf16[4,256,256]{2,1,0:T(8,128)(2,1)S(1)}, u32[]{:S(2)}, u32[]{:S(2)}) collective-permute-start(bf16[4,256,256]{2,1,0:T(8,128)(2,1)S(1)} %pad_maximum_fusion.refs_0_), channel_id=1, source_target_pairs={{0,8},{32,40},{64,72},{96,104},{1,9},{33,41},{65,73},{97,105},{8,1... | collective-permute-start | bytes 1572872 | tf_op jit(solution)/shard_map/ppermute | solution.py:28
  128.8 19.6 %collective-permute-start.50 = (bf16[4,256,256]{2,1,0:T(8,128)(2,1)S(1)}, bf16[4,256,256]{2,1,0:T(8,128)(2,1)}, u32[]{:S(2)}, u32[]{:S(2)}) collective-permute-start(bf16[4,256,256]{2,1,0:T(8,128)(2,1)S(1)} %pad_maximum_fusion.1.refs_1_), channel_id=1, source_target_pairs={{0,32},{32,0},{64,96},{96,64},{1,33},{33,1},{65,97},{97,65},{8,40}... | collective-permute-start | bytes 1572872 | tf_op jit(solution)/shard_map/ppermute | solution.py:28
  133.5 15.0 %collective-permute-start.49 = (bf16[4,256,256]{2,1,0:T(8,128)(2,1)S(1)}, bf16[4,256,256]{2,1,0:T(8,128)(2,1)}, u32[]{:S(2)}, u32[]{:S(2)}) collective-permute-start(bf16[4,256,256]{2,1,0:T(8,128)(2,1)S(1)} %pad_maximum_fusion.refs_0_), channel_id=1, source_target_pairs={{0,32},{32,0},{64,96},{96,64},{1,33},{33,1},{65,97},{97,65},{8,40}... | collective-permute-start | bytes 1572872 | tf_op jit(solution)/shard_map/ppermute | solution.py:28
  137.9 11.5 %collective-permute-start.31 = (bf16[4,256,256]{2,1,0:T(8,128)(2,1)S(1)}, bf16[4,256,256]{2,1,0:T(8,128)(2,1)S(1)}, u32[]{:S(2)}, u32[]{:S(2)}) collective-permute-start(bf16[4,256,256]{2,1,0:T(8,128)(2,1)S(1)} %pad_maximum_fusion.refs_0_), channel_id=1, source_target_pairs={{0,24},{32,56},{64,88},{96,120},{1,25},{33,57},{65,89},{97,121},{8... | collective-permute-start | bytes 1572872 | tf_op jit(solution)/shard_map/ppermute | solution.py:28
  139.1 6.3 %collective-permute-start.23 = (f32[256,256]{1,0:T(8,128)S(1)}, f32[256,256]{1,0:T(8,128)S(1)}, u32[]{:S(2)}, u32[]{:S(2)}) collective-permute-start(f32[256,256]{1,0:T(8,128)S(1)} %get-tuple-element.34), channel_id=1, source_target_pairs={{0,32},{32,0},{64,96},{96,64},{1,33},{33,1},{65,97},{97,65},{8,40}... | collective-permute-start | bytes 786440 | tf_op jit(solution)/shard_map/ppermute | solution.py:28
  145.4 0.7 copy-start.11
  145.4 9.3 %collective-permute-start.38 = (bf16[2,256,256]{2,1,0:T(8,128)(2,1)}, bf16[2,256,256]{2,1,0:T(8,128)(2,1)S(1)}, u32[]{:S(2)}, u32[]{:S(2)}) collective-permute-start(bf16[2,256,256]{2,1,0:T(8,128)(2,1)} %slice.262), channel_id=1, source_target_pairs={{0,2},{32,34},{64,66},{96,98},{1,3},{33,35},{65,67},{97,99},{8,10}... | collective-permute-start | bytes 786440 | tf_op jit(solution)/shard_map/ppermute | solution.py:28
  146.1 9.5 %collective-permute-start.40 = (bf16[2,256,256]{2,1,0:T(8,128)(2,1)}, bf16[2,256,256]{2,1,0:T(8,128)(2,1)}, u32[]{:S(2)}, u32[]{:S(2)}) collective-permute-start(bf16[2,256,256]{2,1,0:T(8,128)(2,1)} %slice.263), channel_id=1, source_target_pairs={{0,6},{32,38},{64,70},{96,102},{1,7},{33,39},{65,71},{97,103},{8,1... | collective-permute-start | bytes 786440 | tf_op jit(solution)/shard_map/ppermute | solution.py:28
  148.4 9.8 %copy-start.4 = (f32[256,512]{1,0:T(8,128)S(1)}, f32[256,512]{1,0:T(8,128)}, u32[]{:S(2)}) copy-start(f32[256,512]{1,0:T(8,128)} %param.12) | copy-start | bytes 1572868
  148.4 9.8 %copy-start.7 = (f32[256,512]{1,0:T(8,128)S(1)}, f32[256,512]{1,0:T(8,128)}, u32[]{:S(2)}) copy-start(f32[256,512]{1,0:T(8,128)} %param.13) | copy-start | bytes 1572868
  148.4 9.8 %copy-start.9 = (f32[256,256]{1,0:T(8,128)S(1)}, f32[256,256]{1,0:T(8,128)}, u32[]{:S(2)}) copy-start(f32[256,256]{1,0:T(8,128)} %copy-done.8) | copy-start | bytes 786436
  148.4 9.8 %copy-start.12 = (f32[256,256]{1,0:T(8,128)S(1)}, f32[256,256]{1,0:T(8,128)}, u32[]{:S(2)}) copy-start(f32[256,256]{1,0:T(8,128)} %copy-done.11) | copy-start | bytes 786436
  148.4 9.7 %collective-permute-start.30 = (bf16[2,256,256]{2,1,0:T(8,128)(2,1)S(1)}, bf16[2,256,256]{2,1,0:T(8,128)(2,1)S(1)}, u32[]{:S(2)}, u32[]{:S(2)}) collective-permute-start(bf16[2,256,256]{2,1,0:T(8,128)(2,1)S(1)} %slice.258), channel_id=1, source_target_pairs={{0,8},{32,40},{64,72},{96,104},{1,9},{33,41},{65,73},{97,105},{8,1... | collective-permute-start | bytes 786440 | tf_op jit(solution)/shard_map/ppermute | solution.py:28
  148.5 20.2 %collective-permute-start.47 = (bf16[4,256,256]{2,1,0:T(8,128)(2,1)S(1)}, bf16[4,256,256]{2,1,0:T(8,128)(2,1)S(1)}, u32[]{:S(2)}, u32[]{:S(2)}) collective-permute-start(bf16[4,256,256]{2,1,0:T(8,128)(2,1)S(1)} %collective-permute-done.37.refs_2_), channel_id=1, source_target_pairs={{0,32},{32,0},{64,96},{96,64},{1,33},{33,1},{65,97},{97,65},{8,40}... | collective-permute-start | bytes 1572872 | tf_op jit(solution)/shard_map/ppermute | solution.py:28
  149.4 19.6 %collective-permute-start.48 = (bf16[4,256,256]{2,1,0:T(8,128)(2,1)S(1)}, bf16[4,256,256]{2,1,0:T(8,128)(2,1)S(1)}, u32[]{:S(2)}, u32[]{:S(2)}) collective-permute-start(bf16[4,256,256]{2,1,0:T(8,128)(2,1)S(1)} %collective-permute-done.39.refs_3_), channel_id=1, source_target_pairs={{0,32},{32,0},{64,96},{96,64},{1,33},{33,1},{65,97},{97,65},{8,40}... | collective-permute-start | bytes 1572872 | tf_op jit(solution)/shard_map/ppermute | solution.py:28
  154.7 14.6 %collective-permute-start.45 = (bf16[4,256,256]{2,1,0:T(8,128)(2,1)S(1)}, bf16[4,256,256]{2,1,0:T(8,128)(2,1)S(1)}, u32[]{:S(2)}, u32[]{:S(2)}) collective-permute-start(bf16[4,256,256]{2,1,0:T(8,128)(2,1)S(1)} %collective-permute-done.29.refs_0_), channel_id=1, source_target_pairs={{0,32},{32,0},{64,96},{96,64},{1,33},{33,1},{65,97},{97,65},{8,40}... | collective-permute-start | bytes 1572872 | tf_op jit(solution)/shard_map/ppermute | solution.py:28
  155.6 14.0 %collective-permute-start.46 = (bf16[4,256,256]{2,1,0:T(8,128)(2,1)S(1)}, bf16[4,256,256]{2,1,0:T(8,128)(2,1)S(1)}, u32[]{:S(2)}, u32[]{:S(2)}) collective-permute-start(bf16[4,256,256]{2,1,0:T(8,128)(2,1)S(1)} %collective-permute-done.31.refs_1_), channel_id=1, source_target_pairs={{0,32},{32,0},{64,96},{96,64},{1,33},{33,1},{65,97},{97,65},{8,40}... | collective-permute-start | bytes 1572872 | tf_op jit(solution)/shard_map/ppermute | solution.py:28
  158.1 10.1 %collective-permute-start.32 = (bf16[2,256,256]{2,1,0:T(8,128)(2,1)S(1)}, bf16[2,256,256]{2,1,0:T(8,128)(2,1)S(1)}, u32[]{:S(2)}, u32[]{:S(2)}) collective-permute-start(bf16[2,256,256]{2,1,0:T(8,128)(2,1)S(1)} %slice.259), channel_id=1, source_target_pairs={{0,24},{32,56},{64,88},{96,120},{1,25},{33,57},{65,89},{97,121},{8... | collective-permute-start | bytes 786440 | tf_op jit(solution)/shard_map/ppermute | solution.py:28
  168.2 17.3 %collective-permute-start.43 = (bf16[2,256,256]{2,1,0:T(8,128)(2,1)S(1)}, bf16[2,256,256]{2,1,0:T(8,128)(2,1)S(1)}, u32[]{:S(2)}, u32[]{:S(2)}) collective-permute-start(bf16[2,256,256]{2,1,0:T(8,128)(2,1)S(1)} %collective-permute-done.38.refs_2_), channel_id=1, source_target_pairs={{0,32},{32,0},{64,96},{96,64},{1,33},{33,1},{65,97},{97,65},{8,40}... | collective-permute-start | bytes 786440 | tf_op jit(solution)/shard_map/ppermute | solution.py:28
  168.7 16.8 %collective-permute-start.44 = (bf16[2,256,256]{2,1,0:T(8,128)(2,1)}, bf16[2,256,256]{2,1,0:T(8,128)(2,1)S(1)}, u32[]{:S(2)}, u32[]{:S(2)}) collective-permute-start(bf16[2,256,256]{2,1,0:T(8,128)(2,1)} %collective-permute-done.40.refs_3_), channel_id=1, source_target_pairs={{0,32},{32,0},{64,96},{96,64},{1,33},{33,1},{65,97},{97,65},{8,40}... | collective-permute-start | bytes 786440 | tf_op jit(solution)/shard_map/ppermute | solution.py:28
  169.0 0.8 copy-start.10
  169.0 16.5 %collective-permute-start.41 = (bf16[2,256,256]{2,1,0:T(8,128)(2,1)S(1)}, bf16[2,256,256]{2,1,0:T(8,128)(2,1)S(1)}, u32[]{:S(2)}, u32[]{:S(2)}) collective-permute-start(bf16[2,256,256]{2,1,0:T(8,128)(2,1)S(1)} %collective-permute-done.30.refs_0_), channel_id=1, source_target_pairs={{0,32},{32,0},{64,96},{96,64},{1,33},{33,1},{65,97},{97,65},{8,40}... | collective-permute-start | bytes 786440 | tf_op jit(solution)/shard_map/ppermute | solution.py:28
  169.2 16.3 %collective-permute-start.42 = (bf16[2,256,256]{2,1,0:T(8,128)(2,1)S(1)}, bf16[2,256,256]{2,1,0:T(8,128)(2,1)S(1)}, u32[]{:S(2)}, u32[]{:S(2)}) collective-permute-start(bf16[2,256,256]{2,1,0:T(8,128)(2,1)S(1)} %collective-permute-done.32.refs_1_), channel_id=1, source_target_pairs={{0,32},{32,0},{64,96},{96,64},{1,33},{33,1},{65,97},{97,65},{8,40}... | collective-permute-start | bytes 786440 | tf_op jit(solution)/shard_map/ppermute | solution.py:28

commit v2 on v0

v2 whole, which is shorter than its diff:
```python
import functools

import jax
import jax.numpy as jnp
from jax import lax
from jax.experimental import pallas as pl
from jax.experimental.pallas import tpu as pltpu
from jax.sharding import PartitionSpec as P

BOTH = ("replica", "fsdp")
BF16, F32 = jnp.bfloat16, jnp.float32
H1, H2 = (2, 1), (3, 0)
VMEM = pl.BlockSpec(memory_space=pltpu.VMEM)
ANY = pl.BlockSpec(memory_space=pl.ANY)


def flat(x, y, z, c):
    x, y, z = x % 4, y % 4, z % 4
    return ((z % 2) * 2 + c) * 32 + (y * 4 + x) * 2 + z // 2


def permute(array, move):
    pairs = []
    for x in range(4):
        for y in range(4):
            for z in range(4):
                for c in range(2):
                    target = move(x, y, z, c)
                    if target is not None:
                        pairs.append((flat(x, y, z, c), flat(*target)))
    return lax.ppermute(array, BOTH, pairs)


def first(step):
    return lambda x, y, z, c: (x, y + step, z, c) if c else (x + step, y, z, c)


def second(step):
    return lambda x, y, z, c: (x + step, y, z, c) if c else (x, y + step, z, c)


def other_core(x, y, z, c):
    return x, y, z, 1 - c


def pair_lo(x, y, z, c):
    return x, y, z ^ 1, c


def pair_hi(x, y, z, c):
    return None if z // 2 == c else (x, y, 3 - z, 1 - c)


def across(x, y, z, c):
    return x, y, z + 2, c


def z_hi():
    return lax.rem(lax.axis_index("fsdp"), 2)


def core_index():
    return lax.rem(lax.axis_index("replica"), 2)


def plane(core, k1, k2):
    f = lax.axis_index("fsdp")
    y, x = lax.div(f, 8), lax.rem(lax.div(f, 2), 4)
    dx, dy = k1 + core * (k2 - k1), k2 + core * (k1 - k2)
    return lax.rem(y + dy, 4) * 4 + lax.rem(x + dx, 4)


def local(kernel, outs, *arrays, limit=16):
    return pl.pallas_call(
        kernel,
        in_specs=[VMEM] * len(arrays),
        out_specs=[VMEM] * len(outs),
        out_shape=[jax.ShapeDtypeStruct(*out) for out in outs],
        compiler_params=pltpu.CompilerParams(vmem_limit_bytes=limit << 20),
    )(*arrays)


def columns(tok_ref, start, width):
    return tok_ref.at[:, pl.ds(pl.multiple_of(start, 256), width)]


def started(copies):
    for copy in copies:
        copy.start()
    return copies


def cost(rows, width, cols):
    return pl.CostEstimate(
        flops=2 * rows * width * cols, bytes_accessed=2 * rows * width, transcendentals=0
    )


def grad_kernel(names, n_recv, tok_ref, grad_ref, *refs):
    groups = len(names) // 2
    recv, outs = refs[:n_recv], refs[n_recv : n_recv + groups]
    held, g_ref, sems = refs[n_recv + groups :]
    g_copy = pltpu.make_async_copy(grad_ref, g_ref, sems.at[len(names)])
    g_copy.start()
    copies = started(
        [
            pltpu.make_async_copy(
                columns(tok_ref, plane(core_index(), *name) * 512, 512),
                held.at[:, 512 * number : 512 * number + 512],
                sems.at[number],
            )
            for number, name in enumerate(names)
        ]
    )
    g_copy.wait()
    for number in range(len(names)):
        copies[number].wait()
        group, rows = number // 2, slice(512 * (number % 2), 512 * (number % 2) + 512)
        term = lax.dot_general(
            held[:, 512 * number : 512 * number + 512],
            g_ref[...],
            (((0,), (0,)), ((), ())),
            preferred_element_type=F32,
        )
        if recv:
            term = term + recv[group][rows].astype(F32)
        outs[group][rows] = term.astype(outs[group].dtype)


def grad_blocks(groups, dtype, limit, tokens, out_grad, *recv):
    names = [(k1, k2) for k1, half in groups for k2 in half]
    width, cols = 512 * len(names), out_grad.shape[1]
    return pl.pallas_call(
        functools.partial(grad_kernel, names, len(recv)),
        in_specs=[ANY, ANY] + [VMEM] * len(recv),
        out_specs=[VMEM] * len(groups),
        out_shape=[jax.ShapeDtypeStruct((1024, cols), dtype)] * len(groups),
        scratch_shapes=[
            pltpu.VMEM((tokens.shape[0], width), BF16),
            pltpu.VMEM(out_grad.shape, BF16),
            pltpu.SemaphoreType.DMA((len(names) + 1,)),
        ],
        compiler_params=pltpu.CompilerParams(vmem_limit_bytes=limit << 20),
        cost_estimate=cost(tokens.shape[0], width, cols),
    )(tokens, out_grad, *recv)


def total_kernel(own1, own2, got1, got2, two, one, three, zero):
    for out, own, got, rows in (
        (two, own1, got1, slice(0, 512)),
        (one, own1, got1, slice(512, 1024)),
        (three, own2, got2, slice(0, 512)),
        (zero, own2, got2, slice(512, 1024)),
    ):
        out[...] = (own[rows] + got[rows].astype(F32)).astype(out.dtype)


def choose_kernel(zero, two, one, three, keep, give):
    rows = keep.shape[0]
    mine = z_hi()
    for which, out in ((mine, keep), (1 - mine, give)):
        part = pl.ds(pl.multiple_of(which * rows, rows), rows)
        total = zero[part]
        for ref in (two, one, three):
            total = total + ref[part].astype(F32)
        out[...] = total.astype(out.dtype)


def reduce_scatter(tokens, out_grad):
    def send(arrays):
        return permute(arrays[0], first(1)), permute(arrays[1], first(-1))

    def blocks(groups, dtype, limit, *recv):
        return grad_blocks(groups, dtype, limit, tokens, out_grad, *recv)

    up1, down1 = send(blocks([(2, H1), (2, H2)], BF16, 50))
    up2, down2 = send(blocks([(1, H2), (3, H1)], BF16, 46))
    up3, down3 = send(blocks([(1, H1), (3, H2)], BF16, 46, up1, down1))
    own1, own2 = blocks([(0, H1), (0, H2)], F32, 46, down2, up2)
    block = (512, 512)
    two, one, three, zero = local(
        total_kernel,
        [(block, BF16), (block, BF16), (block, BF16), (block, F32)],
        own1,
        own2,
        up3,
        down3,
    )
    keep, give = local(
        choose_kernel,
        [((256, 512), F32), ((256, 512), BF16)],
        zero,
        permute(two, second(2)),
        permute(one, second(1)),
        permute(three, second(-1)),
    )
    return keep, permute(give, across)


def update_kernel(
    scale, keep, got, inner_ref, first_ref, second_ref, weights_ref, first_out, second_out, mine, other
):
    grad = (keep[...] + got[...].astype(F32)) * scale
    new_first = 0.9 * first_ref[...] + 0.1 * grad
    new_second = 0.95 * second_ref[...] + 0.05 * grad * grad
    inner = inner_ref[...]
    stepped = inner - 0.25 * (new_first / (jnp.sqrt(new_second) + 1e-08) + 0.1 * inner)
    drift = weights_ref[...] - stepped
    first_out[...] = new_first
    second_out[...] = new_second
    half = drift.shape[1] // 2
    core = core_index()
    for which, out in ((core, mine), (1 - core, other)):
        out[...] = jnp.where(which == 0, drift[:, :half], drift[:, half:])


def add_kernel(left, right, out):
    out[...] = left[...] + right[...]


def outer_kernel(
    n_replica, mine, theirs, weights_ref, momentum_ref, weights_out, momentum_out, synced
):
    half = mine.shape[1]
    low = core_index() == 0
    left, right = mine[...], theirs[...]
    for part, total in (
        (slice(0, half), jnp.where(low, left, right)),
        (slice(half, 2 * half), jnp.where(low, right, left)),
    ):
        pseudo = total / n_replica
        new_momentum = 0.9 * momentum_ref[:, part] + pseudo
        new_global = weights_ref[:, part] - 0.7 * (pseudo + 0.9 * new_momentum)
        weights_out[:, part] = new_global
        momentum_out[:, part] = new_momentum
        synced[:, part] = new_global.astype(BF16)


def pick_kernel(synced, got, out):
    out[...] = jnp.where(z_hi() == core_index(), synced[...], got[...])


def stack_kernel(*refs):
    ins, outs = refs[:4], refs[4:]
    for number, ref in enumerate(ins):
        at = 256 * (number % 2)
        outs[number // 2][at : at + 256] = ref[...]


def project_kernel(places, n_recv, carried, scale, tok_ref, *refs):
    arrays = refs[:n_recv]
    acc = refs[n_recv] if carried else None
    out, held, right, sems = refs[-4:]
    copies, at = [], 0
    for number, (ref, (partner, names)) in enumerate(zip(arrays, places)):
        core = core_index()
        who = 1 - core if partner else core
        batch = [
            pltpu.make_async_copy(
                columns(tok_ref, plane(who, *name) * 512 + who * 256, 256),
                held.at[:, at + 256 * place : at + 256 * place + 256],
                sems.at[3 * number + place],
            )
            for place, name in enumerate(names)
        ]
        batch.append(
            pltpu.make_async_copy(ref, right.at[at : at + 512], sems.at[3 * number + 2])
        )
        copies += started(batch)
        at += 512
    total = acc[...] if carried else None
    step = 1024
    for start in range(0, at, step):
        for copy in copies[3 * start // 512 : 3 * (start + step) // 512]:
            copy.wait()
        term = jnp.dot(
            held[:, start : start + step],
            right[start : start + step],
            preferred_element_type=F32,
        )
        total = term if total is None else total + term
    out[...] = total if scale is None else (total * scale).astype(BF16)


def project(tokens, arrays, names, acc, scale):
    theirs = [permute(array, other_core) for array in arrays]
    both = [*arrays, *theirs]
    places = [(0, name) for name in names] + [(1, name) for name in names]
    carried = [] if acc is None else [acc]
    rows, width, cols = tokens.shape[0], 512 * len(both), arrays[0].shape[1]
    return pl.pallas_call(
        functools.partial(project_kernel, places, len(both), bool(carried), scale),
        in_specs=[ANY] + [ANY] * len(both) + [VMEM] * len(carried),
        out_specs=VMEM,
        out_shape=jax.ShapeDtypeStruct((rows, cols), F32 if scale is None else BF16),
        scratch_shapes=[
            pltpu.VMEM((rows, width), BF16),
            pltpu.VMEM((width, cols), BF16),
            pltpu.SemaphoreType.DMA((3 * len(both),)),
        ],
        compiler_params=pltpu.CompilerParams(vmem_limit_bytes=46 << 20),
        cost_estimate=cost(rows, width, cols),
    )(tokens, *both, *carried)


def gather_project(synced, tokens, scale):
    quarter = ((256, 512), BF16)
    half = ((512, 512), BF16)
    (own,) = local(pick_kernel, [quarter], synced, permute(synced, pair_hi))
    far = permute(own, first(2))
    behind, ahead = permute(own, first(1)), permute(own, first(-1))
    low, high = local(stack_kernel, [half, half], own, behind, ahead, far)
    lows, highs = (0, 3), (1, 2)
    low_up, high_down = permute(low, second(1)), permute(high, second(-1))
    high_up, low_down = permute(high, second(1)), permute(low, second(-1))
    low_far, high_far = permute(low_up, second(1)), permute(high_down, second(-1))

    def names(firsts, k2):
        return [(k1, k2) for k1 in firsts]

    acc = project(tokens, [low, high], [names(lows, 0), names(highs, 0)], None, None)
    acc = project(tokens, [low_up, high_down], [names(lows, 3), names(highs, 1)], acc, None)
    acc = project(tokens, [high_up, low_down], [names(highs, 3), names(lows, 1)], acc, None)
    return project(tokens, [low_far, high_far], [names(lows, 2), names(highs, 2)], acc, scale)


def body(
    tokens, out_grad, inner_weights, first_moment, second_moment, global_weights, outer_momentum
):
    scale = 1.0 / tokens.shape[1] ** 0.5
    n_replica = lax.axis_size("replica")
    keep, got = reduce_scatter(tokens, out_grad)
    block, half = keep.shape, (keep.shape[0], keep.shape[1] // 2)
    new_first, new_second, mine, other = local(
        functools.partial(update_kernel, scale),
        [(block, F32), (block, F32), (half, F32), (half, F32)],
        keep,
        got,
        inner_weights[0],
        first_moment[0],
        second_moment[0],
        global_weights,
    )
    (mine,) = local(add_kernel, [(half, F32)], mine, permute(other, other_core))
    (mine,) = local(add_kernel, [(half, F32)], mine, permute(mine, pair_lo))
    new_global, new_momentum, synced = local(
        functools.partial(outer_kernel, n_replica),
        [(block, F32), (block, F32), (block, BF16)],
        mine,
        permute(mine, other_core),
        global_weights,
        outer_momentum,
    )
    projected = gather_project(synced, tokens, scale)
    return (new_first[None], new_second[None], new_global, new_momentum, projected)


def solution(mesh):
    placed = (
        P(("replica", "fsdp"), None),
        P(("replica", "fsdp"), None),
        P("replica", "fsdp", None),
        P("replica", "fsdp", None),
        P("replica", "fsdp", None),
        P("fsdp", None),
        P("fsdp", None),
    )
    return jax.shard_map(
        body,
        mesh=mesh,
        in_specs=placed,
        out_specs=(
            P("replica", "fsdp", None),
            P("replica", "fsdp", None),
            P("fsdp", None),
            P("fsdp", None),
            P(("replica", "fsdp"), None),
        ),
        check_vma=False,
    )
```

time: 564 us -> 147 us (0.26)
  waiting for transfers between devices: 511 us -> 58.5 us
  starting transfers between devices: 0.12 us -> 47.3 us
  Pallas kernels: 0 us -> 38.4 us
  matrix products: 30.6 us -> 0 us
  between operations: 13.8 us -> 1.04 us
    reduce_scatter x1 -> x0, waiting for transfers between devices: 364 us -> none  [body(): lax.psum_scatter(lax.dot_general(tok_cols, out_grad, (((0,), (0,)), ((),...]
    all_gather x1 -> x0, waiting for transfers between devices: 107 us -> none  [body(): lax.all_gather(synced, 'fsdp', axis=0, tiled=True)]
    ppermute x0 -> x31, waiting for transfers between devices: none -> 58.5 us  [permute(): return lax.ppermute(array, BOTH, pairs)]
    ppermute x0 -> x31, starting transfers between devices: none -> 47.3 us  [permute(): return lax.ppermute(array, BOTH, pairs)]
    psum x1 -> x0, waiting for transfers between devices: 40.7 us -> none  [body(): pseudo = lax.psum(drift, 'replica') / n_replica]
    pallas_call x0 -> x16, Pallas kernels: none -> 38.4 us  [the longest x4 17.9 us: project(): pl.pallas_call(functools.partial(project_kernel, places, len(both), bool(...]
    dot_general x2 -> x0, matrix products: 30.6 us -> none  [the longest x1 15.8 us: body(): lax.dot_general(tok_cols, out_grad, (((0,), (0,)), ((), ())), preferred_e...]
  transfers between devices with their start and end apart: 3 -> 31, of which waited for: 3 -> 17; matrix products, arithmetic and copies ran while one was open for 0% -> 0% of each run, Pallas kernels for 0% -> 18%
where the time goes in v2:
time: 147 us
  waiting for transfers between devices  58.5 us (40%)
  starting transfers between devices  47.3 us (32%)
  Pallas kernels  38.4 us (26%)
    ppermute x31, waiting for transfers between devices, permute(): return lax.ppermute(array, BOTH, pairs)  58.5 us
    ppermute x31, starting transfers between devices, permute(): return lax.ppermute(array, BOTH, pairs)  47.3 us
    pallas_call x4, Pallas kernels, project(): pl.pallas_call(functools.partial(project_kernel, places, len(both), bool(...  17.9 us
    pallas_call x4, Pallas kernels, grad_blocks(): pl.pallas_call(functools.partial(grad_kernel, names, len(recv)), in_specs...  17.4 us
    pallas_call x8, Pallas kernels, local(): pl.pallas_call(kernel, in_specs=[VMEM] * len(arrays), out_specs=[VMEM] *...  3.18 us
  transfers between devices with their start and end apart: 31, of which 17 were waited for; matrix products, arithmetic and copies ran while one was open for 0% of the time, Pallas kernels for 18%

profile of v2, /device:TPU:1, one launch (start us, length us, event | category | flops | bytes accessed | tf_op | source)
XLA Modules:
  0.0 146.5 jit_solution(17025472754688570526)
XLA Ops:
  0.6 1.2 copy-done
  1.9 4.3 %shard_map.112 = (bf16[1024,512]{1,0:T(8,128)(2,1)S(1)}, bf16[1024,512]{1,0:T(8,128)(2,1)S(1)}) custom-call(bf16[1024,8192]{1,0:T(8,128)(2,1)} %tok_ref.15, bf16[1024,512]{1,0:T(8,128)(2,1)S(1)} %copy-done), custom_call_target="tpu_custom_call" | custom-call | flops 2147483648 | bytes 4194304 | tf_op jit(solution)/shard_map/pallas_call | solution.py:133
  6.2 2.2 %collective-permute-start.2 = (bf16[1024,512]{1,0:T(8,128)(2,1)S(1)}, bf16[1024,512]{1,0:T(8,128)(2,1)S(1)}, u32[]{:S(2)}, u32[]{:S(2)}) collective-permute-start(bf16[1024,512]{1,0:T(8,128)(2,1)S(1)} %get-tuple-element.32), channel_id=1, source_target_pairs={{0,2},{32,40},{64,66},{96,104},{1,3},{33,41},{65,67},{97,105},{8,1... | collective-permute-start | bytes 3145736 | tf_op jit(solution)/shard_map/ppermute | solution.py:31
  8.4 1.5 %collective-permute-start.3 = (bf16[1024,512]{1,0:T(8,128)(2,1)S(1)}, bf16[1024,512]{1,0:T(8,128)(2,1)S(1)}, u32[]{:S(2)}, u32[]{:S(2)}) collective-permute-start(bf16[1024,512]{1,0:T(8,128)(2,1)S(1)} %get-tuple-element.33), channel_id=1, source_target_pairs={{0,6},{32,56},{64,70},{96,120},{1,7},{33,57},{65,71},{97,121},{8,1... | collective-permute-start | bytes 3145736 | tf_op jit(solution)/shard_map/ppermute | solution.py:31
  9.9 4.3 %shard_map.110 = (bf16[1024,512]{1,0:T(8,128)(2,1)S(1)}, bf16[1024,512]{1,0:T(8,128)(2,1)S(1)}) custom-call(bf16[1024,8192]{1,0:T(8,128)(2,1)} %tok_ref.15, bf16[1024,512]{1,0:T(8,128)(2,1)S(1)} %copy-done), custom_call_target="tpu_custom_call" | custom-call | flops 2147483648 | bytes 4194304 | tf_op jit(solution)/shard_map/pallas_call | solution.py:133
  14.3 1.5 collective-permute-start
  15.7 0.1 collective-permute-start.1
  15.8 6.5 %collective-permute-done.2.refs_0_ = bf16[1024,512]{1,0:T(8,128)(2,1)S(1)} collective-permute-done((bf16[1024,512]{1,0:T(8,128)(2,1)S(1)}, bf16[1024,512]{1,0:T(8,128)(2,1)S(1)}, u32[]{:S(2)}, u32[]{:S(2)}) %collective-permute-start.2) | collective-permute-done | bytes 1048608 | tf_op jit(solution)/shard_map/ppermute | solution.py:31
  22.3 0.0 collective-permute-done.3.refs_1_
  22.4 4.4 %shard_map.113 = (bf16[1024,512]{1,0:T(8,128)(2,1)S(1)}, bf16[1024,512]{1,0:T(8,128)(2,1)S(1)}) custom-call(bf16[1024,8192]{1,0:T(8,128)(2,1)} %tok_ref.15, bf16[1024,512]{1,0:T(8,128)(2,1)S(1)} %copy-done.1, bf16[1024,512]{1,0:T(8,128)(2,1)S(1)} %collective-permute-done.2.refs_0_, bf16[1024,512]{1,0:T(8,128)(2,1)S(1)} %collective-permute-done.3.refs_1_), custom_call_target="tpu_custom_call" | custom-call | flops 2147483648 | bytes 4194304 | tf_op jit(solution)/shard_map/pallas_call | solution.py:133
  26.7 1.4 collective-permute-start.4
  28.1 1.5 %collective-permute-start.5 = (bf16[1024,512]{1,0:T(8,128)(2,1)S(1)}, bf16[1024,512]{1,0:T(8,128)(2,1)S(1)}, u32[]{:S(2)}, u32[]{:S(2)}) collective-permute-start(bf16[1024,512]{1,0:T(8,128)(2,1)S(1)} %get-tuple-element.35), channel_id=1, source_target_pairs={{0,6},{32,56},{64,70},{96,120},{1,7},{33,57},{65,71},{97,121},{8,1... | collective-permute-start | bytes 3145736 | tf_op jit(solution)/shard_map/ppermute | solution.py:31
  29.6 4.0 %collective-permute-done.refs_0_ = bf16[1024,512]{1,0:T(8,128)(2,1)S(1)} collective-permute-done((bf16[1024,512]{1,0:T(8,128)(2,1)S(1)}, bf16[1024,512]{1,0:T(8,128)(2,1)S(1)}, u32[]{:S(2)}, u32[]{:S(2)}) %collective-permute-start) | collective-permute-done | bytes 1048608 | tf_op jit(solution)/shard_map/ppermute | solution.py:31
  33.6 4.3 %shard_map.111 = (f32[1024,512]{1,0:T(8,128)S(1)}, f32[1024,512]{1,0:T(8,128)S(1)}) custom-call(bf16[1024,8192]{1,0:T(8,128)(2,1)} %tok_ref.15, bf16[1024,512]{1,0:T(8,128)(2,1)S(1)} %copy-done.1, bf16[1024,512]{1,0:T(8,128)(2,1)S(1)} %collective-permute-done.refs_0_, bf16[1024,512]{1,0:T(8,128)(2,1)S(1)} %collective-permute-done.1.refs_1_), custom_call_target="tpu_custom_call" | custom-call | flops 2147483648 | bytes 4194304 | tf_op jit(solution)/shard_map/pallas_call | solution.py:133
  37.9 6.9 %collective-permute-done.4.got1 = bf16[1024,512]{1,0:T(8,128)(2,1)S(1)} collective-permute-done((bf16[1024,512]{1,0:T(8,128)(2,1)S(1)}, bf16[1024,512]{1,0:T(8,128)(2,1)S(1)}, u32[]{:S(2)}, u32[]{:S(2)}) %collective-permute-start.4) | collective-permute-done | bytes 1048608 | tf_op jit(solution)/shard_map/ppermute | solution.py:31
  44.8 0.0 collective-permute-done.5.got2
  44.8 0.3 shard_map.114
  45.2 0.0 copy-start.2
  45.2 0.0 copy-start.5
  45.2 2.8 %collective-permute-start.6 = (bf16[512,512]{1,0:T(8,128)(2,1)S(1)}, bf16[512,512]{1,0:T(8,128)(2,1)S(1)}, u32[]{:S(2)}, u32[]{:S(2)}) collective-permute-start(bf16[512,512]{1,0:T(8,128)(2,1)S(1)} %get-tuple-element.37), channel_id=1, source_target_pairs={{0,16},{32,36},{64,80},{96,100},{1,17},{33,37},{65,81},{97,101},{8... | collective-permute-start | bytes 1572872 | tf_op jit(solution)/shard_map/ppermute | solution.py:31
  48.0 0.3 collective-permute-start.7
  48.4 2.4 %collective-permute-start.8 = (bf16[512,512]{1,0:T(8,128)(2,1)S(1)}, bf16[512,512]{1,0:T(8,128)(2,1)S(1)}, u32[]{:S(2)}, u32[]{:S(2)}) collective-permute-start(bf16[512,512]{1,0:T(8,128)(2,1)S(1)} %get-tuple-element.39), channel_id=1, source_target_pairs={{0,24},{32,38},{64,88},{96,102},{1,25},{33,39},{65,89},{97,103},{8... | collective-permute-start | bytes 1572872 | tf_op jit(solution)/shard_map/ppermute | solution.py:31
  50.7 4.5 %collective-permute-done.6.two = bf16[512,512]{1,0:T(8,128)(2,1)S(1)} collective-permute-done((bf16[512,512]{1,0:T(8,128)(2,1)S(1)}, bf16[512,512]{1,0:T(8,128)(2,1)S(1)}, u32[]{:S(2)}, u32[]{:S(2)}) %collective-permute-start.6) | collective-permute-done | bytes 524320 | tf_op jit(solution)/shard_map/ppermute | solution.py:31
  55.2 5.6 %collective-permute-done.7.one = bf16[512,512]{1,0:T(8,128)(2,1)S(1)} collective-permute-done((bf16[512,512]{1,0:T(8,128)(2,1)S(1)}, bf16[512,512]{1,0:T(8,128)(2,1)S(1)}, u32[]{:S(2)}, u32[]{:S(2)}) %collective-permute-start.7) | collective-permute-done | bytes 524320 | tf_op jit(solution)/shard_map/ppermute | solution.py:31
  60.7 0.1 collective-permute-done.8.three
  60.9 0.2 shard_map.115
  61.1 3.7 %collective-permute-start.9 = (bf16[256,512]{1,0:T(8,128)(2,1)S(1)}, bf16[256,512]{1,0:T(8,128)(2,1)S(1)}, u32[]{:S(2)}, u32[]{:S(2)}) collective-permute-start(bf16[256,512]{1,0:T(8,128)(2,1)S(1)} %get-tuple-element.41), channel_id=1, source_target_pairs={{0,1},{32,33},{64,65},{96,97},{1,0},{33,32},{65,64},{97,96},{8,9},... | collective-permute-start | bytes 786440 | tf_op jit(solution)/shard_map/ppermute | solution.py:31
  64.8 3.8 %collective-permute-done.9.got = bf16[256,512]{1,0:T(8,128)(2,1)S(1)} collective-permute-done((bf16[256,512]{1,0:T(8,128)(2,1)S(1)}, bf16[256,512]{1,0:T(8,128)(2,1)S(1)}, u32[]{:S(2)}, u32[]{:S(2)}) %collective-permute-start.9) | collective-permute-done | bytes 262176 | tf_op jit(solution)/shard_map/ppermute | solution.py:31
  68.5 1.3 shard_map.116
  69.9 3.7 %collective-permute-start.10 = (f32[256,256]{1,0:T(8,128)S(1)}, f32[256,256]{1,0:T(8,128)S(1)}, u32[]{:S(2)}, u32[]{:S(2)}) collective-permute-start(f32[256,256]{1,0:T(8,128)S(1)} %get-tuple-element.45), channel_id=1, source_target_pairs={{0,32},{32,0},{64,96},{96,64},{1,33},{33,1},{65,97},{97,65},{8,40}... | collective-permute-start | bytes 786440 | tf_op jit(solution)/shard_map/ppermute | solution.py:31
  73.6 1.2 collective-permute-done.10.right
  74.8 1.4 collective-permute-start.11
  76.2 6.2 %collective-permute-done.11.right = f32[256,256]{1,0:T(8,128)S(1)} collective-permute-done((f32[256,256]{1,0:T(8,128)S(1)}, f32[256,256]{1,0:T(8,128)S(1)}, u32[]{:S(2)}, u32[]{:S(2)}) %collective-permute-start.11) | collective-permute-done | bytes 262176 | tf_op jit(solution)/shard_map/ppermute | solution.py:31
  82.4 1.3 collective-permute-start.12
  83.7 1.2 collective-permute-done.12.theirs
  84.9 1.1 shard_map.119
  86.0 5.6 %collective-permute-start.13 = (bf16[256,512]{1,0:T(8,128)(2,1)S(1)}, bf16[256,512]{1,0:T(8,128)(2,1)S(1)}, u32[]{:S(2)}, u32[]{:S(2)}) collective-permute-start(bf16[256,512]{1,0:T(8,128)(2,1)S(1)} %get-tuple-element.48.synced), channel_id=1, source_target_pairs={{32,65},{96,1},{1,96},{65,32},{40,73},{104,9},{9,104},{73,40},{48,... | collective-permute-start | bytes 786440 | tf_op jit(solution)/shard_map/ppermute | solution.py:31
  91.6 4.3 %collective-permute-done.13.got = bf16[256,512]{1,0:T(8,128)(2,1)S(1)} collective-permute-done((bf16[256,512]{1,0:T(8,128)(2,1)S(1)}, bf16[256,512]{1,0:T(8,128)(2,1)S(1)}, u32[]{:S(2)}, u32[]{:S(2)}) %collective-permute-start.13) | collective-permute-done | bytes 262176 | tf_op jit(solution)/shard_map/ppermute | solution.py:31
  95.9 1.1 collective-permute-start.14
  97.1 1.6 %collective-permute-start.15 = (bf16[256,512]{1,0:T(8,128)(2,1)S(1)}, bf16[256,512]{1,0:T(8,128)(2,1)S(1)}, u32[]{:S(2)}, u32[]{:S(2)}) collective-permute-start(bf16[256,512]{1,0:T(8,128)(2,1)S(1)} %shard_map.120.refs_0_), channel_id=1, source_target_pairs={{0,6},{32,56},{64,70},{96,120},{1,7},{33,57},{65,71},{97,121},{8,1... | collective-permute-start | bytes 786440 | tf_op jit(solution)/shard_map/ppermute | solution.py:31
  98.7 0.9 collective-permute-start.16
  99.6 2.8 %collective-permute-done.14.refs_1_ = bf16[256,512]{1,0:T(8,128)(2,1)S(1)} collective-permute-done((bf16[256,512]{1,0:T(8,128)(2,1)S(1)}, bf16[256,512]{1,0:T(8,128)(2,1)S(1)}, u32[]{:S(2)}, u32[]{:S(2)}) %collective-permute-start.14) | collective-permute-done | bytes 262176 | tf_op jit(solution)/shard_map/ppermute | solution.py:31
  102.4 2.4 %collective-permute-done.15.refs_2_ = bf16[256,512]{1,0:T(8,128)(2,1)S(1)} collective-permute-done((bf16[256,512]{1,0:T(8,128)(2,1)S(1)}, bf16[256,512]{1,0:T(8,128)(2,1)S(1)}, u32[]{:S(2)}, u32[]{:S(2)}) %collective-permute-start.15) | collective-permute-done | bytes 262176 | tf_op jit(solution)/shard_map/ppermute | solution.py:31
  104.8 1.3 collective-permute-done.16.refs_3_
  106.1 0.1 shard_map.121
  106.2 0.1 collective-permute-start.29
  106.3 1.1 collective-permute-start.17
  107.4 0.5 collective-permute-start.30
  107.9 2.7 %collective-permute-start.19 = (bf16[512,512]{1,0:T(8,128)(2,1)S(1)}, bf16[512,512]{1,0:T(8,128)(2,1)S(1)}, u32[]{:S(2)}, u32[]{:S(2)}) collective-permute-start(bf16[512,512]{1,0:T(8,128)(2,1)S(1)} %get-tuple-element.50.refs_1_), channel_id=1, source_target_pairs={{0,24},{32,38},{64,88},{96,102},{1,25},{33,39},{65,89},{97,103},{8... | collective-permute-start | bytes 1572872 | tf_op jit(solution)/shard_map/ppermute | solution.py:31
  110.6 2.7 %collective-permute-start.24 = (bf16[512,512]{1,0:T(8,128)(2,1)S(1)}, bf16[512,512]{1,0:T(8,128)(2,1)S(1)}, u32[]{:S(2)}, u32[]{:S(2)}) collective-permute-start(bf16[512,512]{1,0:T(8,128)(2,1)S(1)} %get-tuple-element.49.refs_0_), channel_id=1, source_target_pairs={{0,24},{32,38},{64,88},{96,102},{1,25},{33,39},{65,89},{97,103},{8... | collective-permute-start | bytes 1572872 | tf_op jit(solution)/shard_map/ppermute | solution.py:31
  113.3 2.6 %collective-permute-done.17.refs_0_ = bf16[512,512]{1,0:T(8,128)(2,1)S(1)} collective-permute-done((bf16[512,512]{1,0:T(8,128)(2,1)S(1)}, bf16[512,512]{1,0:T(8,128)(2,1)S(1)}, u32[]{:S(2)}, u32[]{:S(2)}) %collective-permute-start.17) | collective-permute-done | bytes 524320 | tf_op jit(solution)/shard_map/ppermute | solution.py:31
  115.9 1.3 collective-permute-start.27
  117.2 1.1 collective-permute-start.18
  118.2 1.9 %collective-permute-start.20 = (bf16[512,512]{1,0:T(8,128)(2,1)S(1)}, bf16[512,512]{1,0:T(8,128)(2,1)S(1)}, u32[]{:S(2)}, u32[]{:S(2)}) collective-permute-start(bf16[512,512]{1,0:T(8,128)(2,1)S(1)} %collective-permute-done.19.refs_1_), channel_id=1, source_target_pairs={{0,24},{32,38},{64,88},{96,102},{1,25},{33,39},{65,89},{97,103},{8... | collective-permute-start | bytes 1572872 | tf_op jit(solution)/shard_map/ppermute | solution.py:31
  120.1 1.4 collective-permute-done.23.refs_0_
  121.5 1.3 collective-permute-start.28
  122.8 0.5 collective-permute-start.26
  123.3 3.8 %collective-permute-done.18.refs_0_ = bf16[512,512]{1,0:T(8,128)(2,1)S(1)} collective-permute-done((bf16[512,512]{1,0:T(8,128)(2,1)S(1)}, bf16[512,512]{1,0:T(8,128)(2,1)S(1)}, u32[]{:S(2)}, u32[]{:S(2)}) %collective-permute-start.18) | collective-permute-done | bytes 524320 | tf_op jit(solution)/shard_map/ppermute | solution.py:31
  127.1 1.3 collective-permute-start.21
  128.4 0.0 collective-permute-start.22
  128.4 4.7 %shard_map.122.refs_4_ = f32[1024,512]{1,0:T(8,128)S(1)} custom-call(bf16[1024,8192]{1,0:T(8,128)(2,1)} %tok_ref.15, bf16[512,512]{1,0:T(8,128)(2,1)S(1)} %get-tuple-element.49.refs_0_, bf16[512,512]{1,0:T(8,128)(2,1)S(1)} %get-tuple-element.50.refs_1_, bf16[512,512]{1,0:T(8,128)(2,1)S(1)} %collective-permute-done.29.refs_2_, ...), custom_call_target="tpu_custom_call" | custom-call | flops 2147483648 | bytes 4194304 | tf_op jit(solution)/shard_map/pallas_call | solution.py:291
  133.1 4.1 %shard_map.123.refs_4_ = f32[1024,512]{1,0:T(8,128)S(1)} custom-call(bf16[1024,8192]{1,0:T(8,128)(2,1)} %tok_ref.15, bf16[512,512]{1,0:T(8,128)(2,1)S(1)} %collective-permute-done.17.refs_0_, bf16[512,512]{1,0:T(8,128)(2,1)S(1)} %collective-permute-done.19.refs_1_, bf16[512,512]{1,0:T(8,128)(2,1)S(1)} %collective-permute-done.27.refs_2_, ...), custom_call_target="tpu_custom_call" | custom-call | flops 2147483648 | bytes 4194304 | tf_op jit(solution)/shard_map/pallas_call | solution.py:291
  137.2 4.1 %shard_map.124.refs_4_ = f32[1024,512]{1,0:T(8,128)S(1)} custom-call(bf16[1024,8192]{1,0:T(8,128)(2,1)} %tok_ref.15, bf16[512,512]{1,0:T(8,128)(2,1)S(1)} %collective-permute-done.23.refs_0_, bf16[512,512]{1,0:T(8,128)(2,1)S(1)} %collective-permute-done.24.refs_1_, bf16[512,512]{1,0:T(8,128)(2,1)S(1)} %collective-permute-done.25.refs_2_, ...), custom_call_target="tpu_custom_call" | custom-call | flops 2147483648 | bytes 4194304 | tf_op jit(solution)/shard_map/pallas_call | solution.py:291
  141.3 5.0 %shard_map.125 = bf16[1024,512]{1,0:T(8,128)(2,1)} custom-call(bf16[1024,8192]{1,0:T(8,128)(2,1)} %tok_ref.15, bf16[512,512]{1,0:T(8,128)(2,1)S(1)} %collective-permute-done.18.refs_0_, bf16[512,512]{1,0:T(8,128)(2,1)S(1)} %collective-permute-done.20.refs_1_, bf16[512,512]{1,0:T(8,128)(2,1)S(1)} %collective-permute-done.21.refs_2_, ...), custom_call_target="tpu_custom_call" | custom-call | flops 2147483648 | bytes 4194304 | tf_op jit(solution)/shard_map/pallas_call | solution.py:291
  (28 shorter events, 0.2 us)
Async XLA Ops:
  0.6 1.2 copy-start
  6.2 16.1 %collective-permute-start.2 = (bf16[1024,512]{1,0:T(8,128)(2,1)S(1)}, bf16[1024,512]{1,0:T(8,128)(2,1)S(1)}, u32[]{:S(2)}, u32[]{:S(2)}) collective-permute-start(bf16[1024,512]{1,0:T(8,128)(2,1)S(1)} %get-tuple-element.32), channel_id=1, source_target_pairs={{0,2},{32,40},{64,66},{96,104},{1,3},{33,41},{65,67},{97,105},{8,1... | collective-permute-start | bytes 3145736 | tf_op jit(solution)/shard_map/ppermute | solution.py:31
  8.4 13.9 %copy-start.1 = (bf16[1024,512]{1,0:T(8,128)(2,1)S(1)}, bf16[1024,512]{1,0:T(8,128)(2,1)}, u32[]{:S(2)}) copy-start(bf16[1024,512]{1,0:T(8,128)(2,1)} %grad_ref.7) | copy-start | bytes 3145732
  8.4 13.9 %collective-permute-start.3 = (bf16[1024,512]{1,0:T(8,128)(2,1)S(1)}, bf16[1024,512]{1,0:T(8,128)(2,1)S(1)}, u32[]{:S(2)}, u32[]{:S(2)}) collective-permute-start(bf16[1024,512]{1,0:T(8,128)(2,1)S(1)} %get-tuple-element.33), channel_id=1, source_target_pairs={{0,6},{32,56},{64,70},{96,120},{1,7},{33,57},{65,71},{97,121},{8,1... | collective-permute-start | bytes 3145736 | tf_op jit(solution)/shard_map/ppermute | solution.py:31
  14.3 19.3 %collective-permute-start = (bf16[1024,512]{1,0:T(8,128)(2,1)S(1)}, bf16[1024,512]{1,0:T(8,128)(2,1)S(1)}, u32[]{:S(2)}, u32[]{:S(2)}) collective-permute-start(bf16[1024,512]{1,0:T(8,128)(2,1)S(1)} %get-tuple-element.28), channel_id=1, source_target_pairs={{0,6},{32,56},{64,70},{96,120},{1,7},{33,57},{65,71},{97,121},{8,1... | collective-permute-start | bytes 3145736 | tf_op jit(solution)/shard_map/ppermute | solution.py:31
  15.7 17.8 %collective-permute-start.1 = (bf16[1024,512]{1,0:T(8,128)(2,1)S(1)}, bf16[1024,512]{1,0:T(8,128)(2,1)S(1)}, u32[]{:S(2)}, u32[]{:S(2)}) collective-permute-start(bf16[1024,512]{1,0:T(8,128)(2,1)S(1)} %get-tuple-element.29), channel_id=1, source_target_pairs={{0,2},{32,40},{64,66},{96,104},{1,3},{33,41},{65,67},{97,105},{8,1... | collective-permute-start | bytes 3145736 | tf_op jit(solution)/shard_map/ppermute | solution.py:31
  26.7 18.1 %collective-permute-start.4 = (bf16[1024,512]{1,0:T(8,128)(2,1)S(1)}, bf16[1024,512]{1,0:T(8,128)(2,1)S(1)}, u32[]{:S(2)}, u32[]{:S(2)}) collective-permute-start(bf16[1024,512]{1,0:T(8,128)(2,1)S(1)} %get-tuple-element.34), channel_id=1, source_target_pairs={{0,2},{32,40},{64,66},{96,104},{1,3},{33,41},{65,67},{97,105},{8,1... | collective-permute-start | bytes 3145736 | tf_op jit(solution)/shard_map/ppermute | solution.py:31
  28.1 16.7 %collective-permute-start.5 = (bf16[1024,512]{1,0:T(8,128)(2,1)S(1)}, bf16[1024,512]{1,0:T(8,128)(2,1)S(1)}, u32[]{:S(2)}, u32[]{:S(2)}) collective-permute-start(bf16[1024,512]{1,0:T(8,128)(2,1)S(1)} %get-tuple-element.35), channel_id=1, source_target_pairs={{0,6},{32,56},{64,70},{96,120},{1,7},{33,57},{65,71},{97,121},{8,1... | collective-permute-start | bytes 3145736 | tf_op jit(solution)/shard_map/ppermute | solution.py:31
  45.2 23.4 %copy-start.2 = (f32[256,512]{1,0:T(8,128)S(1)}, f32[256,512]{1,0:T(8,128)}, u32[]{:S(2)}) copy-start(f32[256,512]{1,0:T(8,128)} %weights_ref.3) | copy-start | bytes 1572868
  45.2 23.3 %copy-start.4 = (f32[1,256,512]{2,1,0:T(8,128)S(1)}, f32[1,256,512]{2,1,0:T(8,128)}, u32[]{:S(2)}) copy-start(f32[1,256,512]{2,1,0:T(8,128)} %param.9) | copy-start | bytes 1572868
  45.2 23.3 %copy-start.5 = (f32[1,256,512]{2,1,0:T(8,128)S(1)}, f32[1,256,512]{2,1,0:T(8,128)}, u32[]{:S(2)}) copy-start(f32[1,256,512]{2,1,0:T(8,128)} %param.10) | copy-start | bytes 1572868
  45.2 23.3 %copy-start.6 = (f32[1,256,512]{2,1,0:T(8,128)S(1)}, f32[1,256,512]{2,1,0:T(8,128)}, u32[]{:S(2)}) copy-start(f32[1,256,512]{2,1,0:T(8,128)} %param.11) | copy-start | bytes 1572868
  45.2 10.0 %collective-permute-start.6 = (bf16[512,512]{1,0:T(8,128)(2,1)S(1)}, bf16[512,512]{1,0:T(8,128)(2,1)S(1)}, u32[]{:S(2)}, u32[]{:S(2)}) collective-permute-start(bf16[512,512]{1,0:T(8,128)(2,1)S(1)} %get-tuple-element.37), channel_id=1, source_target_pairs={{0,16},{32,36},{64,80},{96,100},{1,17},{33,37},{65,81},{97,101},{8... | collective-permute-start | bytes 1572872 | tf_op jit(solution)/shard_map/ppermute | solution.py:31
  48.0 12.7 %collective-permute-start.7 = (bf16[512,512]{1,0:T(8,128)(2,1)S(1)}, bf16[512,512]{1,0:T(8,128)(2,1)S(1)}, u32[]{:S(2)}, u32[]{:S(2)}) collective-permute-start(bf16[512,512]{1,0:T(8,128)(2,1)S(1)} %get-tuple-element.38), channel_id=1, source_target_pairs={{0,8},{32,34},{64,72},{96,98},{1,9},{33,35},{65,73},{97,99},{8,16}... | collective-permute-start | bytes 1572872 | tf_op jit(solution)/shard_map/ppermute | solution.py:31
  48.4 12.5 %collective-permute-start.8 = (bf16[512,512]{1,0:T(8,128)(2,1)S(1)}, bf16[512,512]{1,0:T(8,128)(2,1)S(1)}, u32[]{:S(2)}, u32[]{:S(2)}) collective-permute-start(bf16[512,512]{1,0:T(8,128)(2,1)S(1)} %get-tuple-element.39), channel_id=1, source_target_pairs={{0,24},{32,38},{64,88},{96,102},{1,25},{33,39},{65,89},{97,103},{8... | collective-permute-start | bytes 1572872 | tf_op jit(solution)/shard_map/ppermute | solution.py:31
  61.1 7.4 %collective-permute-start.9 = (bf16[256,512]{1,0:T(8,128)(2,1)S(1)}, bf16[256,512]{1,0:T(8,128)(2,1)S(1)}, u32[]{:S(2)}, u32[]{:S(2)}) collective-permute-start(bf16[256,512]{1,0:T(8,128)(2,1)S(1)} %get-tuple-element.41), channel_id=1, source_target_pairs={{0,1},{32,33},{64,65},{96,97},{1,0},{33,32},{65,64},{97,96},{8,9},... | collective-permute-start | bytes 786440 | tf_op jit(solution)/shard_map/ppermute | solution.py:31
  68.5 16.3 %copy-start.3 = (f32[256,512]{1,0:T(8,128)S(1)}, f32[256,512]{1,0:T(8,128)}, u32[]{:S(2)}) copy-start(f32[256,512]{1,0:T(8,128)} %momentum_ref.1) | copy-start | bytes 1572868
  69.9 4.9 %collective-permute-start.10 = (f32[256,256]{1,0:T(8,128)S(1)}, f32[256,256]{1,0:T(8,128)S(1)}, u32[]{:S(2)}, u32[]{:S(2)}) collective-permute-start(f32[256,256]{1,0:T(8,128)S(1)} %get-tuple-element.45), channel_id=1, source_target_pairs={{0,32},{32,0},{64,96},{96,64},{1,33},{33,1},{65,97},{97,65},{8,40}... | collective-permute-start | bytes 786440 | tf_op jit(solution)/shard_map/ppermute | solution.py:31
  74.8 7.6 %collective-permute-start.11 = (f32[256,256]{1,0:T(8,128)S(1)}, f32[256,256]{1,0:T(8,128)S(1)}, u32[]{:S(2)}, u32[]{:S(2)}) collective-permute-start(f32[256,256]{1,0:T(8,128)S(1)} %shard_map.117.left), channel_id=1, source_target_pairs={{0,64},{32,96},{64,0},{96,32},{1,65},{33,97},{65,1},{97,33},{8,72}... | collective-permute-start | bytes 786440 | tf_op jit(solution)/shard_map/ppermute | solution.py:31
  82.4 2.4 %collective-permute-start.12 = (f32[256,256]{1,0:T(8,128)S(1)}, f32[256,256]{1,0:T(8,128)S(1)}, u32[]{:S(2)}, u32[]{:S(2)}) collective-permute-start(f32[256,256]{1,0:T(8,128)S(1)} %shard_map.118.mine), channel_id=1, source_target_pairs={{0,32},{32,0},{64,96},{96,64},{1,33},{33,1},{65,97},{97,65},{8,40}... | collective-permute-start | bytes 786440 | tf_op jit(solution)/shard_map/ppermute | solution.py:31
  86.0 9.9 %collective-permute-start.13 = (bf16[256,512]{1,0:T(8,128)(2,1)S(1)}, bf16[256,512]{1,0:T(8,128)(2,1)S(1)}, u32[]{:S(2)}, u32[]{:S(2)}) collective-permute-start(bf16[256,512]{1,0:T(8,128)(2,1)S(1)} %get-tuple-element.48.synced), channel_id=1, source_target_pairs={{32,65},{96,1},{1,96},{65,32},{40,73},{104,9},{9,104},{73,40},{48,... | collective-permute-start | bytes 786440 | tf_op jit(solution)/shard_map/ppermute | solution.py:31
  95.9 6.5 %collective-permute-start.14 = (bf16[256,512]{1,0:T(8,128)(2,1)S(1)}, bf16[256,512]{1,0:T(8,128)(2,1)S(1)}, u32[]{:S(2)}, u32[]{:S(2)}) collective-permute-start(bf16[256,512]{1,0:T(8,128)(2,1)S(1)} %shard_map.120.refs_0_), channel_id=1, source_target_pairs={{0,2},{32,40},{64,66},{96,104},{1,3},{33,41},{65,67},{97,105},{8,1... | collective-permute-start | bytes 786440 | tf_op jit(solution)/shard_map/ppermute | solution.py:31
  97.1 7.7 %collective-permute-start.15 = (bf16[256,512]{1,0:T(8,128)(2,1)S(1)}, bf16[256,512]{1,0:T(8,128)(2,1)S(1)}, u32[]{:S(2)}, u32[]{:S(2)}) collective-permute-start(bf16[256,512]{1,0:T(8,128)(2,1)S(1)} %shard_map.120.refs_0_), channel_id=1, source_target_pairs={{0,6},{32,56},{64,70},{96,120},{1,7},{33,57},{65,71},{97,121},{8,1... | collective-permute-start | bytes 786440 | tf_op jit(solution)/shard_map/ppermute | solution.py:31
  98.7 7.4 %collective-permute-start.16 = (bf16[256,512]{1,0:T(8,128)(2,1)S(1)}, bf16[256,512]{1,0:T(8,128)(2,1)S(1)}, u32[]{:S(2)}, u32[]{:S(2)}) collective-permute-start(bf16[256,512]{1,0:T(8,128)(2,1)S(1)} %shard_map.120.refs_0_), channel_id=1, source_target_pairs={{0,4},{32,48},{64,68},{96,112},{1,5},{33,49},{65,69},{97,113},{8,1... | collective-permute-start | bytes 786440 | tf_op jit(solution)/shard_map/ppermute | solution.py:31
  106.2 4.4 %collective-permute-start.29 = (bf16[512,512]{1,0:T(8,128)(2,1)S(1)}, bf16[512,512]{1,0:T(8,128)(2,1)S(1)}, u32[]{:S(2)}, u32[]{:S(2)}) collective-permute-start(bf16[512,512]{1,0:T(8,128)(2,1)S(1)} %get-tuple-element.49.refs_0_), channel_id=1, source_target_pairs={{0,32},{32,0},{64,96},{96,64},{1,33},{33,1},{65,97},{97,65},{8,40}... | collective-permute-start | bytes 1572872 | tf_op jit(solution)/shard_map/ppermute | solution.py:31
  106.3 9.6 %collective-permute-start.17 = (bf16[512,512]{1,0:T(8,128)(2,1)S(1)}, bf16[512,512]{1,0:T(8,128)(2,1)S(1)}, u32[]{:S(2)}, u32[]{:S(2)}) collective-permute-start(bf16[512,512]{1,0:T(8,128)(2,1)S(1)} %get-tuple-element.49.refs_0_), channel_id=1, source_target_pairs={{0,8},{32,34},{64,72},{96,98},{1,9},{33,35},{65,73},{97,99},{8,16}... | collective-permute-start | bytes 1572872 | tf_op jit(solution)/shard_map/ppermute | solution.py:31
  107.4 9.8 %collective-permute-start.30 = (bf16[512,512]{1,0:T(8,128)(2,1)S(1)}, bf16[512,512]{1,0:T(8,128)(2,1)S(1)}, u32[]{:S(2)}, u32[]{:S(2)}) collective-permute-start(bf16[512,512]{1,0:T(8,128)(2,1)S(1)} %get-tuple-element.50.refs_1_), channel_id=1, source_target_pairs={{0,32},{32,0},{64,96},{96,64},{1,33},{33,1},{65,97},{97,65},{8,40}... | collective-permute-start | bytes 1572872 | tf_op jit(solution)/shard_map/ppermute | solution.py:31
  107.9 10.3 %collective-permute-start.19 = (bf16[512,512]{1,0:T(8,128)(2,1)S(1)}, bf16[512,512]{1,0:T(8,128)(2,1)S(1)}, u32[]{:S(2)}, u32[]{:S(2)}) collective-permute-start(bf16[512,512]{1,0:T(8,128)(2,1)S(1)} %get-tuple-element.50.refs_1_), channel_id=1, source_target_pairs={{0,24},{32,38},{64,88},{96,102},{1,25},{33,39},{65,89},{97,103},{8... | collective-permute-start | bytes 1572872 | tf_op jit(solution)/shard_map/ppermute | solution.py:31
  110.6 10.9 %collective-permute-start.23 = (bf16[512,512]{1,0:T(8,128)(2,1)S(1)}, bf16[512,512]{1,0:T(8,128)(2,1)S(1)}, u32[]{:S(2)}, u32[]{:S(2)}) collective-permute-start(bf16[512,512]{1,0:T(8,128)(2,1)S(1)} %get-tuple-element.50.refs_1_), channel_id=1, source_target_pairs={{0,8},{32,34},{64,72},{96,98},{1,9},{33,35},{65,73},{97,99},{8,16}... | collective-permute-start | bytes 1572872 | tf_op jit(solution)/shard_map/ppermute | solution.py:31
  110.6 12.2 %collective-permute-start.24 = (bf16[512,512]{1,0:T(8,128)(2,1)S(1)}, bf16[512,512]{1,0:T(8,128)(2,1)S(1)}, u32[]{:S(2)}, u32[]{:S(2)}) collective-permute-start(bf16[512,512]{1,0:T(8,128)(2,1)S(1)} %get-tuple-element.49.refs_0_), channel_id=1, source_target_pairs={{0,24},{32,38},{64,88},{96,102},{1,25},{33,39},{65,89},{97,103},{8... | collective-permute-start | bytes 1572872 | tf_op jit(solution)/shard_map/ppermute | solution.py:31
  115.9 6.9 %collective-permute-start.27 = (bf16[512,512]{1,0:T(8,128)(2,1)S(1)}, bf16[512,512]{1,0:T(8,128)(2,1)S(1)}, u32[]{:S(2)}, u32[]{:S(2)}) collective-permute-start(bf16[512,512]{1,0:T(8,128)(2,1)S(1)} %collective-permute-done.17.refs_0_), channel_id=1, source_target_pairs={{0,32},{32,0},{64,96},{96,64},{1,33},{33,1},{65,97},{97,65},{8,40}... | collective-permute-start | bytes 1572872 | tf_op jit(solution)/shard_map/ppermute | solution.py:31
  117.2 10.0 %collective-permute-start.18 = (bf16[512,512]{1,0:T(8,128)(2,1)S(1)}, bf16[512,512]{1,0:T(8,128)(2,1)S(1)}, u32[]{:S(2)}, u32[]{:S(2)}) collective-permute-start(bf16[512,512]{1,0:T(8,128)(2,1)S(1)} %collective-permute-done.17.refs_0_), channel_id=1, source_target_pairs={{0,8},{32,34},{64,72},{96,98},{1,9},{33,35},{65,73},{97,99},{8,16}... | collective-permute-start | bytes 1572872 | tf_op jit(solution)/shard_map/ppermute | solution.py:31
  118.2 10.2 %collective-permute-start.20 = (bf16[512,512]{1,0:T(8,128)(2,1)S(1)}, bf16[512,512]{1,0:T(8,128)(2,1)S(1)}, u32[]{:S(2)}, u32[]{:S(2)}) collective-permute-start(bf16[512,512]{1,0:T(8,128)(2,1)S(1)} %collective-permute-done.19.refs_1_), channel_id=1, source_target_pairs={{0,24},{32,38},{64,88},{96,102},{1,25},{33,39},{65,89},{97,103},{8... | collective-permute-start | bytes 1572872 | tf_op jit(solution)/shard_map/ppermute | solution.py:31
  121.5 11.6 %collective-permute-start.28 = (bf16[512,512]{1,0:T(8,128)(2,1)S(1)}, bf16[512,512]{1,0:T(8,128)(2,1)S(1)}, u32[]{:S(2)}, u32[]{:S(2)}) collective-permute-start(bf16[512,512]{1,0:T(8,128)(2,1)S(1)} %collective-permute-done.19.refs_1_), channel_id=1, source_target_pairs={{0,32},{32,0},{64,96},{96,64},{1,33},{33,1},{65,97},{97,65},{8,40}... | collective-permute-start | bytes 1572872 | tf_op jit(solution)/shard_map/ppermute | solution.py:31
  122.8 14.4 %collective-permute-start.25 = (bf16[512,512]{1,0:T(8,128)(2,1)S(1)}, bf16[512,512]{1,0:T(8,128)(2,1)S(1)}, u32[]{:S(2)}, u32[]{:S(2)}) collective-permute-start(bf16[512,512]{1,0:T(8,128)(2,1)S(1)} %collective-permute-done.23.refs_0_), channel_id=1, source_target_pairs={{0,32},{32,0},{64,96},{96,64},{1,33},{33,1},{65,97},{97,65},{8,40}... | collective-permute-start | bytes 1572872 | tf_op jit(solution)/shard_map/ppermute | solution.py:31
  122.8 14.4 %collective-permute-start.26 = (bf16[512,512]{1,0:T(8,128)(2,1)S(1)}, bf16[512,512]{1,0:T(8,128)(2,1)S(1)}, u32[]{:S(2)}, u32[]{:S(2)}) collective-permute-start(bf16[512,512]{1,0:T(8,128)(2,1)S(1)} %collective-permute-done.24.refs_1_), channel_id=1, source_target_pairs={{0,32},{32,0},{64,96},{96,64},{1,33},{33,1},{65,97},{97,65},{8,40}... | collective-permute-start | bytes 1572872 | tf_op jit(solution)/shard_map/ppermute | solution.py:31
  127.1 14.2 %collective-permute-start.21 = (bf16[512,512]{1,0:T(8,128)(2,1)S(1)}, bf16[512,512]{1,0:T(8,128)(2,1)S(1)}, u32[]{:S(2)}, u32[]{:S(2)}) collective-permute-start(bf16[512,512]{1,0:T(8,128)(2,1)S(1)} %collective-permute-done.18.refs_0_), channel_id=1, source_target_pairs={{0,32},{32,0},{64,96},{96,64},{1,33},{33,1},{65,97},{97,65},{8,40}... | collective-permute-start | bytes 1572872 | tf_op jit(solution)/shard_map/ppermute | solution.py:31
  128.4 12.9 %collective-permute-start.22 = (bf16[512,512]{1,0:T(8,128)(2,1)S(1)}, bf16[512,512]{1,0:T(8,128)(2,1)S(1)}, u32[]{:S(2)}, u32[]{:S(2)}) collective-permute-start(bf16[512,512]{1,0:T(8,128)(2,1)S(1)} %collective-permute-done.20.refs_1_), channel_id=1, source_target_pairs={{0,32},{32,0},{64,96},{96,64},{1,33},{33,1},{65,97},{97,65},{8,40}... | collective-permute-start | bytes 1572872 | tf_op jit(solution)/shard_map/ppermute | solution.py:31

commit v3 on v2

v3 whole, which is shorter than its diff:
```python
import functools

import jax
import jax.numpy as jnp
from jax import lax
from jax.experimental import pallas as pl
from jax.experimental.pallas import tpu as pltpu
from jax.sharding import PartitionSpec as P

BOTH = ("replica", "fsdp")
BF16, F32 = jnp.bfloat16, jnp.float32
H1, H2 = (2, 1), (3, 0)
VMEM = pl.BlockSpec(memory_space=pltpu.VMEM)
ANY = pl.BlockSpec(memory_space=pl.ANY)
SMALL = pl.CostEstimate(flops=1, bytes_accessed=1, transcendentals=0)


def flat(x, y, z, c):
    x, y, z = x % 4, y % 4, z % 4
    return ((z % 2) * 2 + c) * 32 + (y * 4 + x) * 2 + z // 2


def permute(array, move):
    pairs = []
    for x in range(4):
        for y in range(4):
            for z in range(4):
                for c in range(2):
                    target = move(x, y, z, c)
                    if target is not None:
                        pairs.append((flat(x, y, z, c), flat(*target)))
    return lax.ppermute(array, BOTH, pairs)


def first(step):
    return lambda x, y, z, c: (x, y + step, z, c) if c else (x + step, y, z, c)


def second(step):
    return lambda x, y, z, c: (x + step, y, z, c) if c else (x, y + step, z, c)


def other_core(x, y, z, c):
    return x, y, z, 1 - c


def pair_lo(x, y, z, c):
    return x, y, z ^ 1, c


def halves_one(x, y, z, c):
    return (x, y, 3 - z, c) if z // 2 == c else (x, y, z, 1 - c)


def halves_two(x, y, z, c):
    return None if z // 2 == c else (x, y, 3 - z, 1 - c)


def across(x, y, z, c):
    return x, y, z + 2, c


def z_hi():
    return lax.rem(lax.axis_index("fsdp"), 2)


def core_index():
    return lax.rem(lax.axis_index("replica"), 2)


def plane(core, k1, k2):
    f = lax.axis_index("fsdp")
    y, x = lax.div(f, 8), lax.rem(lax.div(f, 2), 4)
    dx, dy = k1 + core * (k2 - k1), k2 + core * (k1 - k2)
    return lax.rem(y + dy, 4) * 4 + lax.rem(x + dx, 4)


def local(kernel, outs, *arrays, limit=16):
    return pl.pallas_call(
        kernel,
        in_specs=[VMEM] * len(arrays),
        out_specs=[VMEM] * len(outs),
        out_shape=[jax.ShapeDtypeStruct(*out) for out in outs],
        compiler_params=pltpu.CompilerParams(vmem_limit_bytes=limit << 20),
    )(*arrays)


def columns(tok_ref, start, width):
    return tok_ref.at[:, pl.ds(pl.multiple_of(start, 128), width)]


def started(copies):
    for copy in copies:
        copy.start()
    return copies


def cost(rows, width, cols):
    return pl.CostEstimate(
        flops=2 * rows * width * cols, bytes_accessed=2 * rows * width, transcendentals=0
    )


def grad_kernel(names, n_recv, tok_ref, grad_ref, *refs):
    groups = len(names) // 2
    recv, outs = refs[:n_recv], refs[n_recv : n_recv + groups]
    held, g_ref, sems = refs[n_recv + groups :]
    g_copy = pltpu.make_async_copy(grad_ref, g_ref, sems.at[len(names)])
    g_copy.start()
    copies = started(
        [
            pltpu.make_async_copy(
                columns(tok_ref, plane(core_index(), *name) * 512, 512),
                held.at[:, 512 * number : 512 * number + 512],
                sems.at[number],
            )
            for number, name in enumerate(names)
        ]
    )
    g_copy.wait()
    for number in range(len(names)):
        copies[number].wait()
        group, rows = number // 2, slice(512 * (number % 2), 512 * (number % 2) + 512)
        term = lax.dot_general(
            held[:, 512 * number : 512 * number + 512],
            g_ref[...],
            (((0,), (0,)), ((), ())),
            preferred_element_type=F32,
        )
        if recv:
            term = term + recv[group][rows].astype(F32)
        outs[group][rows] = term.astype(outs[group].dtype)


def grad_blocks(groups, dtype, limit, tokens, out_grad, *recv):
    names = [(k1, k2) for k1, half in groups for k2 in half]
    width, cols = 512 * len(names), out_grad.shape[1]
    return pl.pallas_call(
        functools.partial(grad_kernel, names, len(recv)),
        in_specs=[ANY, ANY] + [VMEM] * len(recv),
        out_specs=[VMEM] * len(groups),
        out_shape=[jax.ShapeDtypeStruct((1024, cols), dtype)] * len(groups),
        scratch_shapes=[
            pltpu.VMEM((tokens.shape[0], width), BF16),
            pltpu.VMEM(out_grad.shape, BF16),
            pltpu.SemaphoreType.DMA((len(names) + 1,)),
        ],
        compiler_params=pltpu.CompilerParams(vmem_limit_bytes=limit << 20),
        cost_estimate=cost(tokens.shape[0], width, cols),
    )(tokens, out_grad, *recv)


def total_kernel(own1, own2, got1, got2, *outs):
    mine = z_hi()
    for number, (own, got, start) in enumerate(
        ((own1, got1, 0), (own1, got1, 512), (own2, got2, 0), (own2, got2, 512))
    ):
        for which, out in ((1 - mine, outs[number]), (mine, outs[4 + number])):
            rows = pl.ds(pl.multiple_of(start + which * 256, 256), 256)
            out[...] = (own[rows] + got[rows].astype(F32)).astype(out.dtype)


def sum_kernel(zero, *refs):
    *refs, out = refs
    total = zero[...]
    for ref in refs:
        total = total + ref[...].astype(F32)
    out[...] = total.astype(out.dtype)


def reduce_scatter(tokens, out_grad):
    def send(arrays):
        return permute(arrays[0], first(1)), permute(arrays[1], first(-1))

    def blocks(groups, dtype, limit, *recv):
        return grad_blocks(groups, dtype, limit, tokens, out_grad, *recv)

    up1, down1 = send(blocks([(2, H1), (2, H2)], BF16, 50))
    up2, down2 = send(blocks([(1, H2), (3, H1)], BF16, 46))
    up3, down3 = send(blocks([(1, H1), (3, H2)], BF16, 46, up1, down1))
    own1, own2 = blocks([(0, H1), (0, H2)], F32, 46, down2, up2)
    block = (256, 512)
    sums = local(
        total_kernel,
        [(block, BF16), (block, BF16), (block, BF16), (block, F32)] * 2,
        own1,
        own2,
        up3,
        down3,
    )

    def exchange(two, one, three, zero):
        return zero, permute(two, second(2)), permute(one, second(1)), permute(three, second(-1))

    (give,) = local(sum_kernel, [(block, BF16)], *exchange(*sums[:4]))
    (keep,) = local(sum_kernel, [(block, F32)], *exchange(*sums[4:]))
    give, tokens = lax.optimization_barrier((give, tokens))
    got, held = lax.optimization_barrier((permute(give, across), arrange(ORDER, tokens)))
    return keep, got, held


def update_kernel(
    scale, keep, got, inner_ref, first_ref, second_ref, first_out, second_out, mine, other
):
    grad = (keep[...] + got[...].astype(F32)) * scale
    new_first = 0.9 * first_ref[...] + 0.1 * grad
    new_second = 0.95 * second_ref[...] + 0.05 * grad * grad
    inner = inner_ref[...]
    stepped = inner - 0.25 * (new_first / (jnp.sqrt(new_second) + 1e-08) + 0.1 * inner)
    first_out[...] = new_first
    second_out[...] = new_second
    half = stepped.shape[1] // 2
    core = core_index()
    for which, out in ((core, mine), (1 - core, other)):
        out[...] = jnp.where(which == 0, stepped[:, :half], stepped[:, half:])


def add_kernel(left, right, out):
    out[...] = (left[...].astype(F32) + right[...].astype(F32)).astype(out.dtype)


def outer(total, weights, momentum, n_replica):
    pseudo = weights - total / n_replica
    new_momentum = 0.9 * momentum + pseudo
    return weights - 0.7 * (pseudo + 0.9 * new_momentum), new_momentum


def synced_kernel(n_replica, left, right, weights_ref, momentum_ref, total, synced):
    half = left.shape[1]
    both = left[...].astype(F32) + right[...].astype(F32)
    total[...] = both
    low = core_index() == 0
    weights, momentum = (
        jnp.where(low, ref[:, :half], ref[:, half:]) for ref in (weights_ref, momentum_ref)
    )
    synced[...] = outer(both, weights, momentum, n_replica)[0].astype(BF16)


def outer_kernel(n_replica, mine, theirs, weights_ref, momentum_ref, weights_out, momentum_out):
    half = mine.shape[1]
    low = core_index() == 0
    left, right = mine[...], theirs[...]
    for part, total in (
        (slice(0, half), jnp.where(low, left, right)),
        (slice(half, 2 * half), jnp.where(low, right, left)),
    ):
        weights_out[:, part], momentum_out[:, part] = outer(
            total, weights_ref[:, part], momentum_ref[:, part], n_replica
        )


def join_kernel(mine, one, two, out):
    half = mine.shape[1]
    core = core_index()
    own = z_hi() == core
    same = jnp.where(own, mine[...], one[...])
    cross = jnp.where(own, one[...], two[...])
    out[:, :half] = jnp.where(core == 0, same, cross)
    out[:, half:] = jnp.where(core == 0, cross, same)


def mid_kernel(*refs):
    *ins, mid, near = refs
    for number, ref in enumerate(ins):
        near[256 * number : 256 * number + 256] = ref[...]
        if number < 3:
            mid[256 * number : 256 * number + 256] = ref[...]


def cut_kernel(up, down, up_out, down_out):
    rows = up_out.shape[0]
    up_out[...] = up[:rows]
    down_out[...] = down[rows:]


def arrange_kernel(places, tok_ref, out, sems):
    core = core_index()
    copies = started(
        [
            pltpu.make_async_copy(
                columns(tok_ref, plane(who, *place) * 512 + who * 256, 256),
                out.at[:, 256 * number : 256 * number + 256],
                sems.at[number],
            )
            for number, (partner, place) in enumerate(places)
            for who in (1 - core if partner else core,)
        ]
    )
    for copy in copies:
        copy.wait()


def arrange(places, tokens):
    return pl.pallas_call(
        functools.partial(arrange_kernel, places),
        in_specs=[ANY],
        out_specs=VMEM,
        out_shape=jax.ShapeDtypeStruct((tokens.shape[0], 256 * len(places)), BF16),
        scratch_shapes=[pltpu.SemaphoreType.DMA((len(places),))],
        compiler_params=pltpu.CompilerParams(vmem_limit_bytes=34 << 20),
        cost_estimate=SMALL,
    )(tokens)


def project_kernel(start, carried, scale, held, *refs):
    *arrays, out, right, sems = refs
    if carried:
        *arrays, acc = arrays
    copies, at = [], 0
    for number, ref in enumerate(arrays):
        rows = ref.shape[0]
        copies.append(pltpu.make_async_copy(ref, right.at[at : at + rows], sems.at[number]))
        at += rows
    for copy in started(copies):
        copy.wait()
    total = jnp.dot(held[:, start : start + at], right[...], preferred_element_type=F32)
    if carried:
        total = total + acc[...]
    out[...] = total if scale is None else (total * scale).astype(BF16)


def project(held, start, arrays, acc, scale):
    carried = [] if acc is None else [acc]
    rows, cols = held.shape[0], arrays[0].shape[1]
    return pl.pallas_call(
        functools.partial(project_kernel, start, bool(carried), scale),
        in_specs=[VMEM] * (1 + len(arrays) + len(carried)),
        out_specs=VMEM,
        out_shape=jax.ShapeDtypeStruct((rows, cols), F32 if scale is None else BF16),
        scratch_shapes=[
            pltpu.VMEM((sum(array.shape[0] for array in arrays), cols), BF16),
            pltpu.SemaphoreType.DMA((len(arrays),)),
        ],
        compiler_params=pltpu.CompilerParams(vmem_limit_bytes=16 << 20),
        cost_estimate=SMALL,
    )(held, *arrays, *carried)


def swap(arrays):
    return [permute(array, other_core) for array in arrays]


NEAR = [(3, 0), (1, 0), (2, 0), (0, 0), (0, 3), (0, 1)]
MIDDLE = [(3, 3), (1, 3), (2, 3), (3, 1), (1, 1), (2, 1)]
FAR = [(0, 2), (3, 2), (1, 2), (2, 2)]
ORDER = [
    (partner, place) for part in (NEAR, MIDDLE, FAR) for partner in range(2) for place in part
]


def gather_project(synced, held, scale, finish):
    quarter = ((256, 512), BF16)
    (own,) = local(
        join_kernel, [quarter], synced, permute(synced, halves_one), permute(synced, halves_two)
    )
    own_down, own_up = permute(own, second(-1)), permute(own, second(1))
    far = permute(own, first(2))
    ahead, behind = permute(own, first(-1)), permute(own, first(1))
    behind, ahead, far, own_up, own_down = lax.optimization_barrier(
        (behind, ahead, far, own_up, own_down)
    )
    mid, one = local(
        mid_kernel,
        [((768, 512), BF16), ((1536, 512), BF16)],
        behind,
        ahead,
        far,
        own,
        own_up,
        own_down,
    )
    mid_up, mid_down = permute(mid, second(1)), permute(mid, second(-1))
    own_far = permute(own_up, second(1))
    acc = project(held, 0, [one, *swap([one])], None, None)
    mid_up, mid_down, acc = lax.optimization_barrier((mid_up, mid_down, acc))
    cut_up, cut_down = local(
        cut_kernel, [((256, 512), BF16), ((512, 512), BF16)], mid_up, mid_down
    )
    far_down, far_up = permute(cut_down, second(-1)), permute(cut_up, second(1))
    two = [mid_up, mid_down]
    theirs = swap(two)
    finished = finish(acc)
    acc = project(held, 3072, two, acc, None)
    acc = project(held, 4608, theirs, acc, None)
    three = [own_far, far_up, far_down]
    *three, acc, new_global, new_momentum = lax.optimization_barrier((*three, acc, *finished))
    theirs = swap(three)
    acc = project(held, 6144, three, acc, None)
    return project(held, 7168, theirs, acc, scale), new_global, new_momentum


def body(
    tokens, out_grad, inner_weights, first_moment, second_moment, global_weights, outer_momentum
):
    scale = 1.0 / tokens.shape[1] ** 0.5
    n_replica = lax.axis_size("replica")
    keep, got, held = reduce_scatter(tokens, out_grad)
    block, half = keep.shape, (keep.shape[0], keep.shape[1] // 2)
    new_first, new_second, mine, other = local(
        functools.partial(update_kernel, scale),
        [(block, F32), (block, F32), (half, F32), (half, F32)],
        keep,
        got,
        inner_weights[0],
        first_moment[0],
        second_moment[0],
    )
    (mine,) = local(add_kernel, [(half, BF16)], mine, permute(other, other_core))
    total, synced = local(
        functools.partial(synced_kernel, n_replica),
        [(half, F32), (half, BF16)],
        mine,
        permute(mine, pair_lo),
        global_weights,
        outer_momentum,
    )

    def finish(after):
        mine, _ = lax.optimization_barrier((total, after))
        return local(
            functools.partial(outer_kernel, n_replica),
            [(block, F32), (block, F32)],
            mine,
            permute(mine, other_core),
            global_weights,
            outer_momentum,
        )

    projected, new_global, new_momentum = gather_project(synced, held, scale, finish)
    return (new_first[None], new_second[None], new_global, new_momentum, projected)


def solution(mesh):
    placed = (
        P(("replica", "fsdp"), None),
        P(("replica", "fsdp"), None),
        P("replica", "fsdp", None),
        P("replica", "fsdp", None),
        P("replica", "fsdp", None),
        P("fsdp", None),
        P("fsdp", None),
    )
    return jax.shard_map(
        body,
        mesh=mesh,
        in_specs=placed,
        out_specs=(
            P("replica", "fsdp", None),
            P("replica", "fsdp", None),
            P("fsdp", None),
            P("fsdp", None),
            P(("replica", "fsdp"), None),
        ),
        check_vma=False,
    )
```

time: 147 us -> 135 us (0.918)
  waiting for transfers between devices: 58.5 us -> 47.8 us
  starting transfers between devices: 47.3 us -> 45.6 us
    ppermute x31 -> x34, waiting for transfers between devices: 58.5 us -> 47.8 us  [permute(): return lax.ppermute(array, BOTH, pairs)]
    ppermute x31 -> x34, starting transfers between devices: 47.3 us -> 45.6 us  [permute(): return lax.ppermute(array, BOTH, pairs)]
    pallas_call x4 -> x6, Pallas kernels: 17.9 us -> 17.4 us  [the longest x5 11.1 us: project(): pl.pallas_call(functools.partial(project_kernel, start, bool(carried), sc...]
    pallas_call x8 -> x10, Pallas kernels: 3.18 us -> 3.38 us  [local(): pl.pallas_call(kernel, in_specs=[VMEM] * len(arrays), out_specs=[VMEM] *...]
  transfers between devices with their start and end apart: 31 -> 34, of which waited for: 17 -> 18; matrix products, arithmetic and copies ran while one was open for 0% -> 0% of each run, Pallas kernels for 18% -> 22%
where the time goes in v3:
time: 135 us
  waiting for transfers between devices  47.8 us (35%)
  starting transfers between devices  45.6 us (34%)
  Pallas kernels  38.2 us (28%)
  local copies, waits for them, and re-layouts  2.4 us (2%)
    ppermute x34, waiting for transfers between devices, permute(): return lax.ppermute(array, BOTH, pairs)  47.8 us
    ppermute x34, starting transfers between devices, permute(): return lax.ppermute(array, BOTH, pairs)  45.6 us
    pallas_call x4, Pallas kernels, grad_blocks(): pl.pallas_call(functools.partial(grad_kernel, names, len(recv)), in_specs...  17.4 us
    pallas_call x5, Pallas kernels, project(): pl.pallas_call(functools.partial(project_kernel, start, bool(carried), sc...  11.1 us
    pallas_call x1, Pallas kernels, arrange(): pl.pallas_call(functools.partial(arrange_kernel, places), in_specs=[ANY],...  6.31 us
    pallas_call x10, Pallas kernels, local(): pl.pallas_call(kernel, in_specs=[VMEM] * len(arrays), out_specs=[VMEM] *...  3.38 us
  transfers between devices with their start and end apart: 34, of which 18 were waited for; matrix products, arithmetic and copies ran while one was open for 0% of the time, Pallas kernels for 22%

profile of v3, /device:TPU:1, one launch (start us, length us, event | category | flops | bytes accessed | tf_op | source)
XLA Modules:
  0.0 135.0 jit_solution(17061735007038479089)
XLA Ops:
  0.6 1.2 copy-done
  1.9 4.3 %shard_map.112 = (bf16[1024,512]{1,0:T(8,128)(2,1)S(1)}, bf16[1024,512]{1,0:T(8,128)(2,1)S(1)}) custom-call(bf16[1024,8192]{1,0:T(8,128)(2,1)} %tok_ref.8, bf16[1024,512]{1,0:T(8,128)(2,1)S(1)} %copy-done), custom_call_target="tpu_custom_call" | custom-call | flops 2147483648 | bytes 4194304 | tf_op jit(solution)/shard_map/pallas_call | solution.py:138
  6.2 2.2 %collective-permute-start.2 = (bf16[1024,512]{1,0:T(8,128)(2,1)S(1)}, bf16[1024,512]{1,0:T(8,128)(2,1)S(1)}, u32[]{:S(2)}, u32[]{:S(2)}) collective-permute-start(bf16[1024,512]{1,0:T(8,128)(2,1)S(1)} %get-tuple-element.56), channel_id=1, source_target_pairs={{0,2},{32,40},{64,66},{96,104},{1,3},{33,41},{65,67},{97,105},{8,1... | collective-permute-start | bytes 3145736 | tf_op jit(solution)/shard_map/ppermute | solution.py:32
  8.4 1.5 %collective-permute-start.3 = (bf16[1024,512]{1,0:T(8,128)(2,1)S(1)}, bf16[1024,512]{1,0:T(8,128)(2,1)S(1)}, u32[]{:S(2)}, u32[]{:S(2)}) collective-permute-start(bf16[1024,512]{1,0:T(8,128)(2,1)S(1)} %get-tuple-element.57), channel_id=1, source_target_pairs={{0,6},{32,56},{64,70},{96,120},{1,7},{33,57},{65,71},{97,121},{8,1... | collective-permute-start | bytes 3145736 | tf_op jit(solution)/shard_map/ppermute | solution.py:32
  9.9 4.3 %shard_map.110 = (bf16[1024,512]{1,0:T(8,128)(2,1)S(1)}, bf16[1024,512]{1,0:T(8,128)(2,1)S(1)}) custom-call(bf16[1024,8192]{1,0:T(8,128)(2,1)} %tok_ref.8, bf16[1024,512]{1,0:T(8,128)(2,1)S(1)} %copy-done), custom_call_target="tpu_custom_call" | custom-call | flops 2147483648 | bytes 4194304 | tf_op jit(solution)/shard_map/pallas_call | solution.py:138
  14.3 1.5 %collective-permute-start = (bf16[1024,512]{1,0:T(8,128)(2,1)S(1)}, bf16[1024,512]{1,0:T(8,128)(2,1)S(1)}, u32[]{:S(2)}, u32[]{:S(2)}) collective-permute-start(bf16[1024,512]{1,0:T(8,128)(2,1)S(1)} %get-tuple-element.52), channel_id=1, source_target_pairs={{0,6},{32,56},{64,70},{96,120},{1,7},{33,57},{65,71},{97,121},{8,1... | collective-permute-start | bytes 3145736 | tf_op jit(solution)/shard_map/ppermute | solution.py:32
  15.8 6.5 %collective-permute-done.2.refs_0_ = bf16[1024,512]{1,0:T(8,128)(2,1)S(1)} collective-permute-done((bf16[1024,512]{1,0:T(8,128)(2,1)S(1)}, bf16[1024,512]{1,0:T(8,128)(2,1)S(1)}, u32[]{:S(2)}, u32[]{:S(2)}) %collective-permute-start.2) | collective-permute-done | bytes 1048608 | tf_op jit(solution)/shard_map/ppermute | solution.py:32
  22.4 4.4 %shard_map.113 = (bf16[1024,512]{1,0:T(8,128)(2,1)S(1)}, bf16[1024,512]{1,0:T(8,128)(2,1)S(1)}) custom-call(bf16[1024,8192]{1,0:T(8,128)(2,1)} %tok_ref.8, bf16[1024,512]{1,0:T(8,128)(2,1)S(1)} %copy-done.1, bf16[1024,512]{1,0:T(8,128)(2,1)S(1)} %collective-permute-done.2.refs_0_, bf16[1024,512]{1,0:T(8,128)(2,1)S(1)} %collective-permute-done.3.refs_1_), custom_call_target="tpu_custom_call" | custom-call | flops 2147483648 | bytes 4194304 | tf_op jit(solution)/shard_map/pallas_call | solution.py:138
  26.7 1.4 %collective-permute-start.4 = (bf16[1024,512]{1,0:T(8,128)(2,1)S(1)}, bf16[1024,512]{1,0:T(8,128)(2,1)S(1)}, u32[]{:S(2)}, u32[]{:S(2)}) collective-permute-start(bf16[1024,512]{1,0:T(8,128)(2,1)S(1)} %get-tuple-element.58), channel_id=1, source_target_pairs={{0,2},{32,40},{64,66},{96,104},{1,3},{33,41},{65,67},{97,105},{8,1... | collective-permute-start | bytes 3145736 | tf_op jit(solution)/shard_map/ppermute | solution.py:32
  28.1 1.5 %collective-permute-start.5 = (bf16[1024,512]{1,0:T(8,128)(2,1)S(1)}, bf16[1024,512]{1,0:T(8,128)(2,1)S(1)}, u32[]{:S(2)}, u32[]{:S(2)}) collective-permute-start(bf16[1024,512]{1,0:T(8,128)(2,1)S(1)} %get-tuple-element.59), channel_id=1, source_target_pairs={{0,6},{32,56},{64,70},{96,120},{1,7},{33,57},{65,71},{97,121},{8,1... | collective-permute-start | bytes 3145736 | tf_op jit(solution)/shard_map/ppermute | solution.py:32
  29.6 4.0 %collective-permute-done.refs_0_ = bf16[1024,512]{1,0:T(8,128)(2,1)S(1)} collective-permute-done((bf16[1024,512]{1,0:T(8,128)(2,1)S(1)}, bf16[1024,512]{1,0:T(8,128)(2,1)S(1)}, u32[]{:S(2)}, u32[]{:S(2)}) %collective-permute-start) | collective-permute-done | bytes 1048608 | tf_op jit(solution)/shard_map/ppermute | solution.py:32
  33.6 4.3 %shard_map.111 = (f32[1024,512]{1,0:T(8,128)S(1)}, f32[1024,512]{1,0:T(8,128)S(1)}) custom-call(bf16[1024,8192]{1,0:T(8,128)(2,1)} %tok_ref.8, bf16[1024,512]{1,0:T(8,128)(2,1)S(1)} %copy-done.1, bf16[1024,512]{1,0:T(8,128)(2,1)S(1)} %collective-permute-done.refs_0_, bf16[1024,512]{1,0:T(8,128)(2,1)S(1)} %collective-permute-done.1.refs_1_), custom_call_target="tpu_custom_call" | custom-call | flops 2147483648 | bytes 4194304 | tf_op jit(solution)/shard_map/pallas_call | solution.py:138
  37.9 6.9 %collective-permute-done.4.got1 = bf16[1024,512]{1,0:T(8,128)(2,1)S(1)} collective-permute-done((bf16[1024,512]{1,0:T(8,128)(2,1)S(1)}, bf16[1024,512]{1,0:T(8,128)(2,1)S(1)}, u32[]{:S(2)}, u32[]{:S(2)}) %collective-permute-start.4) | collective-permute-done | bytes 1048608 | tf_op jit(solution)/shard_map/ppermute | solution.py:32
  44.8 0.3 shard_map.114
  45.2 1.3 collective-permute-start.10
  46.4 1.5 %collective-permute-start.11 = (bf16[256,512]{1,0:T(8,128)(2,1)S(1)}, bf16[256,512]{1,0:T(8,128)(2,1)S(1)}, u32[]{:S(2)}, u32[]{:S(2)}) collective-permute-start(bf16[256,512]{1,0:T(8,128)(2,1)S(1)} %get-tuple-element.67), channel_id=1, source_target_pairs={{0,24},{32,38},{64,88},{96,102},{1,25},{33,39},{65,89},{97,103},{8... | collective-permute-start | bytes 786440 | tf_op jit(solution)/shard_map/ppermute | solution.py:32
  47.9 1.5 %collective-permute-start.9 = (bf16[256,512]{1,0:T(8,128)(2,1)S(1)}, bf16[256,512]{1,0:T(8,128)(2,1)S(1)}, u32[]{:S(2)}, u32[]{:S(2)}) collective-permute-start(bf16[256,512]{1,0:T(8,128)(2,1)S(1)} %get-tuple-element.65), channel_id=1, source_target_pairs={{0,16},{32,36},{64,80},{96,100},{1,17},{33,37},{65,81},{97,101},{8... | collective-permute-start | bytes 786440 | tf_op jit(solution)/shard_map/ppermute | solution.py:32
  49.4 1.4 %collective-permute-start.6 = (bf16[256,512]{1,0:T(8,128)(2,1)S(1)}, bf16[256,512]{1,0:T(8,128)(2,1)S(1)}, u32[]{:S(2)}, u32[]{:S(2)}) collective-permute-start(bf16[256,512]{1,0:T(8,128)(2,1)S(1)} %get-tuple-element.61), channel_id=1, source_target_pairs={{0,16},{32,36},{64,80},{96,100},{1,17},{33,37},{65,81},{97,101},{8... | collective-permute-start | bytes 786440 | tf_op jit(solution)/shard_map/ppermute | solution.py:32
  50.9 1.1 collective-permute-done.10.refs_1_
  52.0 1.6 %collective-permute-start.8 = (bf16[256,512]{1,0:T(8,128)(2,1)S(1)}, bf16[256,512]{1,0:T(8,128)(2,1)S(1)}, u32[]{:S(2)}, u32[]{:S(2)}) collective-permute-start(bf16[256,512]{1,0:T(8,128)(2,1)S(1)} %get-tuple-element.63), channel_id=1, source_target_pairs={{0,24},{32,38},{64,88},{96,102},{1,25},{33,39},{65,89},{97,103},{8... | collective-permute-start | bytes 786440 | tf_op jit(solution)/shard_map/ppermute | solution.py:32
  53.6 2.2 %collective-permute-done.9.refs_0_ = bf16[256,512]{1,0:T(8,128)(2,1)S(1)} collective-permute-done((bf16[256,512]{1,0:T(8,128)(2,1)S(1)}, bf16[256,512]{1,0:T(8,128)(2,1)S(1)}, u32[]{:S(2)}, u32[]{:S(2)}) %collective-permute-start.9) | collective-permute-done | bytes 262176 | tf_op jit(solution)/shard_map/ppermute | solution.py:32
  55.9 3.7 %collective-permute-start.12 = (bf16[256,512]{1,0:T(8,128)(2,1)S(1)}, bf16[256,512]{1,0:T(8,128)(2,1)S(1)}, u32[]{:S(2)}, u32[]{:S(2)}) collective-permute-start(bf16[256,512]{1,0:T(8,128)(2,1)S(1)} %shard_map.116), channel_id=1, source_target_pairs={{0,1},{32,33},{64,65},{96,97},{1,0},{33,32},{65,64},{97,96},{8,9},... | collective-permute-start | bytes 786440 | tf_op jit(solution)/shard_map/ppermute | solution.py:32
  59.5 6.3 %shard_map.117.held = bf16[1024,8192]{1,0:T(8,128)(2,1)S(1)} custom-call(bf16[1024,8192]{1,0:T(8,128)(2,1)} %tok_ref.8), custom_call_target="tpu_custom_call" | custom-call | flops 1 | bytes 1 | tf_op jit(solution)/shard_map/pallas_call | solution.py:294
  66.1 0.8 copy-done.4
  66.9 0.2 copy-done.5
  67.1 0.2 copy-done.6
  67.2 1.3 shard_map.118
  68.5 3.1 %collective-permute-start.13 = (f32[256,256]{1,0:T(8,128)S(1)}, f32[256,256]{1,0:T(8,128)S(1)}, u32[]{:S(2)}, u32[]{:S(2)}) collective-permute-start(f32[256,256]{1,0:T(8,128)S(1)} %get-tuple-element.74), channel_id=1, source_target_pairs={{0,32},{32,0},{64,96},{96,64},{1,33},{33,1},{65,97},{97,65},{8,40}... | collective-permute-start | bytes 786440 | tf_op jit(solution)/shard_map/ppermute | solution.py:32
  71.7 1.2 collective-permute-done.13.right
  72.8 0.8 collective-permute-start.14
  73.7 4.0 %collective-permute-done.14.right = bf16[256,256]{1,0:T(8,128)(2,1)S(1)} collective-permute-done((bf16[256,256]{1,0:T(8,128)(2,1)S(1)}, bf16[256,256]{1,0:T(8,128)(2,1)S(1)}, u32[]{:S(2)}, u32[]{:S(2)}) %collective-permute-start.14) | collective-permute-done | bytes 131104 | tf_op jit(solution)/shard_map/ppermute | solution.py:32
  77.6 0.1 shard_map.120
  77.8 1.3 collective-permute-start.15
  79.1 2.2 %collective-permute-start.16 = (bf16[256,256]{1,0:T(8,128)(2,1)S(1)}, bf16[256,256]{1,0:T(8,128)(2,1)S(1)}, u32[]{:S(2)}, u32[]{:S(2)}) collective-permute-start(bf16[256,256]{1,0:T(8,128)(2,1)S(1)} %get-tuple-element.75.mine), channel_id=1, source_target_pairs={{32,65},{96,1},{1,96},{65,32},{40,73},{104,9},{9,104},{73,40},{48,... | collective-permute-start | bytes 393224 | tf_op jit(solution)/shard_map/ppermute | solution.py:32
  81.3 1.6 %collective-permute-done.15.one = bf16[256,256]{1,0:T(8,128)(2,1)S(1)} collective-permute-done((bf16[256,256]{1,0:T(8,128)(2,1)S(1)}, bf16[256,256]{1,0:T(8,128)(2,1)S(1)}, u32[]{:S(2)}, u32[]{:S(2)}) %collective-permute-start.15) | collective-permute-done | bytes 131104 | tf_op jit(solution)/shard_map/ppermute | solution.py:32
  82.9 3.7 %collective-permute-done.16.two = bf16[256,256]{1,0:T(8,128)(2,1)S(1)} collective-permute-done((bf16[256,256]{1,0:T(8,128)(2,1)S(1)}, bf16[256,256]{1,0:T(8,128)(2,1)S(1)}, u32[]{:S(2)}, u32[]{:S(2)}) %collective-permute-start.16) | collective-permute-done | bytes 131104 | tf_op jit(solution)/shard_map/ppermute | solution.py:32
  86.6 1.3 collective-permute-start.17
  87.9 3.7 %collective-permute-start.18 = (bf16[256,512]{1,0:T(8,128)(2,1)S(1)}, bf16[256,512]{1,0:T(8,128)(2,1)S(1)}, u32[]{:S(2)}, u32[]{:S(2)}) collective-permute-start(bf16[256,512]{1,0:T(8,128)(2,1)S(1)} %shard_map.121.refs_3_), channel_id=1, source_target_pairs={{0,6},{32,56},{64,70},{96,120},{1,7},{33,57},{65,71},{97,121},{8,1... | collective-permute-start | bytes 786440 | tf_op jit(solution)/shard_map/ppermute | solution.py:32
  91.6 1.1 collective-permute-start.19
  92.7 0.9 collective-permute-start.20
  93.6 1.7 %collective-permute-start.21 = (bf16[256,512]{1,0:T(8,128)(2,1)S(1)}, bf16[256,512]{1,0:T(8,128)(2,1)S(1)}, u32[]{:S(2)}, u32[]{:S(2)}) collective-permute-start(bf16[256,512]{1,0:T(8,128)(2,1)S(1)} %shard_map.121.refs_3_), channel_id=1, source_target_pairs={{0,24},{32,38},{64,88},{96,102},{1,25},{33,39},{65,89},{97,103},{8... | collective-permute-start | bytes 786440 | tf_op jit(solution)/shard_map/ppermute | solution.py:32
  95.3 2.7 %collective-permute-done.17.refs_0_ = bf16[256,512]{1,0:T(8,128)(2,1)S(1)} collective-permute-done((bf16[256,512]{1,0:T(8,128)(2,1)S(1)}, bf16[256,512]{1,0:T(8,128)(2,1)S(1)}, u32[]{:S(2)}, u32[]{:S(2)}) %collective-permute-start.17) | collective-permute-done | bytes 262176 | tf_op jit(solution)/shard_map/ppermute | solution.py:32
  98.0 1.9 %collective-permute-done.18.refs_1_ = bf16[256,512]{1,0:T(8,128)(2,1)S(1)} collective-permute-done((bf16[256,512]{1,0:T(8,128)(2,1)S(1)}, bf16[256,512]{1,0:T(8,128)(2,1)S(1)}, u32[]{:S(2)}, u32[]{:S(2)}) %collective-permute-start.18) | collective-permute-done | bytes 262176 | tf_op jit(solution)/shard_map/ppermute | solution.py:32
  99.9 2.1 %collective-permute-done.19.refs_2_ = bf16[256,512]{1,0:T(8,128)(2,1)S(1)} collective-permute-done((bf16[256,512]{1,0:T(8,128)(2,1)S(1)}, bf16[256,512]{1,0:T(8,128)(2,1)S(1)}, u32[]{:S(2)}, u32[]{:S(2)}) %collective-permute-start.19) | collective-permute-done | bytes 262176 | tf_op jit(solution)/shard_map/ppermute | solution.py:32
  102.0 0.2 shard_map.122
  102.3 1.0 collective-permute-start.23
  103.3 1.7 %collective-permute-start.24 = (bf16[768,512]{1,0:T(8,128)(2,1)S(1)}, bf16[768,512]{1,0:T(8,128)(2,1)S(1)}, u32[]{:S(2)}, u32[]{:S(2)}) collective-permute-start(bf16[768,512]{1,0:T(8,128)(2,1)S(1)} %get-tuple-element.81), channel_id=1, source_target_pairs={{0,24},{32,38},{64,88},{96,102},{1,25},{33,39},{65,89},{97,103},{8... | collective-permute-start | bytes 2359304 | tf_op jit(solution)/shard_map/ppermute | solution.py:32
  105.0 0.7 collective-permute-done.25.refs_1_
  105.7 3.6 %shard_map.123.refs_2_ = f32[1024,512]{1,0:T(8,128)S(1)} custom-call(bf16[1024,8192]{1,0:T(8,128)(2,1)S(1)} %shard_map.117.held, bf16[1536,512]{1,0:T(8,128)(2,1)S(1)} %get-tuple-element.83.refs_0_, bf16[1536,512]{1,0:T(8,128)(2,1)S(1)} %collective-permute-done.25.refs_1_), custom_call_target="tpu_custom_call" | custom-call | flops 1 | bytes 1 | tf_op jit(solution)/shard_map/pallas_call | solution.py:325
  109.3 5.4 %collective-permute-done.23.up.refs_0_ = bf16[768,512]{1,0:T(8,128)(2,1)S(1)} collective-permute-done((bf16[768,512]{1,0:T(8,128)(2,1)S(1)}, bf16[768,512]{1,0:T(8,128)(2,1)S(1)}, u32[]{:S(2)}, u32[]{:S(2)}) %collective-permute-start.23) | collective-permute-done | bytes 786464 | tf_op jit(solution)/shard_map/ppermute | solution.py:32
  114.7 1.3 collective-permute-start.28
  116.0 0.5 collective-permute-start.30
  116.6 2.1 %collective-permute-start.27 = (bf16[512,512]{1,0:T(8,128)(2,1)S(1)}, bf16[512,512]{1,0:T(8,128)(2,1)S(1)}, u32[]{:S(2)}, u32[]{:S(2)}) collective-permute-start(bf16[512,512]{1,0:T(8,128)(2,1)S(1)} %get-tuple-element.87), channel_id=1, source_target_pairs={{0,24},{32,38},{64,88},{96,102},{1,25},{33,39},{65,89},{97,103},{8... | collective-permute-start | bytes 1572872 | tf_op jit(solution)/shard_map/ppermute | solution.py:32
  118.7 0.7 collective-permute-done.30.theirs
  119.4 0.9 collective-permute-start.26
  120.3 1.9 %shard_map.125.refs_2_ = f32[1024,512]{1,0:T(8,128)S(1)} custom-call(bf16[1024,8192]{1,0:T(8,128)(2,1)S(1)} %shard_map.117.held, bf16[768,512]{1,0:T(8,128)(2,1)S(1)} %collective-permute-done.23.up.refs_0_, bf16[768,512]{1,0:T(8,128)(2,1)S(1)} %collective-permute-done.24.down.refs_1_, f32[1024,512]{1,0:T(8,128)S(1)} %shard_map.123.refs_2_), custom_call_target="tpu_custom_call" | custom-call | flops 1 | bytes 1 | tf_op jit(solution)/shard_map/pallas_call | solution.py:325
  122.2 1.1 shard_map.127
  123.4 1.9 %shard_map.126.refs_3_ = f32[1024,512]{1,0:T(8,128)S(1)} custom-call(bf16[1024,8192]{1,0:T(8,128)(2,1)S(1)} %shard_map.117.held, bf16[768,512]{1,0:T(8,128)(2,1)S(1)} %collective-permute-done.28.refs_0_, bf16[768,512]{1,0:T(8,128)(2,1)S(1)} %collective-permute-done.29.refs_1_, f32[1024,512]{1,0:T(8,128)S(1)} %shard_map.125.refs_2_), custom_call_target="tpu_custom_call" | custom-call | flops 1 | bytes 1 | tf_op jit(solution)/shard_map/pallas_call | solution.py:325
  125.4 2.8 %collective-permute-done.26.refs_1_ = bf16[256,512]{1,0:T(8,128)(2,1)S(1)} collective-permute-done((bf16[256,512]{1,0:T(8,128)(2,1)S(1)}, bf16[256,512]{1,0:T(8,128)(2,1)S(1)}, u32[]{:S(2)}, u32[]{:S(2)}) %collective-permute-start.26) | collective-permute-done | bytes 262176 | tf_op jit(solution)/shard_map/ppermute | solution.py:32
  128.2 2.1 %collective-permute-start.33 = (bf16[512,512]{1,0:T(8,128)(2,1)S(1)}, bf16[512,512]{1,0:T(8,128)(2,1)S(1)}, u32[]{:S(2)}, u32[]{:S(2)}) collective-permute-start(bf16[512,512]{1,0:T(8,128)(2,1)S(1)} %collective-permute-done.27.refs_2_), channel_id=1, source_target_pairs={{0,32},{32,0},{64,96},{96,64},{1,33},{33,1},{65,97},{97,65},{8,40}... | collective-permute-start | bytes 1572872 | tf_op jit(solution)/shard_map/ppermute | solution.py:32
  130.3 0.5 collective-permute-start.32
  130.8 1.4 %shard_map.128.refs_3_ = f32[1024,512]{1,0:T(8,128)S(1)} custom-call(bf16[1024,8192]{1,0:T(8,128)(2,1)S(1)} %shard_map.117.held, bf16[256,512]{1,0:T(8,128)(2,1)S(1)} %collective-permute-done.22.refs_0_, bf16[256,512]{1,0:T(8,128)(2,1)S(1)} %collective-permute-done.26.refs_1_, bf16[512,512]{1,0:T(8,128)(2,1)S(1)} %collective-permute-done.27.refs_2_, ...), custom_call_target="tpu_custom_call" | custom-call | flops 1 | bytes 1 | tf_op jit(solution)/shard_map/pallas_call | solution.py:325
  132.2 0.4 collective-permute-done.32.refs_1_
  132.5 2.3 %shard_map.129 = bf16[1024,512]{1,0:T(8,128)(2,1)} custom-call(bf16[1024,8192]{1,0:T(8,128)(2,1)S(1)} %shard_map.117.held, bf16[256,512]{1,0:T(8,128)(2,1)S(1)} %collective-permute-done.31.refs_0_, bf16[256,512]{1,0:T(8,128)(2,1)S(1)} %collective-permute-done.32.refs_1_, bf16[512,512]{1,0:T(8,128)(2,1)S(1)} %collective-permute-done.33.refs_2_, ...), custom_call_target="tpu_custom_call" | custom-call | flops 1 | bytes 1 | tf_op jit(solution)/shard_map/pallas_call | solution.py:325
  (38 shorter events, 0.7 us)
Async XLA Ops:
  0.6 1.2 copy-start
  6.2 16.1 %collective-permute-start.2 = (bf16[1024,512]{1,0:T(8,128)(2,1)S(1)}, bf16[1024,512]{1,0:T(8,128)(2,1)S(1)}, u32[]{:S(2)}, u32[]{:S(2)}) collective-permute-start(bf16[1024,512]{1,0:T(8,128)(2,1)S(1)} %get-tuple-element.56), channel_id=1, source_target_pairs={{0,2},{32,40},{64,66},{96,104},{1,3},{33,41},{65,67},{97,105},{8,1... | collective-permute-start | bytes 3145736 | tf_op jit(solution)/shard_map/ppermute | solution.py:32
  8.4 13.9 %copy-start.1 = (bf16[1024,512]{1,0:T(8,128)(2,1)S(1)}, bf16[1024,512]{1,0:T(8,128)(2,1)}, u32[]{:S(2)}) copy-start(bf16[1024,512]{1,0:T(8,128)(2,1)} %grad_ref.7) | copy-start | bytes 3145732
  8.4 13.9 %collective-permute-start.3 = (bf16[1024,512]{1,0:T(8,128)(2,1)S(1)}, bf16[1024,512]{1,0:T(8,128)(2,1)S(1)}, u32[]{:S(2)}, u32[]{:S(2)}) collective-permute-start(bf16[1024,512]{1,0:T(8,128)(2,1)S(1)} %get-tuple-element.57), channel_id=1, source_target_pairs={{0,6},{32,56},{64,70},{96,120},{1,7},{33,57},{65,71},{97,121},{8,1... | collective-permute-start | bytes 3145736 | tf_op jit(solution)/shard_map/ppermute | solution.py:32
  14.3 19.3 %collective-permute-start = (bf16[1024,512]{1,0:T(8,128)(2,1)S(1)}, bf16[1024,512]{1,0:T(8,128)(2,1)S(1)}, u32[]{:S(2)}, u32[]{:S(2)}) collective-permute-start(bf16[1024,512]{1,0:T(8,128)(2,1)S(1)} %get-tuple-element.52), channel_id=1, source_target_pairs={{0,6},{32,56},{64,70},{96,120},{1,7},{33,57},{65,71},{97,121},{8,1... | collective-permute-start | bytes 3145736 | tf_op jit(solution)/shard_map/ppermute | solution.py:32
  15.7 17.8 %collective-permute-start.1 = (bf16[1024,512]{1,0:T(8,128)(2,1)S(1)}, bf16[1024,512]{1,0:T(8,128)(2,1)S(1)}, u32[]{:S(2)}, u32[]{:S(2)}) collective-permute-start(bf16[1024,512]{1,0:T(8,128)(2,1)S(1)} %get-tuple-element.53), channel_id=1, source_target_pairs={{0,2},{32,40},{64,66},{96,104},{1,3},{33,41},{65,67},{97,105},{8,1... | collective-permute-start | bytes 3145736 | tf_op jit(solution)/shard_map/ppermute | solution.py:32
  26.7 18.1 %collective-permute-start.4 = (bf16[1024,512]{1,0:T(8,128)(2,1)S(1)}, bf16[1024,512]{1,0:T(8,128)(2,1)S(1)}, u32[]{:S(2)}, u32[]{:S(2)}) collective-permute-start(bf16[1024,512]{1,0:T(8,128)(2,1)S(1)} %get-tuple-element.58), channel_id=1, source_target_pairs={{0,2},{32,40},{64,66},{96,104},{1,3},{33,41},{65,67},{97,105},{8,1... | collective-permute-start | bytes 3145736 | tf_op jit(solution)/shard_map/ppermute | solution.py:32
  28.1 16.7 %collective-permute-start.5 = (bf16[1024,512]{1,0:T(8,128)(2,1)S(1)}, bf16[1024,512]{1,0:T(8,128)(2,1)S(1)}, u32[]{:S(2)}, u32[]{:S(2)}) collective-permute-start(bf16[1024,512]{1,0:T(8,128)(2,1)S(1)} %get-tuple-element.59), channel_id=1, source_target_pairs={{0,6},{32,56},{64,70},{96,120},{1,7},{33,57},{65,71},{97,121},{8,1... | collective-permute-start | bytes 3145736 | tf_op jit(solution)/shard_map/ppermute | solution.py:32
  45.2 6.8 %collective-permute-start.10 = (bf16[256,512]{1,0:T(8,128)(2,1)S(1)}, bf16[256,512]{1,0:T(8,128)(2,1)S(1)}, u32[]{:S(2)}, u32[]{:S(2)}) collective-permute-start(bf16[256,512]{1,0:T(8,128)(2,1)S(1)} %get-tuple-element.66), channel_id=1, source_target_pairs={{0,8},{32,34},{64,72},{96,98},{1,9},{33,35},{65,73},{97,99},{8,16}... | collective-permute-start | bytes 786440 | tf_op jit(solution)/shard_map/ppermute | solution.py:32
  46.4 7.1 %collective-permute-start.11 = (bf16[256,512]{1,0:T(8,128)(2,1)S(1)}, bf16[256,512]{1,0:T(8,128)(2,1)S(1)}, u32[]{:S(2)}, u32[]{:S(2)}) collective-permute-start(bf16[256,512]{1,0:T(8,128)(2,1)S(1)} %get-tuple-element.67), channel_id=1, source_target_pairs={{0,24},{32,38},{64,88},{96,102},{1,25},{33,39},{65,89},{97,103},{8... | collective-permute-start | bytes 786440 | tf_op jit(solution)/shard_map/ppermute | solution.py:32
  47.9 7.9 %collective-permute-start.9 = (bf16[256,512]{1,0:T(8,128)(2,1)S(1)}, bf16[256,512]{1,0:T(8,128)(2,1)S(1)}, u32[]{:S(2)}, u32[]{:S(2)}) collective-permute-start(bf16[256,512]{1,0:T(8,128)(2,1)S(1)} %get-tuple-element.65), channel_id=1, source_target_pairs={{0,16},{32,36},{64,80},{96,100},{1,17},{33,37},{65,81},{97,101},{8... | collective-permute-start | bytes 786440 | tf_op jit(solution)/shard_map/ppermute | solution.py:32
  49.4 16.5 %collective-permute-start.6 = (bf16[256,512]{1,0:T(8,128)(2,1)S(1)}, bf16[256,512]{1,0:T(8,128)(2,1)S(1)}, u32[]{:S(2)}, u32[]{:S(2)}) collective-permute-start(bf16[256,512]{1,0:T(8,128)(2,1)S(1)} %get-tuple-element.61), channel_id=1, source_target_pairs={{0,16},{32,36},{64,80},{96,100},{1,17},{33,37},{65,81},{97,101},{8... | collective-permute-start | bytes 786440 | tf_op jit(solution)/shard_map/ppermute | solution.py:32
  50.9 15.0 %collective-permute-start.7 = (bf16[256,512]{1,0:T(8,128)(2,1)S(1)}, bf16[256,512]{1,0:T(8,128)(2,1)S(1)}, u32[]{:S(2)}, u32[]{:S(2)}) collective-permute-start(bf16[256,512]{1,0:T(8,128)(2,1)S(1)} %get-tuple-element.62), channel_id=1, source_target_pairs={{0,8},{32,34},{64,72},{96,98},{1,9},{33,35},{65,73},{97,99},{8,16}... | collective-permute-start | bytes 786440 | tf_op jit(solution)/shard_map/ppermute | solution.py:32
  52.0 14.0 %collective-permute-start.8 = (bf16[256,512]{1,0:T(8,128)(2,1)S(1)}, bf16[256,512]{1,0:T(8,128)(2,1)S(1)}, u32[]{:S(2)}, u32[]{:S(2)}) collective-permute-start(bf16[256,512]{1,0:T(8,128)(2,1)S(1)} %get-tuple-element.63), channel_id=1, source_target_pairs={{0,24},{32,38},{64,88},{96,102},{1,25},{33,39},{65,89},{97,103},{8... | collective-permute-start | bytes 786440 | tf_op jit(solution)/shard_map/ppermute | solution.py:32
  55.9 10.2 %collective-permute-start.12 = (bf16[256,512]{1,0:T(8,128)(2,1)S(1)}, bf16[256,512]{1,0:T(8,128)(2,1)S(1)}, u32[]{:S(2)}, u32[]{:S(2)}) collective-permute-start(bf16[256,512]{1,0:T(8,128)(2,1)S(1)} %shard_map.116), channel_id=1, source_target_pairs={{0,1},{32,33},{64,65},{96,97},{1,0},{33,32},{65,64},{97,96},{8,9},... | collective-permute-start | bytes 786440 | tf_op jit(solution)/shard_map/ppermute | solution.py:32
  65.9 1.0 copy-start.4
  65.9 1.2 copy-start.5
  65.9 1.3 copy-start.6
  65.9 11.7 %copy-start.2 = (f32[256,512]{1,0:T(8,128)S(1)}, f32[256,512]{1,0:T(8,128)}, u32[]{:S(2)}) copy-start(f32[256,512]{1,0:T(8,128)} %weights_ref.3) | copy-start | bytes 1572868
  65.9 11.7 %copy-start.3 = (f32[256,512]{1,0:T(8,128)S(1)}, f32[256,512]{1,0:T(8,128)}, u32[]{:S(2)}) copy-start(f32[256,512]{1,0:T(8,128)} %momentum_ref.3) | copy-start | bytes 1572868
  68.5 4.3 %collective-permute-start.13 = (f32[256,256]{1,0:T(8,128)S(1)}, f32[256,256]{1,0:T(8,128)S(1)}, u32[]{:S(2)}, u32[]{:S(2)}) collective-permute-start(f32[256,256]{1,0:T(8,128)S(1)} %get-tuple-element.74), channel_id=1, source_target_pairs={{0,32},{32,0},{64,96},{96,64},{1,33},{33,1},{65,97},{97,65},{8,40}... | collective-permute-start | bytes 786440 | tf_op jit(solution)/shard_map/ppermute | solution.py:32
  72.8 4.8 %collective-permute-start.14 = (bf16[256,256]{1,0:T(8,128)(2,1)S(1)}, bf16[256,256]{1,0:T(8,128)(2,1)S(1)}, u32[]{:S(2)}, u32[]{:S(2)}) collective-permute-start(bf16[256,256]{1,0:T(8,128)(2,1)S(1)} %shard_map.119.left), channel_id=1, source_target_pairs={{0,64},{32,96},{64,0},{96,32},{1,65},{33,97},{65,1},{97,33},{8,72}... | collective-permute-start | bytes 393224 | tf_op jit(solution)/shard_map/ppermute | solution.py:32
  77.8 5.1 %collective-permute-start.15 = (bf16[256,256]{1,0:T(8,128)(2,1)S(1)}, bf16[256,256]{1,0:T(8,128)(2,1)S(1)}, u32[]{:S(2)}, u32[]{:S(2)}) collective-permute-start(bf16[256,256]{1,0:T(8,128)(2,1)S(1)} %get-tuple-element.75.mine), channel_id=1, source_target_pairs={{0,65},{32,0},{64,1},{96,64},{1,33},{33,96},{65,97},{97,32},{8,73}... | collective-permute-start | bytes 393224 | tf_op jit(solution)/shard_map/ppermute | solution.py:32
  79.1 7.5 %collective-permute-start.16 = (bf16[256,256]{1,0:T(8,128)(2,1)S(1)}, bf16[256,256]{1,0:T(8,128)(2,1)S(1)}, u32[]{:S(2)}, u32[]{:S(2)}) collective-permute-start(bf16[256,256]{1,0:T(8,128)(2,1)S(1)} %get-tuple-element.75.mine), channel_id=1, source_target_pairs={{32,65},{96,1},{1,96},{65,32},{40,73},{104,9},{9,104},{73,40},{48,... | collective-permute-start | bytes 393224 | tf_op jit(solution)/shard_map/ppermute | solution.py:32
  86.6 11.5 %collective-permute-start.17 = (bf16[256,512]{1,0:T(8,128)(2,1)S(1)}, bf16[256,512]{1,0:T(8,128)(2,1)S(1)}, u32[]{:S(2)}, u32[]{:S(2)}) collective-permute-start(bf16[256,512]{1,0:T(8,128)(2,1)S(1)} %shard_map.121.refs_3_), channel_id=1, source_target_pairs={{0,2},{32,40},{64,66},{96,104},{1,3},{33,41},{65,67},{97,105},{8,1... | collective-permute-start | bytes 786440 | tf_op jit(solution)/shard_map/ppermute | solution.py:32
  87.9 12.1 %collective-permute-start.18 = (bf16[256,512]{1,0:T(8,128)(2,1)S(1)}, bf16[256,512]{1,0:T(8,128)(2,1)S(1)}, u32[]{:S(2)}, u32[]{:S(2)}) collective-permute-start(bf16[256,512]{1,0:T(8,128)(2,1)S(1)} %shard_map.121.refs_3_), channel_id=1, source_target_pairs={{0,6},{32,56},{64,70},{96,120},{1,7},{33,57},{65,71},{97,121},{8,1... | collective-permute-start | bytes 786440 | tf_op jit(solution)/shard_map/ppermute | solution.py:32
  91.6 10.5 %collective-permute-start.19 = (bf16[256,512]{1,0:T(8,128)(2,1)S(1)}, bf16[256,512]{1,0:T(8,128)(2,1)S(1)}, u32[]{:S(2)}, u32[]{:S(2)}) collective-permute-start(bf16[256,512]{1,0:T(8,128)(2,1)S(1)} %shard_map.121.refs_3_), channel_id=1, source_target_pairs={{0,4},{32,48},{64,68},{96,112},{1,5},{33,49},{65,69},{97,113},{8,1... | collective-permute-start | bytes 786440 | tf_op jit(solution)/shard_map/ppermute | solution.py:32
  92.7 9.4 %collective-permute-start.20 = (bf16[256,512]{1,0:T(8,128)(2,1)S(1)}, bf16[256,512]{1,0:T(8,128)(2,1)S(1)}, u32[]{:S(2)}, u32[]{:S(2)}) collective-permute-start(bf16[256,512]{1,0:T(8,128)(2,1)S(1)} %shard_map.121.refs_3_), channel_id=1, source_target_pairs={{0,8},{32,34},{64,72},{96,98},{1,9},{33,35},{65,73},{97,99},{8,16}... | collective-permute-start | bytes 786440 | tf_op jit(solution)/shard_map/ppermute | solution.py:32
  93.6 8.4 %collective-permute-start.21 = (bf16[256,512]{1,0:T(8,128)(2,1)S(1)}, bf16[256,512]{1,0:T(8,128)(2,1)S(1)}, u32[]{:S(2)}, u32[]{:S(2)}) collective-permute-start(bf16[256,512]{1,0:T(8,128)(2,1)S(1)} %shard_map.121.refs_3_), channel_id=1, source_target_pairs={{0,24},{32,38},{64,88},{96,102},{1,25},{33,39},{65,89},{97,103},{8... | collective-permute-start | bytes 786440 | tf_op jit(solution)/shard_map/ppermute | solution.py:32
  102.2 3.5 %collective-permute-start.25 = (bf16[1536,512]{1,0:T(8,128)(2,1)S(1)}, bf16[1536,512]{1,0:T(8,128)(2,1)S(1)}, u32[]{:S(2)}, u32[]{:S(2)}) collective-permute-start(bf16[1536,512]{1,0:T(8,128)(2,1)S(1)} %get-tuple-element.83.refs_0_), channel_id=1, source_target_pairs={{0,32},{32,0},{64,96},{96,64},{1,33},{33,1},{65,97},{97,65},{8,40}... | collective-permute-start | bytes 4718600 | tf_op jit(solution)/shard_map/ppermute | solution.py:32
  102.3 12.4 %collective-permute-start.23 = (bf16[768,512]{1,0:T(8,128)(2,1)S(1)}, bf16[768,512]{1,0:T(8,128)(2,1)S(1)}, u32[]{:S(2)}, u32[]{:S(2)}) collective-permute-start(bf16[768,512]{1,0:T(8,128)(2,1)S(1)} %get-tuple-element.81), channel_id=1, source_target_pairs={{0,8},{32,34},{64,72},{96,98},{1,9},{33,35},{65,73},{97,99},{8,16}... | collective-permute-start | bytes 2359304 | tf_op jit(solution)/shard_map/ppermute | solution.py:32
  103.3 11.4 %collective-permute-start.24 = (bf16[768,512]{1,0:T(8,128)(2,1)S(1)}, bf16[768,512]{1,0:T(8,128)(2,1)S(1)}, u32[]{:S(2)}, u32[]{:S(2)}) collective-permute-start(bf16[768,512]{1,0:T(8,128)(2,1)S(1)} %get-tuple-element.81), channel_id=1, source_target_pairs={{0,24},{32,38},{64,88},{96,102},{1,25},{33,39},{65,89},{97,103},{8... | collective-permute-start | bytes 2359304 | tf_op jit(solution)/shard_map/ppermute | solution.py:32
  114.7 8.7 %collective-permute-start.28 = (bf16[768,512]{1,0:T(8,128)(2,1)S(1)}, bf16[768,512]{1,0:T(8,128)(2,1)S(1)}, u32[]{:S(2)}, u32[]{:S(2)}) collective-permute-start(bf16[768,512]{1,0:T(8,128)(2,1)S(1)} %collective-permute-done.23.up.refs_0_), channel_id=1, source_target_pairs={{0,32},{32,0},{64,96},{96,64},{1,33},{33,1},{65,97},{97,65},{8,40}... | collective-permute-start | bytes 2359304 | tf_op jit(solution)/shard_map/ppermute | solution.py:32
  116.0 7.4 %collective-permute-start.29 = (bf16[768,512]{1,0:T(8,128)(2,1)S(1)}, bf16[768,512]{1,0:T(8,128)(2,1)S(1)}, u32[]{:S(2)}, u32[]{:S(2)}) collective-permute-start(bf16[768,512]{1,0:T(8,128)(2,1)S(1)} %collective-permute-done.24.down.refs_1_), channel_id=1, source_target_pairs={{0,32},{32,0},{64,96},{96,64},{1,33},{33,1},{65,97},{97,65},{8,40}... | collective-permute-start | bytes 2359304 | tf_op jit(solution)/shard_map/ppermute | solution.py:32
  116.0 3.4 %collective-permute-start.30 = (f32[256,256]{1,0:T(8,128)S(1)}, f32[256,256]{1,0:T(8,128)S(1)}, u32[]{:S(2)}, u32[]{:S(2)}) collective-permute-start(f32[256,256]{1,0:T(8,128)S(1)} %get-tuple-element.90.mine), channel_id=1, source_target_pairs={{0,32},{32,0},{64,96},{96,64},{1,33},{33,1},{65,97},{97,65},{8,40}... | collective-permute-start | bytes 786440 | tf_op jit(solution)/shard_map/ppermute | solution.py:32
  116.6 11.6 %collective-permute-start.27 = (bf16[512,512]{1,0:T(8,128)(2,1)S(1)}, bf16[512,512]{1,0:T(8,128)(2,1)S(1)}, u32[]{:S(2)}, u32[]{:S(2)}) collective-permute-start(bf16[512,512]{1,0:T(8,128)(2,1)S(1)} %get-tuple-element.87), channel_id=1, source_target_pairs={{0,24},{32,38},{64,88},{96,102},{1,25},{33,39},{65,89},{97,103},{8... | collective-permute-start | bytes 1572872 | tf_op jit(solution)/shard_map/ppermute | solution.py:32
  118.7 6.7 %collective-permute-start.22 = (bf16[256,512]{1,0:T(8,128)(2,1)S(1)}, bf16[256,512]{1,0:T(8,128)(2,1)S(1)}, u32[]{:S(2)}, u32[]{:S(2)}) collective-permute-start(bf16[256,512]{1,0:T(8,128)(2,1)S(1)} %collective-permute-done.20.refs_4_), channel_id=1, source_target_pairs={{0,8},{32,34},{64,72},{96,98},{1,9},{33,35},{65,73},{97,99},{8,16}... | collective-permute-start | bytes 786440 | tf_op jit(solution)/shard_map/ppermute | solution.py:32
  119.4 8.8 %collective-permute-start.26 = (bf16[256,512]{1,0:T(8,128)(2,1)S(1)}, bf16[256,512]{1,0:T(8,128)(2,1)S(1)}, u32[]{:S(2)}, u32[]{:S(2)}) collective-permute-start(bf16[256,512]{1,0:T(8,128)(2,1)S(1)} %get-tuple-element.86), channel_id=1, source_target_pairs={{0,8},{32,34},{64,72},{96,98},{1,9},{33,35},{65,73},{97,99},{8,16}... | collective-permute-start | bytes 786440 | tf_op jit(solution)/shard_map/ppermute | solution.py:32
  128.2 4.4 %collective-permute-start.33 = (bf16[512,512]{1,0:T(8,128)(2,1)S(1)}, bf16[512,512]{1,0:T(8,128)(2,1)S(1)}, u32[]{:S(2)}, u32[]{:S(2)}) collective-permute-start(bf16[512,512]{1,0:T(8,128)(2,1)S(1)} %collective-permute-done.27.refs_2_), channel_id=1, source_target_pairs={{0,32},{32,0},{64,96},{96,64},{1,33},{33,1},{65,97},{97,65},{8,40}... | collective-permute-start | bytes 1572872 | tf_op jit(solution)/shard_map/ppermute | solution.py:32
  130.3 1.9 %collective-permute-start.31 = (bf16[256,512]{1,0:T(8,128)(2,1)S(1)}, bf16[256,512]{1,0:T(8,128)(2,1)S(1)}, u32[]{:S(2)}, u32[]{:S(2)}) collective-permute-start(bf16[256,512]{1,0:T(8,128)(2,1)S(1)} %collective-permute-done.22.refs_0_), channel_id=1, source_target_pairs={{0,32},{32,0},{64,96},{96,64},{1,33},{33,1},{65,97},{97,65},{8,40}... | collective-permute-start | bytes 786440 | tf_op jit(solution)/shard_map/ppermute | solution.py:32
  130.3 2.3 %collective-permute-start.32 = (bf16[256,512]{1,0:T(8,128)(2,1)S(1)}, bf16[256,512]{1,0:T(8,128)(2,1)S(1)}, u32[]{:S(2)}, u32[]{:S(2)}) collective-permute-start(bf16[256,512]{1,0:T(8,128)(2,1)S(1)} %collective-permute-done.26.refs_1_), channel_id=1, source_target_pairs={{0,32},{32,0},{64,96},{96,64},{1,33},{33,1},{65,97},{97,65},{8,40}... | collective-permute-start | bytes 786440 | tf_op jit(solution)/shard_map/ppermute | solution.py:32

commit v4 on v3

--- a/solution.py
+++ b/solution.py
@@ -259,18 +259,12 @@
     out[:, half:] = jnp.where(core == 0, cross, same)
 
 
-def mid_kernel(*refs):
-    *ins, mid, near = refs
+def stack_kernel(*refs):
+    ins, (low, high, near) = refs[:4], refs[4:]
     for number, ref in enumerate(ins):
         near[256 * number : 256 * number + 256] = ref[...]
-        if number < 3:
-            mid[256 * number : 256 * number + 256] = ref[...]
-
-
-def cut_kernel(up, down, up_out, down_out):
-    rows = up_out.shape[0]
-    up_out[...] = up[:rows]
-    down_out[...] = down[rows:]
+        at = 256 * (number % 2)
+        (low, high)[number // 2][at : at + 256] = ref[...]
 
 
 def arrange_kernel(places, tok_ref, out, sems):
@@ -336,15 +330,27 @@
     )(held, *arrays, *carried)
 
 
-def swap(arrays):
-    return [permute(array, other_core) for array in arrays]
-
-
-NEAR = [(3, 0), (1, 0), (2, 0), (0, 0), (0, 3), (0, 1)]
-MIDDLE = [(3, 3), (1, 3), (2, 3), (3, 1), (1, 1), (2, 1)]
-FAR = [(0, 2), (3, 2), (1, 2), (2, 2)]
+def join_pair_kernel(left, right, out):
+    rows = left.shape[0]
+    out[:rows] = left[...]
+    out[rows:] = right[...]
+
+
+def join(left, right):
+    (both,) = local(join_pair_kernel, [((1024, 512), BF16)], left, right)
+    return both
+
+
 ORDER = [
-    (partner, place) for part in (NEAR, MIDDLE, FAR) for partner in range(2) for place in part
+    (partner, place)
+    for part in (
+        [(0, 0), (3, 0), (1, 0), (2, 0)],
+        [(0, 3), (3, 3), (1, 1), (2, 1)],
+        [(1, 3), (2, 3), (0, 1), (3, 1)],
+        [(0, 2), (3, 2), (1, 2), (2, 2)],
+    )
+    for partner in range(2)
+    for place in part
 ]
 
 
@@ -353,40 +359,29 @@
     (own,) = local(
         join_kernel, [quarter], synced, permute(synced, halves_one), permute(synced, halves_two)
     )
-    own_down, own_up = permute(own, second(-1)), permute(own, second(1))
     far = permute(own, first(2))
     ahead, behind = permute(own, first(-1)), permute(own, first(1))
-    behind, ahead, far, own_up, own_down = lax.optimization_barrier(
-        (behind, ahead, far, own_up, own_down)
-    )
-    mid, one = local(
-        mid_kernel,
-        [((768, 512), BF16), ((1536, 512), BF16)],
-        behind,
-        ahead,
-        far,
-        own,
-        own_up,
-        own_down,
-    )
-    mid_up, mid_down = permute(mid, second(1)), permute(mid, second(-1))
-    own_far = permute(own_up, second(1))
-    acc = project(held, 0, [one, *swap([one])], None, None)
-    mid_up, mid_down, acc = lax.optimization_barrier((mid_up, mid_down, acc))
-    cut_up, cut_down = local(
-        cut_kernel, [((256, 512), BF16), ((512, 512), BF16)], mid_up, mid_down
-    )
-    far_down, far_up = permute(cut_down, second(-1)), permute(cut_up, second(1))
-    two = [mid_up, mid_down]
-    theirs = swap(two)
+    half = ((512, 512), BF16)
+    low, high, near = local(
+        stack_kernel, [half, half, ((1024, 512), BF16)], own, behind, ahead, far
+    )
+    low_up, high_down = permute(low, second(1)), permute(high, second(-1))
+    high_up, low_down = permute(high, second(1)), permute(low, second(-1))
+    acc = project(held, 0, [near, permute(near, other_core)], None, None)
+    low_up, high_down, acc = lax.optimization_barrier((low_up, high_down, acc))
+    far_low, far_high = permute(low_up, second(1)), permute(high_down, second(-1))
+    wave = join(low_up, high_down)
+    acc = project(held, 2048, [wave, permute(wave, other_core)], acc, None)
     finished = finish(acc)
-    acc = project(held, 3072, two, acc, None)
-    acc = project(held, 4608, theirs, acc, None)
-    three = [own_far, far_up, far_down]
-    *three, acc, new_global, new_momentum = lax.optimization_barrier((*three, acc, *finished))
-    theirs = swap(three)
-    acc = project(held, 6144, three, acc, None)
-    return project(held, 7168, theirs, acc, scale), new_global, new_momentum
+    wave = join(high_up, low_down)
+    acc = project(held, 4096, [wave, permute(wave, other_core)], acc, None)
+    far_low, far_high, acc, new_global, new_momentum = lax.optimization_barrier(
+        (far_low, far_high, acc, *finished)
+    )
+    wave = join(far_low, far_high)
+    theirs = permute(wave, other_core)
+    acc = project(held, 6144, [wave], acc, None)
+    return project(held, 7168, [theirs], acc, scale), new_global, new_momentum
 
 
 def body(

time: 135 us -> 132 us (0.978)
  waiting for transfers between devices: 47.8 us -> 44.4 us
    ppermute x34 -> x31, waiting for transfers between devices: 47.8 us -> 44.4 us  [permute(): return lax.ppermute(array, BOTH, pairs)]
    ppermute x34 -> x31, starting transfers between devices: 45.6 us -> 45.3 us  [permute(): return lax.ppermute(array, BOTH, pairs)]
    pallas_call x10 -> x12, Pallas kernels: 3.38 us -> 3.52 us  [local(): pl.pallas_call(kernel, in_specs=[VMEM] * len(arrays), out_specs=[VMEM] *...]
  transfers between devices with their start and end apart: 34 -> 31, of which waited for: 18 -> 15; matrix products, arithmetic and copies ran while one was open for 0% -> 0% of each run, Pallas kernels for 22% -> 23%
where the time goes in v4:
time: 132 us
  starting transfers between devices  45.3 us (34%)
  waiting for transfers between devices  44.4 us (34%)
  Pallas kernels  38.3 us (29%)
  local copies, waits for them, and re-layouts  2.4 us (2%)
    ppermute x31, starting transfers between devices, permute(): return lax.ppermute(array, BOTH, pairs)  45.3 us
    ppermute x31, waiting for transfers between devices, permute(): return lax.ppermute(array, BOTH, pairs)  44.4 us
    pallas_call x4, Pallas kernels, grad_blocks(): pl.pallas_call(functools.partial(grad_kernel, names, len(recv)), in_specs...  17.4 us
    pallas_call x5, Pallas kernels, project(): pl.pallas_call(functools.partial(project_kernel, start, bool(carried), sc...  11.1 us
    pallas_call x1, Pallas kernels, arrange(): pl.pallas_call(functools.partial(arrange_kernel, places), in_specs=[ANY],...  6.32 us
    pallas_call x12, Pallas kernels, local(): pl.pallas_call(kernel, in_specs=[VMEM] * len(arrays), out_specs=[VMEM] *...  3.52 us
  transfers between devices with their start and end apart: 31, of which 15 were waited for; matrix products, arithmetic and copies ran while one was open for 0% of the time, Pallas kernels for 23%

profile of v4, /device:TPU:1, one launch (start us, length us, event | category | flops | bytes accessed | tf_op | source)
XLA Modules:
  0.0 131.5 jit_solution(2048853155508135330)
XLA Ops:
  0.6 1.2 copy-done
  1.9 4.3 %shard_map.112 = (bf16[1024,512]{1,0:T(8,128)(2,1)S(1)}, bf16[1024,512]{1,0:T(8,128)(2,1)S(1)}) custom-call(bf16[1024,8192]{1,0:T(8,128)(2,1)} %tok_ref.8, bf16[1024,512]{1,0:T(8,128)(2,1)S(1)} %copy-done), custom_call_target="tpu_custom_call" | custom-call | flops 2147483648 | bytes 4194304 | tf_op jit(solution)/shard_map/pallas_call | solution.py:138
  6.2 2.2 %collective-permute-start.2 = (bf16[1024,512]{1,0:T(8,128)(2,1)S(1)}, bf16[1024,512]{1,0:T(8,128)(2,1)S(1)}, u32[]{:S(2)}, u32[]{:S(2)}) collective-permute-start(bf16[1024,512]{1,0:T(8,128)(2,1)S(1)} %get-tuple-element.49), channel_id=1, source_target_pairs={{0,2},{32,40},{64,66},{96,104},{1,3},{33,41},{65,67},{97,105},{8,1... | collective-permute-start | bytes 3145736 | tf_op jit(solution)/shard_map/ppermute | solution.py:32
  8.4 1.5 %collective-permute-start.3 = (bf16[1024,512]{1,0:T(8,128)(2,1)S(1)}, bf16[1024,512]{1,0:T(8,128)(2,1)S(1)}, u32[]{:S(2)}, u32[]{:S(2)}) collective-permute-start(bf16[1024,512]{1,0:T(8,128)(2,1)S(1)} %get-tuple-element.50), channel_id=1, source_target_pairs={{0,6},{32,56},{64,70},{96,120},{1,7},{33,57},{65,71},{97,121},{8,1... | collective-permute-start | bytes 3145736 | tf_op jit(solution)/shard_map/ppermute | solution.py:32
  9.9 4.3 %shard_map.110 = (bf16[1024,512]{1,0:T(8,128)(2,1)S(1)}, bf16[1024,512]{1,0:T(8,128)(2,1)S(1)}) custom-call(bf16[1024,8192]{1,0:T(8,128)(2,1)} %tok_ref.8, bf16[1024,512]{1,0:T(8,128)(2,1)S(1)} %copy-done), custom_call_target="tpu_custom_call" | custom-call | flops 2147483648 | bytes 4194304 | tf_op jit(solution)/shard_map/pallas_call | solution.py:138
  14.3 1.5 %collective-permute-start = (bf16[1024,512]{1,0:T(8,128)(2,1)S(1)}, bf16[1024,512]{1,0:T(8,128)(2,1)S(1)}, u32[]{:S(2)}, u32[]{:S(2)}) collective-permute-start(bf16[1024,512]{1,0:T(8,128)(2,1)S(1)} %get-tuple-element.45), channel_id=1, source_target_pairs={{0,6},{32,56},{64,70},{96,120},{1,7},{33,57},{65,71},{97,121},{8,1... | collective-permute-start | bytes 3145736 | tf_op jit(solution)/shard_map/ppermute | solution.py:32
  15.8 6.5 %collective-permute-done.2.refs_0_ = bf16[1024,512]{1,0:T(8,128)(2,1)S(1)} collective-permute-done((bf16[1024,512]{1,0:T(8,128)(2,1)S(1)}, bf16[1024,512]{1,0:T(8,128)(2,1)S(1)}, u32[]{:S(2)}, u32[]{:S(2)}) %collective-permute-start.2) | collective-permute-done | bytes 1048608 | tf_op jit(solution)/shard_map/ppermute | solution.py:32
  22.4 4.4 %shard_map.113 = (bf16[1024,512]{1,0:T(8,128)(2,1)S(1)}, bf16[1024,512]{1,0:T(8,128)(2,1)S(1)}) custom-call(bf16[1024,8192]{1,0:T(8,128)(2,1)} %tok_ref.8, bf16[1024,512]{1,0:T(8,128)(2,1)S(1)} %copy-done.1, bf16[1024,512]{1,0:T(8,128)(2,1)S(1)} %collective-permute-done.2.refs_0_, bf16[1024,512]{1,0:T(8,128)(2,1)S(1)} %collective-permute-done.3.refs_1_), custom_call_target="tpu_custom_call" | custom-call | flops 2147483648 | bytes 4194304 | tf_op jit(solution)/shard_map/pallas_call | solution.py:138
  26.7 1.4 %collective-permute-start.4 = (bf16[1024,512]{1,0:T(8,128)(2,1)S(1)}, bf16[1024,512]{1,0:T(8,128)(2,1)S(1)}, u32[]{:S(2)}, u32[]{:S(2)}) collective-permute-start(bf16[1024,512]{1,0:T(8,128)(2,1)S(1)} %get-tuple-element.51), channel_id=1, source_target_pairs={{0,2},{32,40},{64,66},{96,104},{1,3},{33,41},{65,67},{97,105},{8,1... | collective-permute-start | bytes 3145736 | tf_op jit(solution)/shard_map/ppermute | solution.py:32
  28.1 1.5 %collective-permute-start.5 = (bf16[1024,512]{1,0:T(8,128)(2,1)S(1)}, bf16[1024,512]{1,0:T(8,128)(2,1)S(1)}, u32[]{:S(2)}, u32[]{:S(2)}) collective-permute-start(bf16[1024,512]{1,0:T(8,128)(2,1)S(1)} %get-tuple-element.52), channel_id=1, source_target_pairs={{0,6},{32,56},{64,70},{96,120},{1,7},{33,57},{65,71},{97,121},{8,1... | collective-permute-start | bytes 3145736 | tf_op jit(solution)/shard_map/ppermute | solution.py:32
  29.6 4.0 %collective-permute-done.refs_0_ = bf16[1024,512]{1,0:T(8,128)(2,1)S(1)} collective-permute-done((bf16[1024,512]{1,0:T(8,128)(2,1)S(1)}, bf16[1024,512]{1,0:T(8,128)(2,1)S(1)}, u32[]{:S(2)}, u32[]{:S(2)}) %collective-permute-start) | collective-permute-done | bytes 1048608 | tf_op jit(solution)/shard_map/ppermute | solution.py:32
  33.6 4.3 %shard_map.111 = (f32[1024,512]{1,0:T(8,128)S(1)}, f32[1024,512]{1,0:T(8,128)S(1)}) custom-call(bf16[1024,8192]{1,0:T(8,128)(2,1)} %tok_ref.8, bf16[1024,512]{1,0:T(8,128)(2,1)S(1)} %copy-done.1, bf16[1024,512]{1,0:T(8,128)(2,1)S(1)} %collective-permute-done.refs_0_, bf16[1024,512]{1,0:T(8,128)(2,1)S(1)} %collective-permute-done.1.refs_1_), custom_call_target="tpu_custom_call" | custom-call | flops 2147483648 | bytes 4194304 | tf_op jit(solution)/shard_map/pallas_call | solution.py:138
  37.9 6.9 %collective-permute-done.4.got1 = bf16[1024,512]{1,0:T(8,128)(2,1)S(1)} collective-permute-done((bf16[1024,512]{1,0:T(8,128)(2,1)S(1)}, bf16[1024,512]{1,0:T(8,128)(2,1)S(1)}, u32[]{:S(2)}, u32[]{:S(2)}) %collective-permute-start.4) | collective-permute-done | bytes 1048608 | tf_op jit(solution)/shard_map/ppermute | solution.py:32
  44.8 0.3 shard_map.114
  45.2 1.3 collective-permute-start.10
  46.4 1.5 %collective-permute-start.11 = (bf16[256,512]{1,0:T(8,128)(2,1)S(1)}, bf16[256,512]{1,0:T(8,128)(2,1)S(1)}, u32[]{:S(2)}, u32[]{:S(2)}) collective-permute-start(bf16[256,512]{1,0:T(8,128)(2,1)S(1)} %get-tuple-element.60), channel_id=1, source_target_pairs={{0,24},{32,38},{64,88},{96,102},{1,25},{33,39},{65,89},{97,103},{8... | collective-permute-start | bytes 786440 | tf_op jit(solution)/shard_map/ppermute | solution.py:32
  47.9 1.5 %collective-permute-start.9 = (bf16[256,512]{1,0:T(8,128)(2,1)S(1)}, bf16[256,512]{1,0:T(8,128)(2,1)S(1)}, u32[]{:S(2)}, u32[]{:S(2)}) collective-permute-start(bf16[256,512]{1,0:T(8,128)(2,1)S(1)} %get-tuple-element.58), channel_id=1, source_target_pairs={{0,16},{32,36},{64,80},{96,100},{1,17},{33,37},{65,81},{97,101},{8... | collective-permute-start | bytes 786440 | tf_op jit(solution)/shard_map/ppermute | solution.py:32
  49.4 1.4 %collective-permute-start.6 = (bf16[256,512]{1,0:T(8,128)(2,1)S(1)}, bf16[256,512]{1,0:T(8,128)(2,1)S(1)}, u32[]{:S(2)}, u32[]{:S(2)}) collective-permute-start(bf16[256,512]{1,0:T(8,128)(2,1)S(1)} %get-tuple-element.54), channel_id=1, source_target_pairs={{0,16},{32,36},{64,80},{96,100},{1,17},{33,37},{65,81},{97,101},{8... | collective-permute-start | bytes 786440 | tf_op jit(solution)/shard_map/ppermute | solution.py:32
  50.9 1.1 collective-permute-done.10.refs_1_
  52.0 1.6 %collective-permute-start.8 = (bf16[256,512]{1,0:T(8,128)(2,1)S(1)}, bf16[256,512]{1,0:T(8,128)(2,1)S(1)}, u32[]{:S(2)}, u32[]{:S(2)}) collective-permute-start(bf16[256,512]{1,0:T(8,128)(2,1)S(1)} %get-tuple-element.56), channel_id=1, source_target_pairs={{0,24},{32,38},{64,88},{96,102},{1,25},{33,39},{65,89},{97,103},{8... | collective-permute-start | bytes 786440 | tf_op jit(solution)/shard_map/ppermute | solution.py:32
  53.6 2.2 %collective-permute-done.9.refs_0_ = bf16[256,512]{1,0:T(8,128)(2,1)S(1)} collective-permute-done((bf16[256,512]{1,0:T(8,128)(2,1)S(1)}, bf16[256,512]{1,0:T(8,128)(2,1)S(1)}, u32[]{:S(2)}, u32[]{:S(2)}) %collective-permute-start.9) | collective-permute-done | bytes 262176 | tf_op jit(solution)/shard_map/ppermute | solution.py:32
  55.8 0.1 shard_map.116
  55.9 3.7 %collective-permute-start.12 = (bf16[256,512]{1,0:T(8,128)(2,1)S(1)}, bf16[256,512]{1,0:T(8,128)(2,1)S(1)}, u32[]{:S(2)}, u32[]{:S(2)}) collective-permute-start(bf16[256,512]{1,0:T(8,128)(2,1)S(1)} %shard_map.116), channel_id=1, source_target_pairs={{0,1},{32,33},{64,65},{96,97},{1,0},{33,32},{65,64},{97,96},{8,9},... | collective-permute-start | bytes 786440 | tf_op jit(solution)/shard_map/ppermute | solution.py:32
  59.5 6.3 %shard_map.117.held = bf16[1024,8192]{1,0:T(8,128)(2,1)S(1)} custom-call(bf16[1024,8192]{1,0:T(8,128)(2,1)} %tok_ref.8), custom_call_target="tpu_custom_call" | custom-call | flops 1 | bytes 1 | tf_op jit(solution)/shard_map/pallas_call | solution.py:288
  66.0 0.1 shard_map.115.keep
  66.1 0.8 copy-done.4
  66.9 0.2 copy-done.5
  67.1 0.2 copy-done.6
  67.2 1.3 shard_map.118
  68.5 3.1 %collective-permute-start.13 = (f32[256,256]{1,0:T(8,128)S(1)}, f32[256,256]{1,0:T(8,128)S(1)}, u32[]{:S(2)}, u32[]{:S(2)}) collective-permute-start(f32[256,256]{1,0:T(8,128)S(1)} %get-tuple-element.67), channel_id=1, source_target_pairs={{0,32},{32,0},{64,96},{96,64},{1,33},{33,1},{65,97},{97,65},{8,40}... | collective-permute-start | bytes 786440 | tf_op jit(solution)/shard_map/ppermute | solution.py:32
  71.7 1.2 collective-permute-done.13.right
  72.8 0.8 collective-permute-start.14
  73.7 4.0 %collective-permute-done.14.right = bf16[256,256]{1,0:T(8,128)(2,1)S(1)} collective-permute-done((bf16[256,256]{1,0:T(8,128)(2,1)S(1)}, bf16[256,256]{1,0:T(8,128)(2,1)S(1)}, u32[]{:S(2)}, u32[]{:S(2)}) %collective-permute-start.14) | collective-permute-done | bytes 131104 | tf_op jit(solution)/shard_map/ppermute | solution.py:32
  77.6 0.1 shard_map.120
  77.8 1.3 collective-permute-start.15
  79.1 2.2 %collective-permute-start.16 = (bf16[256,256]{1,0:T(8,128)(2,1)S(1)}, bf16[256,256]{1,0:T(8,128)(2,1)S(1)}, u32[]{:S(2)}, u32[]{:S(2)}) collective-permute-start(bf16[256,256]{1,0:T(8,128)(2,1)S(1)} %get-tuple-element.68.mine), channel_id=1, source_target_pairs={{32,65},{96,1},{1,96},{65,32},{40,73},{104,9},{9,104},{73,40},{48,... | collective-permute-start | bytes 393224 | tf_op jit(solution)/shard_map/ppermute | solution.py:32
  81.3 1.6 %collective-permute-done.15.one = bf16[256,256]{1,0:T(8,128)(2,1)S(1)} collective-permute-done((bf16[256,256]{1,0:T(8,128)(2,1)S(1)}, bf16[256,256]{1,0:T(8,128)(2,1)S(1)}, u32[]{:S(2)}, u32[]{:S(2)}) %collective-permute-start.15) | collective-permute-done | bytes 131104 | tf_op jit(solution)/shard_map/ppermute | solution.py:32
  82.9 3.7 %collective-permute-done.16.two = bf16[256,256]{1,0:T(8,128)(2,1)S(1)} collective-permute-done((bf16[256,256]{1,0:T(8,128)(2,1)S(1)}, bf16[256,256]{1,0:T(8,128)(2,1)S(1)}, u32[]{:S(2)}, u32[]{:S(2)}) %collective-permute-start.16) | collective-permute-done | bytes 131104 | tf_op jit(solution)/shard_map/ppermute | solution.py:32
  86.6 1.3 collective-permute-start.17
  87.9 3.7 %collective-permute-start.18 = (bf16[256,512]{1,0:T(8,128)(2,1)S(1)}, bf16[256,512]{1,0:T(8,128)(2,1)S(1)}, u32[]{:S(2)}, u32[]{:S(2)}) collective-permute-start(bf16[256,512]{1,0:T(8,128)(2,1)S(1)} %shard_map.121.refs_0_), channel_id=1, source_target_pairs={{0,6},{32,56},{64,70},{96,120},{1,7},{33,57},{65,71},{97,121},{8,1... | collective-permute-start | bytes 786440 | tf_op jit(solution)/shard_map/ppermute | solution.py:32
  91.6 1.1 collective-permute-start.19
  92.7 2.6 %collective-permute-done.17.refs_1_ = bf16[256,512]{1,0:T(8,128)(2,1)S(1)} collective-permute-done((bf16[256,512]{1,0:T(8,128)(2,1)S(1)}, bf16[256,512]{1,0:T(8,128)(2,1)S(1)}, u32[]{:S(2)}, u32[]{:S(2)}) %collective-permute-start.17) | collective-permute-done | bytes 262176 | tf_op jit(solution)/shard_map/ppermute | solution.py:32
  95.2 2.4 %collective-permute-done.18.refs_2_ = bf16[256,512]{1,0:T(8,128)(2,1)S(1)} collective-permute-done((bf16[256,512]{1,0:T(8,128)(2,1)S(1)}, bf16[256,512]{1,0:T(8,128)(2,1)S(1)}, u32[]{:S(2)}, u32[]{:S(2)}) %collective-permute-start.18) | collective-permute-done | bytes 262176 | tf_op jit(solution)/shard_map/ppermute | solution.py:32
  97.7 1.5 %collective-permute-done.19.refs_3_ = bf16[256,512]{1,0:T(8,128)(2,1)S(1)} collective-permute-done((bf16[256,512]{1,0:T(8,128)(2,1)S(1)}, bf16[256,512]{1,0:T(8,128)(2,1)S(1)}, u32[]{:S(2)}, u32[]{:S(2)}) %collective-permute-start.19) | collective-permute-done | bytes 262176 | tf_op jit(solution)/shard_map/ppermute | solution.py:32
  99.2 0.1 shard_map.122
  99.4 0.1 collective-permute-start.22
  99.5 1.0 collective-permute-start.20
  100.4 1.8 %collective-permute-start.21 = (bf16[512,512]{1,0:T(8,128)(2,1)S(1)}, bf16[512,512]{1,0:T(8,128)(2,1)S(1)}, u32[]{:S(2)}, u32[]{:S(2)}) collective-permute-start(bf16[512,512]{1,0:T(8,128)(2,1)S(1)} %get-tuple-element.70), channel_id=1, source_target_pairs={{0,24},{32,38},{64,88},{96,102},{1,25},{33,39},{65,89},{97,103},{8... | collective-permute-start | bytes 1572872 | tf_op jit(solution)/shard_map/ppermute | solution.py:32
  102.2 2.7 %collective-permute-start.26 = (bf16[512,512]{1,0:T(8,128)(2,1)S(1)}, bf16[512,512]{1,0:T(8,128)(2,1)S(1)}, u32[]{:S(2)}, u32[]{:S(2)}) collective-permute-start(bf16[512,512]{1,0:T(8,128)(2,1)S(1)} %get-tuple-element.69), channel_id=1, source_target_pairs={{0,24},{32,38},{64,88},{96,102},{1,25},{33,39},{65,89},{97,103},{8... | collective-permute-start | bytes 1572872 | tf_op jit(solution)/shard_map/ppermute | solution.py:32
  104.9 2.5 %shard_map.123.refs_2_ = f32[1024,512]{1,0:T(8,128)S(1)} custom-call(bf16[1024,8192]{1,0:T(8,128)(2,1)S(1)} %shard_map.117.held, bf16[1024,512]{1,0:T(8,128)(2,1)S(1)} %get-tuple-element.72.refs_0_, bf16[1024,512]{1,0:T(8,128)(2,1)S(1)} %collective-permute-done.22.refs_1_), custom_call_target="tpu_custom_call" | custom-call | flops 1 | bytes 1 | tf_op jit(solution)/shard_map/pallas_call | solution.py:319
  107.4 1.7 %collective-permute-done.20.left = bf16[512,512]{1,0:T(8,128)(2,1)S(1)} collective-permute-done((bf16[512,512]{1,0:T(8,128)(2,1)S(1)}, bf16[512,512]{1,0:T(8,128)(2,1)S(1)}, u32[]{:S(2)}, u32[]{:S(2)}) %collective-permute-start.20) | collective-permute-done | bytes 524320 | tf_op jit(solution)/shard_map/ppermute | solution.py:32
  109.1 1.4 %collective-permute-start.28 = (bf16[1024,512]{1,0:T(8,128)(2,1)S(1)}, bf16[1024,512]{1,0:T(8,128)(2,1)S(1)}, u32[]{:S(2)}, u32[]{:S(2)}) collective-permute-start(bf16[1024,512]{1,0:T(8,128)(2,1)S(1)} %shard_map.125.refs_0_), channel_id=1, source_target_pairs={{0,32},{32,0},{64,96},{96,64},{1,33},{33,1},{65,97},{97,65},{8,40}... | collective-permute-start | bytes 3145736 | tf_op jit(solution)/shard_map/ppermute | solution.py:32
  110.5 4.2 %collective-permute-done.25.left = bf16[512,512]{1,0:T(8,128)(2,1)S(1)} collective-permute-done((bf16[512,512]{1,0:T(8,128)(2,1)S(1)}, bf16[512,512]{1,0:T(8,128)(2,1)S(1)}, u32[]{:S(2)}, u32[]{:S(2)}) %collective-permute-start.25) | collective-permute-done | bytes 524320 | tf_op jit(solution)/shard_map/ppermute | solution.py:32
  114.8 1.4 %collective-permute-start.27 = (bf16[1024,512]{1,0:T(8,128)(2,1)S(1)}, bf16[1024,512]{1,0:T(8,128)(2,1)S(1)}, u32[]{:S(2)}, u32[]{:S(2)}) collective-permute-start(bf16[1024,512]{1,0:T(8,128)(2,1)S(1)} %shard_map.124.refs_0_), channel_id=1, source_target_pairs={{0,32},{32,0},{64,96},{96,64},{1,33},{33,1},{65,97},{97,65},{8,40}... | collective-permute-start | bytes 3145736 | tf_op jit(solution)/shard_map/ppermute | solution.py:32
  116.1 0.9 collective-permute-start.23
  117.0 1.8 %collective-permute-start.24 = (bf16[512,512]{1,0:T(8,128)(2,1)S(1)}, bf16[512,512]{1,0:T(8,128)(2,1)S(1)}, u32[]{:S(2)}, u32[]{:S(2)}) collective-permute-start(bf16[512,512]{1,0:T(8,128)(2,1)S(1)} %collective-permute-done.21.right), channel_id=1, source_target_pairs={{0,24},{32,38},{64,88},{96,102},{1,25},{33,39},{65,89},{97,103},{8... | collective-permute-start | bytes 1572872 | tf_op jit(solution)/shard_map/ppermute | solution.py:32
  118.8 2.5 %shard_map.126.refs_2_ = f32[1024,512]{1,0:T(8,128)S(1)} custom-call(bf16[1024,8192]{1,0:T(8,128)(2,1)S(1)} %shard_map.117.held, bf16[1024,512]{1,0:T(8,128)(2,1)S(1)} %shard_map.125.refs_0_, bf16[1024,512]{1,0:T(8,128)(2,1)S(1)} %collective-permute-done.28.refs_1_, f32[1024,512]{1,0:T(8,128)S(1)} %shard_map.123.refs_2_), custom_call_target="tpu_custom_call" | custom-call | flops 1 | bytes 1 | tf_op jit(solution)/shard_map/pallas_call | solution.py:319
  121.3 1.0 collective-permute-start.29
  122.3 2.5 %shard_map.127.refs_1_ = f32[1024,512]{1,0:T(8,128)S(1)} custom-call(bf16[1024,8192]{1,0:T(8,128)(2,1)S(1)} %shard_map.117.held, bf16[1024,512]{1,0:T(8,128)(2,1)S(1)} %shard_map.124.refs_0_, bf16[1024,512]{1,0:T(8,128)(2,1)S(1)} %collective-permute-done.27.refs_1_, f32[1024,512]{1,0:T(8,128)S(1)} %shard_map.126.refs_2_), custom_call_target="tpu_custom_call" | custom-call | flops 1 | bytes 1 | tf_op jit(solution)/shard_map/pallas_call | solution.py:319
  124.8 1.1 shard_map.128
  126.0 0.7 collective-permute-start.30
  126.7 1.3 %shard_map.130.refs_1_ = f32[1024,512]{1,0:T(8,128)S(1)} custom-call(bf16[1024,8192]{1,0:T(8,128)(2,1)S(1)} %shard_map.117.held, bf16[1024,512]{1,0:T(8,128)(2,1)S(1)} %shard_map.129.refs_0_, f32[1024,512]{1,0:T(8,128)S(1)} %shard_map.127.refs_1_), custom_call_target="tpu_custom_call" | custom-call | flops 1 | bytes 1 | tf_op jit(solution)/shard_map/pallas_call | solution.py:319
  128.1 1.0 collective-permute-done.30.refs_0_
  129.0 2.3 %shard_map.131 = bf16[1024,512]{1,0:T(8,128)(2,1)} custom-call(bf16[1024,8192]{1,0:T(8,128)(2,1)S(1)} %shard_map.117.held, bf16[1024,512]{1,0:T(8,128)(2,1)S(1)} %collective-permute-done.30.refs_0_, f32[1024,512]{1,0:T(8,128)S(1)} %shard_map.130.refs_1_), custom_call_target="tpu_custom_call" | custom-call | flops 1 | bytes 1 | tf_op jit(solution)/shard_map/pallas_call | solution.py:319
  (34 shorter events, 0.5 us)
Async XLA Ops:
  0.6 1.2 copy-start
  6.2 16.1 %collective-permute-start.2 = (bf16[1024,512]{1,0:T(8,128)(2,1)S(1)}, bf16[1024,512]{1,0:T(8,128)(2,1)S(1)}, u32[]{:S(2)}, u32[]{:S(2)}) collective-permute-start(bf16[1024,512]{1,0:T(8,128)(2,1)S(1)} %get-tuple-element.49), channel_id=1, source_target_pairs={{0,2},{32,40},{64,66},{96,104},{1,3},{33,41},{65,67},{97,105},{8,1... | collective-permute-start | bytes 3145736 | tf_op jit(solution)/shard_map/ppermute | solution.py:32
  8.4 13.9 %copy-start.1 = (bf16[1024,512]{1,0:T(8,128)(2,1)S(1)}, bf16[1024,512]{1,0:T(8,128)(2,1)}, u32[]{:S(2)}) copy-start(bf16[1024,512]{1,0:T(8,128)(2,1)} %grad_ref.7) | copy-start | bytes 3145732
  8.4 13.9 %collective-permute-start.3 = (bf16[1024,512]{1,0:T(8,128)(2,1)S(1)}, bf16[1024,512]{1,0:T(8,128)(2,1)S(1)}, u32[]{:S(2)}, u32[]{:S(2)}) collective-permute-start(bf16[1024,512]{1,0:T(8,128)(2,1)S(1)} %get-tuple-element.50), channel_id=1, source_target_pairs={{0,6},{32,56},{64,70},{96,120},{1,7},{33,57},{65,71},{97,121},{8,1... | collective-permute-start | bytes 3145736 | tf_op jit(solution)/shard_map/ppermute | solution.py:32
  14.3 19.3 %collective-permute-start = (bf16[1024,512]{1,0:T(8,128)(2,1)S(1)}, bf16[1024,512]{1,0:T(8,128)(2,1)S(1)}, u32[]{:S(2)}, u32[]{:S(2)}) collective-permute-start(bf16[1024,512]{1,0:T(8,128)(2,1)S(1)} %get-tuple-element.45), channel_id=1, source_target_pairs={{0,6},{32,56},{64,70},{96,120},{1,7},{33,57},{65,71},{97,121},{8,1... | collective-permute-start | bytes 3145736 | tf_op jit(solution)/shard_map/ppermute | solution.py:32
  15.7 17.8 %collective-permute-start.1 = (bf16[1024,512]{1,0:T(8,128)(2,1)S(1)}, bf16[1024,512]{1,0:T(8,128)(2,1)S(1)}, u32[]{:S(2)}, u32[]{:S(2)}) collective-permute-start(bf16[1024,512]{1,0:T(8,128)(2,1)S(1)} %get-tuple-element.46), channel_id=1, source_target_pairs={{0,2},{32,40},{64,66},{96,104},{1,3},{33,41},{65,67},{97,105},{8,1... | collective-permute-start | bytes 3145736 | tf_op jit(solution)/shard_map/ppermute | solution.py:32
  26.7 18.1 %collective-permute-start.4 = (bf16[1024,512]{1,0:T(8,128)(2,1)S(1)}, bf16[1024,512]{1,0:T(8,128)(2,1)S(1)}, u32[]{:S(2)}, u32[]{:S(2)}) collective-permute-start(bf16[1024,512]{1,0:T(8,128)(2,1)S(1)} %get-tuple-element.51), channel_id=1, source_target_pairs={{0,2},{32,40},{64,66},{96,104},{1,3},{33,41},{65,67},{97,105},{8,1... | collective-permute-start | bytes 3145736 | tf_op jit(solution)/shard_map/ppermute | solution.py:32
  28.1 16.7 %collective-permute-start.5 = (bf16[1024,512]{1,0:T(8,128)(2,1)S(1)}, bf16[1024,512]{1,0:T(8,128)(2,1)S(1)}, u32[]{:S(2)}, u32[]{:S(2)}) collective-permute-start(bf16[1024,512]{1,0:T(8,128)(2,1)S(1)} %get-tuple-element.52), channel_id=1, source_target_pairs={{0,6},{32,56},{64,70},{96,120},{1,7},{33,57},{65,71},{97,121},{8,1... | collective-permute-start | bytes 3145736 | tf_op jit(solution)/shard_map/ppermute | solution.py:32
  45.2 6.8 %collective-permute-start.10 = (bf16[256,512]{1,0:T(8,128)(2,1)S(1)}, bf16[256,512]{1,0:T(8,128)(2,1)S(1)}, u32[]{:S(2)}, u32[]{:S(2)}) collective-permute-start(bf16[256,512]{1,0:T(8,128)(2,1)S(1)} %get-tuple-element.59), channel_id=1, source_target_pairs={{0,8},{32,34},{64,72},{96,98},{1,9},{33,35},{65,73},{97,99},{8,16}... | collective-permute-start | bytes 786440 | tf_op jit(solution)/shard_map/ppermute | solution.py:32
  46.4 7.1 %collective-permute-start.11 = (bf16[256,512]{1,0:T(8,128)(2,1)S(1)}, bf16[256,512]{1,0:T(8,128)(2,1)S(1)}, u32[]{:S(2)}, u32[]{:S(2)}) collective-permute-start(bf16[256,512]{1,0:T(8,128)(2,1)S(1)} %get-tuple-element.60), channel_id=1, source_target_pairs={{0,24},{32,38},{64,88},{96,102},{1,25},{33,39},{65,89},{97,103},{8... | collective-permute-start | bytes 786440 | tf_op jit(solution)/shard_map/ppermute | solution.py:32
  47.9 7.9 %collective-permute-start.9 = (bf16[256,512]{1,0:T(8,128)(2,1)S(1)}, bf16[256,512]{1,0:T(8,128)(2,1)S(1)}, u32[]{:S(2)}, u32[]{:S(2)}) collective-permute-start(bf16[256,512]{1,0:T(8,128)(2,1)S(1)} %get-tuple-element.58), channel_id=1, source_target_pairs={{0,16},{32,36},{64,80},{96,100},{1,17},{33,37},{65,81},{97,101},{8... | collective-permute-start | bytes 786440 | tf_op jit(solution)/shard_map/ppermute | solution.py:32
  49.4 16.5 %collective-permute-start.6 = (bf16[256,512]{1,0:T(8,128)(2,1)S(1)}, bf16[256,512]{1,0:T(8,128)(2,1)S(1)}, u32[]{:S(2)}, u32[]{:S(2)}) collective-permute-start(bf16[256,512]{1,0:T(8,128)(2,1)S(1)} %get-tuple-element.54), channel_id=1, source_target_pairs={{0,16},{32,36},{64,80},{96,100},{1,17},{33,37},{65,81},{97,101},{8... | collective-permute-start | bytes 786440 | tf_op jit(solution)/shard_map/ppermute | solution.py:32
  50.9 15.0 %collective-permute-start.7 = (bf16[256,512]{1,0:T(8,128)(2,1)S(1)}, bf16[256,512]{1,0:T(8,128)(2,1)S(1)}, u32[]{:S(2)}, u32[]{:S(2)}) collective-permute-start(bf16[256,512]{1,0:T(8,128)(2,1)S(1)} %get-tuple-element.55), channel_id=1, source_target_pairs={{0,8},{32,34},{64,72},{96,98},{1,9},{33,35},{65,73},{97,99},{8,16}... | collective-permute-start | bytes 786440 | tf_op jit(solution)/shard_map/ppermute | solution.py:32
  52.0 14.0 %collective-permute-start.8 = (bf16[256,512]{1,0:T(8,128)(2,1)S(1)}, bf16[256,512]{1,0:T(8,128)(2,1)S(1)}, u32[]{:S(2)}, u32[]{:S(2)}) collective-permute-start(bf16[256,512]{1,0:T(8,128)(2,1)S(1)} %get-tuple-element.56), channel_id=1, source_target_pairs={{0,24},{32,38},{64,88},{96,102},{1,25},{33,39},{65,89},{97,103},{8... | collective-permute-start | bytes 786440 | tf_op jit(solution)/shard_map/ppermute | solution.py:32
  55.9 10.2 %collective-permute-start.12 = (bf16[256,512]{1,0:T(8,128)(2,1)S(1)}, bf16[256,512]{1,0:T(8,128)(2,1)S(1)}, u32[]{:S(2)}, u32[]{:S(2)}) collective-permute-start(bf16[256,512]{1,0:T(8,128)(2,1)S(1)} %shard_map.116), channel_id=1, source_target_pairs={{0,1},{32,33},{64,65},{96,97},{1,0},{33,32},{65,64},{97,96},{8,9},... | collective-permute-start | bytes 786440 | tf_op jit(solution)/shard_map/ppermute | solution.py:32
  65.9 1.0 copy-start.4
  65.9 1.2 copy-start.5
  65.9 1.3 %copy-start.6 = (f32[1,256,512]{2,1,0:T(8,128)S(1)}, f32[1,256,512]{2,1,0:T(8,128)}, u32[]{:S(2)}) copy-start(f32[1,256,512]{2,1,0:T(8,128)} %param.11) | copy-start | bytes 1572868
  65.9 11.7 %copy-start.2 = (f32[256,512]{1,0:T(8,128)S(1)}, f32[256,512]{1,0:T(8,128)}, u32[]{:S(2)}) copy-start(f32[256,512]{1,0:T(8,128)} %weights_ref.3) | copy-start | bytes 1572868
  65.9 11.7 %copy-start.3 = (f32[256,512]{1,0:T(8,128)S(1)}, f32[256,512]{1,0:T(8,128)}, u32[]{:S(2)}) copy-start(f32[256,512]{1,0:T(8,128)} %momentum_ref.3) | copy-start | bytes 1572868
  68.5 4.3 %collective-permute-start.13 = (f32[256,256]{1,0:T(8,128)S(1)}, f32[256,256]{1,0:T(8,128)S(1)}, u32[]{:S(2)}, u32[]{:S(2)}) collective-permute-start(f32[256,256]{1,0:T(8,128)S(1)} %get-tuple-element.67), channel_id=1, source_target_pairs={{0,32},{32,0},{64,96},{96,64},{1,33},{33,1},{65,97},{97,65},{8,40}... | collective-permute-start | bytes 786440 | tf_op jit(solution)/shard_map/ppermute | solution.py:32
  72.8 4.8 %collective-permute-start.14 = (bf16[256,256]{1,0:T(8,128)(2,1)S(1)}, bf16[256,256]{1,0:T(8,128)(2,1)S(1)}, u32[]{:S(2)}, u32[]{:S(2)}) collective-permute-start(bf16[256,256]{1,0:T(8,128)(2,1)S(1)} %shard_map.119.left), channel_id=1, source_target_pairs={{0,64},{32,96},{64,0},{96,32},{1,65},{33,97},{65,1},{97,33},{8,72}... | collective-permute-start | bytes 393224 | tf_op jit(solution)/shard_map/ppermute | solution.py:32
  77.8 5.1 %collective-permute-start.15 = (bf16[256,256]{1,0:T(8,128)(2,1)S(1)}, bf16[256,256]{1,0:T(8,128)(2,1)S(1)}, u32[]{:S(2)}, u32[]{:S(2)}) collective-permute-start(bf16[256,256]{1,0:T(8,128)(2,1)S(1)} %get-tuple-element.68.mine), channel_id=1, source_target_pairs={{0,65},{32,0},{64,1},{96,64},{1,33},{33,96},{65,97},{97,32},{8,73}... | collective-permute-start | bytes 393224 | tf_op jit(solution)/shard_map/ppermute | solution.py:32
  79.1 7.5 %collective-permute-start.16 = (bf16[256,256]{1,0:T(8,128)(2,1)S(1)}, bf16[256,256]{1,0:T(8,128)(2,1)S(1)}, u32[]{:S(2)}, u32[]{:S(2)}) collective-permute-start(bf16[256,256]{1,0:T(8,128)(2,1)S(1)} %get-tuple-element.68.mine), channel_id=1, source_target_pairs={{32,65},{96,1},{1,96},{65,32},{40,73},{104,9},{9,104},{73,40},{48,... | collective-permute-start | bytes 393224 | tf_op jit(solution)/shard_map/ppermute | solution.py:32
  86.6 8.7 %collective-permute-start.17 = (bf16[256,512]{1,0:T(8,128)(2,1)S(1)}, bf16[256,512]{1,0:T(8,128)(2,1)S(1)}, u32[]{:S(2)}, u32[]{:S(2)}) collective-permute-start(bf16[256,512]{1,0:T(8,128)(2,1)S(1)} %shard_map.121.refs_0_), channel_id=1, source_target_pairs={{0,2},{32,40},{64,66},{96,104},{1,3},{33,41},{65,67},{97,105},{8,1... | collective-permute-start | bytes 786440 | tf_op jit(solution)/shard_map/ppermute | solution.py:32
  87.9 9.8 %collective-permute-start.18 = (bf16[256,512]{1,0:T(8,128)(2,1)S(1)}, bf16[256,512]{1,0:T(8,128)(2,1)S(1)}, u32[]{:S(2)}, u32[]{:S(2)}) collective-permute-start(bf16[256,512]{1,0:T(8,128)(2,1)S(1)} %shard_map.121.refs_0_), channel_id=1, source_target_pairs={{0,6},{32,56},{64,70},{96,120},{1,7},{33,57},{65,71},{97,121},{8,1... | collective-permute-start | bytes 786440 | tf_op jit(solution)/shard_map/ppermute | solution.py:32
  91.6 7.7 %collective-permute-start.19 = (bf16[256,512]{1,0:T(8,128)(2,1)S(1)}, bf16[256,512]{1,0:T(8,128)(2,1)S(1)}, u32[]{:S(2)}, u32[]{:S(2)}) collective-permute-start(bf16[256,512]{1,0:T(8,128)(2,1)S(1)} %shard_map.121.refs_0_), channel_id=1, source_target_pairs={{0,4},{32,48},{64,68},{96,112},{1,5},{33,49},{65,69},{97,113},{8,1... | collective-permute-start | bytes 786440 | tf_op jit(solution)/shard_map/ppermute | solution.py:32
  99.4 5.5 %collective-permute-start.22 = (bf16[1024,512]{1,0:T(8,128)(2,1)S(1)}, bf16[1024,512]{1,0:T(8,128)(2,1)S(1)}, u32[]{:S(2)}, u32[]{:S(2)}) collective-permute-start(bf16[1024,512]{1,0:T(8,128)(2,1)S(1)} %get-tuple-element.72.refs_0_), channel_id=1, source_target_pairs={{0,32},{32,0},{64,96},{96,64},{1,33},{33,1},{65,97},{97,65},{8,40}... | collective-permute-start | bytes 3145736 | tf_op jit(solution)/shard_map/ppermute | solution.py:32
  99.5 9.6 %collective-permute-start.20 = (bf16[512,512]{1,0:T(8,128)(2,1)S(1)}, bf16[512,512]{1,0:T(8,128)(2,1)S(1)}, u32[]{:S(2)}, u32[]{:S(2)}) collective-permute-start(bf16[512,512]{1,0:T(8,128)(2,1)S(1)} %get-tuple-element.69), channel_id=1, source_target_pairs={{0,8},{32,34},{64,72},{96,98},{1,9},{33,35},{65,73},{97,99},{8,16}... | collective-permute-start | bytes 1572872 | tf_op jit(solution)/shard_map/ppermute | solution.py:32
  100.4 8.6 %collective-permute-start.21 = (bf16[512,512]{1,0:T(8,128)(2,1)S(1)}, bf16[512,512]{1,0:T(8,128)(2,1)S(1)}, u32[]{:S(2)}, u32[]{:S(2)}) collective-permute-start(bf16[512,512]{1,0:T(8,128)(2,1)S(1)} %get-tuple-element.70), channel_id=1, source_target_pairs={{0,24},{32,38},{64,88},{96,102},{1,25},{33,39},{65,89},{97,103},{8... | collective-permute-start | bytes 1572872 | tf_op jit(solution)/shard_map/ppermute | solution.py:32
  102.2 12.5 %collective-permute-start.25 = (bf16[512,512]{1,0:T(8,128)(2,1)S(1)}, bf16[512,512]{1,0:T(8,128)(2,1)S(1)}, u32[]{:S(2)}, u32[]{:S(2)}) collective-permute-start(bf16[512,512]{1,0:T(8,128)(2,1)S(1)} %get-tuple-element.70), channel_id=1, source_target_pairs={{0,8},{32,34},{64,72},{96,98},{1,9},{33,35},{65,73},{97,99},{8,16}... | collective-permute-start | bytes 1572872 | tf_op jit(solution)/shard_map/ppermute | solution.py:32
  102.2 12.5 %collective-permute-start.26 = (bf16[512,512]{1,0:T(8,128)(2,1)S(1)}, bf16[512,512]{1,0:T(8,128)(2,1)S(1)}, u32[]{:S(2)}, u32[]{:S(2)}) collective-permute-start(bf16[512,512]{1,0:T(8,128)(2,1)S(1)} %get-tuple-element.69), channel_id=1, source_target_pairs={{0,24},{32,38},{64,88},{96,102},{1,25},{33,39},{65,89},{97,103},{8... | collective-permute-start | bytes 1572872 | tf_op jit(solution)/shard_map/ppermute | solution.py:32
  109.1 9.7 %collective-permute-start.28 = (bf16[1024,512]{1,0:T(8,128)(2,1)S(1)}, bf16[1024,512]{1,0:T(8,128)(2,1)S(1)}, u32[]{:S(2)}, u32[]{:S(2)}) collective-permute-start(bf16[1024,512]{1,0:T(8,128)(2,1)S(1)} %shard_map.125.refs_0_), channel_id=1, source_target_pairs={{0,32},{32,0},{64,96},{96,64},{1,33},{33,1},{65,97},{97,65},{8,40}... | collective-permute-start | bytes 3145736 | tf_op jit(solution)/shard_map/ppermute | solution.py:32
  114.8 7.6 %collective-permute-start.27 = (bf16[1024,512]{1,0:T(8,128)(2,1)S(1)}, bf16[1024,512]{1,0:T(8,128)(2,1)S(1)}, u32[]{:S(2)}, u32[]{:S(2)}) collective-permute-start(bf16[1024,512]{1,0:T(8,128)(2,1)S(1)} %shard_map.124.refs_0_), channel_id=1, source_target_pairs={{0,32},{32,0},{64,96},{96,64},{1,33},{33,1},{65,97},{97,65},{8,40}... | collective-permute-start | bytes 3145736 | tf_op jit(solution)/shard_map/ppermute | solution.py:32
  116.1 9.8 %collective-permute-start.23 = (bf16[512,512]{1,0:T(8,128)(2,1)S(1)}, bf16[512,512]{1,0:T(8,128)(2,1)S(1)}, u32[]{:S(2)}, u32[]{:S(2)}) collective-permute-start(bf16[512,512]{1,0:T(8,128)(2,1)S(1)} %collective-permute-done.20.left), channel_id=1, source_target_pairs={{0,8},{32,34},{64,72},{96,98},{1,9},{33,35},{65,73},{97,99},{8,16}... | collective-permute-start | bytes 1572872 | tf_op jit(solution)/shard_map/ppermute | solution.py:32
  117.0 8.9 %collective-permute-start.24 = (bf16[512,512]{1,0:T(8,128)(2,1)S(1)}, bf16[512,512]{1,0:T(8,128)(2,1)S(1)}, u32[]{:S(2)}, u32[]{:S(2)}) collective-permute-start(bf16[512,512]{1,0:T(8,128)(2,1)S(1)} %collective-permute-done.21.right), channel_id=1, source_target_pairs={{0,24},{32,38},{64,88},{96,102},{1,25},{33,39},{65,89},{97,103},{8... | collective-permute-start | bytes 1572872 | tf_op jit(solution)/shard_map/ppermute | solution.py:32
  121.3 3.5 %collective-permute-start.29 = (f32[256,256]{1,0:T(8,128)S(1)}, f32[256,256]{1,0:T(8,128)S(1)}, u32[]{:S(2)}, u32[]{:S(2)}) collective-permute-start(f32[256,256]{1,0:T(8,128)S(1)} %get-tuple-element.77.mine), channel_id=1, source_target_pairs={{0,32},{32,0},{64,96},{96,64},{1,33},{33,1},{65,97},{97,65},{8,40}... | collective-permute-start | bytes 786440 | tf_op jit(solution)/shard_map/ppermute | solution.py:32
  126.0 3.0 %collective-permute-start.30 = (bf16[1024,512]{1,0:T(8,128)(2,1)S(1)}, bf16[1024,512]{1,0:T(8,128)(2,1)S(1)}, u32[]{:S(2)}, u32[]{:S(2)}) collective-permute-start(bf16[1024,512]{1,0:T(8,128)(2,1)S(1)} %shard_map.129.refs_0_), channel_id=1, source_target_pairs={{0,32},{32,0},{64,96},{96,64},{1,33},{33,1},{65,97},{97,65},{8,40}... | collective-permute-start | bytes 3145736 | tf_op jit(solution)/shard_map/ppermute | solution.py:32

commit v5 on v4

--- a/solution.py
+++ b/solution.py
@@ -368,19 +368,22 @@
     low_up, high_down = permute(low, second(1)), permute(high, second(-1))
     high_up, low_down = permute(high, second(1)), permute(low, second(-1))
     acc = project(held, 0, [near, permute(near, other_core)], None, None)
+    finished = finish(acc)
     low_up, high_down, acc = lax.optimization_barrier((low_up, high_down, acc))
     far_low, far_high = permute(low_up, second(1)), permute(high_down, second(-1))
-    wave = join(low_up, high_down)
-    acc = project(held, 2048, [wave, permute(wave, other_core)], acc, None)
-    finished = finish(acc)
-    wave = join(high_up, low_down)
-    acc = project(held, 4096, [wave, permute(wave, other_core)], acc, None)
+    wave_one = join(low_up, high_down)
+    acc = project(held, 2048, [wave_one], acc, None)
+    wave_two = join(high_up, low_down)
+    acc = project(held, 4096, [wave_two], acc, None)
     far_low, far_high, acc, new_global, new_momentum = lax.optimization_barrier(
         (far_low, far_high, acc, *finished)
     )
     wave = join(far_low, far_high)
+    waves = [permute(array, other_core) for array in (wave_one, wave_two)]
     theirs = permute(wave, other_core)
     acc = project(held, 6144, [wave], acc, None)
+    acc = project(held, 3072, waves[:1], acc, None)
+    acc = project(held, 5120, waves[1:], acc, None)
     return project(held, 7168, [theirs], acc, scale), new_global, new_momentum
 
 

time: 132 us -> 129 us (0.977)
  waiting for transfers between devices: 44.4 us -> 40.6 us
    ppermute x31, waiting for transfers between devices: 44.4 us -> 40.6 us  [permute(): return lax.ppermute(array, BOTH, pairs)]
    pallas_call x5 -> x7, Pallas kernels: 11.1 us -> 11.4 us  [project(): pl.pallas_call(functools.partial(project_kernel, start, bool(carried), sc...]
where the time goes in v5:
time: 129 us; the launch traced here: 128 us
  starting transfers between devices  45.8 us (36%)
  waiting for transfers between devices  40.6 us (31%)
  Pallas kernels  38.6 us (30%)
  local copies, waits for them, and re-layouts  2.4 us (2%)
    ppermute x31, starting transfers between devices, permute(): return lax.ppermute(array, BOTH, pairs)  45.8 us
    ppermute x31, waiting for transfers between devices, permute(): return lax.ppermute(array, BOTH, pairs)  40.6 us
    pallas_call x4, Pallas kernels, grad_blocks(): pl.pallas_call(functools.partial(grad_kernel, names, len(recv)), in_specs...  17.4 us
    pallas_call x7, Pallas kernels, project(): pl.pallas_call(functools.partial(project_kernel, start, bool(carried), sc...  11.4 us
    pallas_call x1, Pallas kernels, arrange(): pl.pallas_call(functools.partial(arrange_kernel, places), in_specs=[ANY],...  6.32 us
    pallas_call x12, Pallas kernels, local(): pl.pallas_call(kernel, in_specs=[VMEM] * len(arrays), out_specs=[VMEM] *...  3.52 us
  transfers between devices with their start and end apart: 31, of which 15 were waited for; matrix products, arithmetic and copies ran while one was open for 0% of the time, Pallas kernels for 23%

profile of v5, /device:TPU:1, one launch (start us, length us, event | category | flops | bytes accessed | tf_op | source)
XLA Modules:
  0.0 128.5 jit_solution(6694316941282025130)
XLA Ops:
  0.6 1.2 copy-done
  1.9 4.3 %shard_map.112 = (bf16[1024,512]{1,0:T(8,128)(2,1)S(1)}, bf16[1024,512]{1,0:T(8,128)(2,1)S(1)}) custom-call(bf16[1024,8192]{1,0:T(8,128)(2,1)} %tok_ref.8, bf16[1024,512]{1,0:T(8,128)(2,1)S(1)} %copy-done), custom_call_target="tpu_custom_call" | custom-call | flops 2147483648 | bytes 4194304 | tf_op jit(solution)/shard_map/pallas_call | solution.py:138
  6.2 2.2 %collective-permute-start.2 = (bf16[1024,512]{1,0:T(8,128)(2,1)S(1)}, bf16[1024,512]{1,0:T(8,128)(2,1)S(1)}, u32[]{:S(2)}, u32[]{:S(2)}) collective-permute-start(bf16[1024,512]{1,0:T(8,128)(2,1)S(1)} %get-tuple-element.49), channel_id=1, source_target_pairs={{0,2},{32,40},{64,66},{96,104},{1,3},{33,41},{65,67},{97,105},{8,1... | collective-permute-start | bytes 3145736 | tf_op jit(solution)/shard_map/ppermute | solution.py:32
  8.4 1.5 %collective-permute-start.3 = (bf16[1024,512]{1,0:T(8,128)(2,1)S(1)}, bf16[1024,512]{1,0:T(8,128)(2,1)S(1)}, u32[]{:S(2)}, u32[]{:S(2)}) collective-permute-start(bf16[1024,512]{1,0:T(8,128)(2,1)S(1)} %get-tuple-element.50), channel_id=1, source_target_pairs={{0,6},{32,56},{64,70},{96,120},{1,7},{33,57},{65,71},{97,121},{8,1... | collective-permute-start | bytes 3145736 | tf_op jit(solution)/shard_map/ppermute | solution.py:32
  9.9 4.3 %shard_map.110 = (bf16[1024,512]{1,0:T(8,128)(2,1)S(1)}, bf16[1024,512]{1,0:T(8,128)(2,1)S(1)}) custom-call(bf16[1024,8192]{1,0:T(8,128)(2,1)} %tok_ref.8, bf16[1024,512]{1,0:T(8,128)(2,1)S(1)} %copy-done), custom_call_target="tpu_custom_call" | custom-call | flops 2147483648 | bytes 4194304 | tf_op jit(solution)/shard_map/pallas_call | solution.py:138
  14.3 1.5 %collective-permute-start = (bf16[1024,512]{1,0:T(8,128)(2,1)S(1)}, bf16[1024,512]{1,0:T(8,128)(2,1)S(1)}, u32[]{:S(2)}, u32[]{:S(2)}) collective-permute-start(bf16[1024,512]{1,0:T(8,128)(2,1)S(1)} %get-tuple-element.45), channel_id=1, source_target_pairs={{0,6},{32,56},{64,70},{96,120},{1,7},{33,57},{65,71},{97,121},{8,1... | collective-permute-start | bytes 3145736 | tf_op jit(solution)/shard_map/ppermute | solution.py:32
  15.8 6.5 %collective-permute-done.2.refs_0_ = bf16[1024,512]{1,0:T(8,128)(2,1)S(1)} collective-permute-done((bf16[1024,512]{1,0:T(8,128)(2,1)S(1)}, bf16[1024,512]{1,0:T(8,128)(2,1)S(1)}, u32[]{:S(2)}, u32[]{:S(2)}) %collective-permute-start.2) | collective-permute-done | bytes 1048608 | tf_op jit(solution)/shard_map/ppermute | solution.py:32
  22.4 4.4 %shard_map.113 = (bf16[1024,512]{1,0:T(8,128)(2,1)S(1)}, bf16[1024,512]{1,0:T(8,128)(2,1)S(1)}) custom-call(bf16[1024,8192]{1,0:T(8,128)(2,1)} %tok_ref.8, bf16[1024,512]{1,0:T(8,128)(2,1)S(1)} %copy-done.1, bf16[1024,512]{1,0:T(8,128)(2,1)S(1)} %collective-permute-done.2.refs_0_, bf16[1024,512]{1,0:T(8,128)(2,1)S(1)} %collective-permute-done.3.refs_1_), custom_call_target="tpu_custom_call" | custom-call | flops 2147483648 | bytes 4194304 | tf_op jit(solution)/shard_map/pallas_call | solution.py:138
  26.7 1.4 %collective-permute-start.4 = (bf16[1024,512]{1,0:T(8,128)(2,1)S(1)}, bf16[1024,512]{1,0:T(8,128)(2,1)S(1)}, u32[]{:S(2)}, u32[]{:S(2)}) collective-permute-start(bf16[1024,512]{1,0:T(8,128)(2,1)S(1)} %get-tuple-element.51), channel_id=1, source_target_pairs={{0,2},{32,40},{64,66},{96,104},{1,3},{33,41},{65,67},{97,105},{8,1... | collective-permute-start | bytes 3145736 | tf_op jit(solution)/shard_map/ppermute | solution.py:32
  28.1 1.5 %collective-permute-start.5 = (bf16[1024,512]{1,0:T(8,128)(2,1)S(1)}, bf16[1024,512]{1,0:T(8,128)(2,1)S(1)}, u32[]{:S(2)}, u32[]{:S(2)}) collective-permute-start(bf16[1024,512]{1,0:T(8,128)(2,1)S(1)} %get-tuple-element.52), channel_id=1, source_target_pairs={{0,6},{32,56},{64,70},{96,120},{1,7},{33,57},{65,71},{97,121},{8,1... | collective-permute-start | bytes 3145736 | tf_op jit(solution)/shard_map/ppermute | solution.py:32
  29.6 4.0 %collective-permute-done.refs_0_ = bf16[1024,512]{1,0:T(8,128)(2,1)S(1)} collective-permute-done((bf16[1024,512]{1,0:T(8,128)(2,1)S(1)}, bf16[1024,512]{1,0:T(8,128)(2,1)S(1)}, u32[]{:S(2)}, u32[]{:S(2)}) %collective-permute-start) | collective-permute-done | bytes 1048608 | tf_op jit(solution)/shard_map/ppermute | solution.py:32
  33.6 4.3 %shard_map.111 = (f32[1024,512]{1,0:T(8,128)S(1)}, f32[1024,512]{1,0:T(8,128)S(1)}) custom-call(bf16[1024,8192]{1,0:T(8,128)(2,1)} %tok_ref.8, bf16[1024,512]{1,0:T(8,128)(2,1)S(1)} %copy-done.1, bf16[1024,512]{1,0:T(8,128)(2,1)S(1)} %collective-permute-done.refs_0_, bf16[1024,512]{1,0:T(8,128)(2,1)S(1)} %collective-permute-done.1.refs_1_), custom_call_target="tpu_custom_call" | custom-call | flops 2147483648 | bytes 4194304 | tf_op jit(solution)/shard_map/pallas_call | solution.py:138
  37.9 6.9 %collective-permute-done.4.got1 = bf16[1024,512]{1,0:T(8,128)(2,1)S(1)} collective-permute-done((bf16[1024,512]{1,0:T(8,128)(2,1)S(1)}, bf16[1024,512]{1,0:T(8,128)(2,1)S(1)}, u32[]{:S(2)}, u32[]{:S(2)}) %collective-permute-start.4) | collective-permute-done | bytes 1048608 | tf_op jit(solution)/shard_map/ppermute | solution.py:32
  44.8 0.3 shard_map.114
  45.2 1.3 collective-permute-start.10
  46.4 1.5 %collective-permute-start.11 = (bf16[256,512]{1,0:T(8,128)(2,1)S(1)}, bf16[256,512]{1,0:T(8,128)(2,1)S(1)}, u32[]{:S(2)}, u32[]{:S(2)}) collective-permute-start(bf16[256,512]{1,0:T(8,128)(2,1)S(1)} %get-tuple-element.60), channel_id=1, source_target_pairs={{0,24},{32,38},{64,88},{96,102},{1,25},{33,39},{65,89},{97,103},{8... | collective-permute-start | bytes 786440 | tf_op jit(solution)/shard_map/ppermute | solution.py:32
  47.9 1.5 %collective-permute-start.9 = (bf16[256,512]{1,0:T(8,128)(2,1)S(1)}, bf16[256,512]{1,0:T(8,128)(2,1)S(1)}, u32[]{:S(2)}, u32[]{:S(2)}) collective-permute-start(bf16[256,512]{1,0:T(8,128)(2,1)S(1)} %get-tuple-element.58), channel_id=1, source_target_pairs={{0,16},{32,36},{64,80},{96,100},{1,17},{33,37},{65,81},{97,101},{8... | collective-permute-start | bytes 786440 | tf_op jit(solution)/shard_map/ppermute | solution.py:32
  49.4 1.4 %collective-permute-start.6 = (bf16[256,512]{1,0:T(8,128)(2,1)S(1)}, bf16[256,512]{1,0:T(8,128)(2,1)S(1)}, u32[]{:S(2)}, u32[]{:S(2)}) collective-permute-start(bf16[256,512]{1,0:T(8,128)(2,1)S(1)} %get-tuple-element.54), channel_id=1, source_target_pairs={{0,16},{32,36},{64,80},{96,100},{1,17},{33,37},{65,81},{97,101},{8... | collective-permute-start | bytes 786440 | tf_op jit(solution)/shard_map/ppermute | solution.py:32
  50.9 1.1 collective-permute-done.10.refs_1_
  52.0 1.6 %collective-permute-start.8 = (bf16[256,512]{1,0:T(8,128)(2,1)S(1)}, bf16[256,512]{1,0:T(8,128)(2,1)S(1)}, u32[]{:S(2)}, u32[]{:S(2)}) collective-permute-start(bf16[256,512]{1,0:T(8,128)(2,1)S(1)} %get-tuple-element.56), channel_id=1, source_target_pairs={{0,24},{32,38},{64,88},{96,102},{1,25},{33,39},{65,89},{97,103},{8... | collective-permute-start | bytes 786440 | tf_op jit(solution)/shard_map/ppermute | solution.py:32
  53.6 2.2 %collective-permute-done.9.refs_0_ = bf16[256,512]{1,0:T(8,128)(2,1)S(1)} collective-permute-done((bf16[256,512]{1,0:T(8,128)(2,1)S(1)}, bf16[256,512]{1,0:T(8,128)(2,1)S(1)}, u32[]{:S(2)}, u32[]{:S(2)}) %collective-permute-start.9) | collective-permute-done | bytes 262176 | tf_op jit(solution)/shard_map/ppermute | solution.py:32
  55.8 0.1 shard_map.116
  55.9 3.7 %collective-permute-start.12 = (bf16[256,512]{1,0:T(8,128)(2,1)S(1)}, bf16[256,512]{1,0:T(8,128)(2,1)S(1)}, u32[]{:S(2)}, u32[]{:S(2)}) collective-permute-start(bf16[256,512]{1,0:T(8,128)(2,1)S(1)} %shard_map.116), channel_id=1, source_target_pairs={{0,1},{32,33},{64,65},{96,97},{1,0},{33,32},{65,64},{97,96},{8,9},... | collective-permute-start | bytes 786440 | tf_op jit(solution)/shard_map/ppermute | solution.py:32
  59.5 6.3 %shard_map.117.held = bf16[1024,8192]{1,0:T(8,128)(2,1)S(1)} custom-call(bf16[1024,8192]{1,0:T(8,128)(2,1)} %tok_ref.8), custom_call_target="tpu_custom_call" | custom-call | flops 1 | bytes 1 | tf_op jit(solution)/shard_map/pallas_call | solution.py:288
  66.0 0.1 shard_map.115.keep
  66.1 0.8 copy-done.4
  66.9 0.2 copy-done.5
  67.1 0.2 copy-done.6
  67.2 1.3 %shard_map.118 = (f32[256,512]{1,0:T(8,128)}, f32[256,512]{1,0:T(8,128)}, f32[256,256]{1,0:T(8,128)S(1)}, f32[256,256]{1,0:T(8,128)S(1)}) custom-call(f32[256,512]{1,0:T(8,128)S(1)} %shard_map.115.keep, bf16[256,512]{1,0:T(8,128)(2,1)S(1)} %collective-permute-done.12.got, f32[256,512]{1,0:T(8,128)S(1)} %bitcast.5, f32[256,512]{1,0:T(8,128)S(1)} %bitcast.6, ...), custom_call_target="tpu_custom_call" | custom-call | tf_op jit(solution)/shard_map/pallas_call | solution.py:79
  68.5 3.1 %collective-permute-start.13 = (f32[256,256]{1,0:T(8,128)S(1)}, f32[256,256]{1,0:T(8,128)S(1)}, u32[]{:S(2)}, u32[]{:S(2)}) collective-permute-start(f32[256,256]{1,0:T(8,128)S(1)} %get-tuple-element.67), channel_id=1, source_target_pairs={{0,32},{32,0},{64,96},{96,64},{1,33},{33,1},{65,97},{97,65},{8,40}... | collective-permute-start | bytes 786440 | tf_op jit(solution)/shard_map/ppermute | solution.py:32
  71.7 1.2 collective-permute-done.13.right
  72.8 0.8 collective-permute-start.14
  73.7 4.0 %collective-permute-done.14.right = bf16[256,256]{1,0:T(8,128)(2,1)S(1)} collective-permute-done((bf16[256,256]{1,0:T(8,128)(2,1)S(1)}, bf16[256,256]{1,0:T(8,128)(2,1)S(1)}, u32[]{:S(2)}, u32[]{:S(2)}) %collective-permute-start.14) | collective-permute-done | bytes 131104 | tf_op jit(solution)/shard_map/ppermute | solution.py:32
  77.6 0.1 shard_map.120
  77.8 1.3 collective-permute-start.15
  79.1 2.2 %collective-permute-start.16 = (bf16[256,256]{1,0:T(8,128)(2,1)S(1)}, bf16[256,256]{1,0:T(8,128)(2,1)S(1)}, u32[]{:S(2)}, u32[]{:S(2)}) collective-permute-start(bf16[256,256]{1,0:T(8,128)(2,1)S(1)} %get-tuple-element.68.mine), channel_id=1, source_target_pairs={{32,65},{96,1},{1,96},{65,32},{40,73},{104,9},{9,104},{73,40},{48,... | collective-permute-start | bytes 393224 | tf_op jit(solution)/shard_map/ppermute | solution.py:32
  81.3 1.6 %collective-permute-done.15.one = bf16[256,256]{1,0:T(8,128)(2,1)S(1)} collective-permute-done((bf16[256,256]{1,0:T(8,128)(2,1)S(1)}, bf16[256,256]{1,0:T(8,128)(2,1)S(1)}, u32[]{:S(2)}, u32[]{:S(2)}) %collective-permute-start.15) | collective-permute-done | bytes 131104 | tf_op jit(solution)/shard_map/ppermute | solution.py:32
  82.9 3.7 %collective-permute-done.16.two = bf16[256,256]{1,0:T(8,128)(2,1)S(1)} collective-permute-done((bf16[256,256]{1,0:T(8,128)(2,1)S(1)}, bf16[256,256]{1,0:T(8,128)(2,1)S(1)}, u32[]{:S(2)}, u32[]{:S(2)}) %collective-permute-start.16) | collective-permute-done | bytes 131104 | tf_op jit(solution)/shard_map/ppermute | solution.py:32
  86.6 1.3 %collective-permute-start.17 = (bf16[256,512]{1,0:T(8,128)(2,1)S(1)}, bf16[256,512]{1,0:T(8,128)(2,1)S(1)}, u32[]{:S(2)}, u32[]{:S(2)}) collective-permute-start(bf16[256,512]{1,0:T(8,128)(2,1)S(1)} %shard_map.121.refs_0_), channel_id=1, source_target_pairs={{0,2},{32,40},{64,66},{96,104},{1,3},{33,41},{65,67},{97,105},{8,1... | collective-permute-start | bytes 786440 | tf_op jit(solution)/shard_map/ppermute | solution.py:32
  87.9 3.7 %collective-permute-start.18 = (bf16[256,512]{1,0:T(8,128)(2,1)S(1)}, bf16[256,512]{1,0:T(8,128)(2,1)S(1)}, u32[]{:S(2)}, u32[]{:S(2)}) collective-permute-start(bf16[256,512]{1,0:T(8,128)(2,1)S(1)} %shard_map.121.refs_0_), channel_id=1, source_target_pairs={{0,6},{32,56},{64,70},{96,120},{1,7},{33,57},{65,71},{97,121},{8,1... | collective-permute-start | bytes 786440 | tf_op jit(solution)/shard_map/ppermute | solution.py:32
  91.6 1.1 collective-permute-start.19
  92.7 2.6 %collective-permute-done.17.refs_1_ = bf16[256,512]{1,0:T(8,128)(2,1)S(1)} collective-permute-done((bf16[256,512]{1,0:T(8,128)(2,1)S(1)}, bf16[256,512]{1,0:T(8,128)(2,1)S(1)}, u32[]{:S(2)}, u32[]{:S(2)}) %collective-permute-start.17) | collective-permute-done | bytes 262176 | tf_op jit(solution)/shard_map/ppermute | solution.py:32
  95.2 2.4 %collective-permute-done.18.refs_2_ = bf16[256,512]{1,0:T(8,128)(2,1)S(1)} collective-permute-done((bf16[256,512]{1,0:T(8,128)(2,1)S(1)}, bf16[256,512]{1,0:T(8,128)(2,1)S(1)}, u32[]{:S(2)}, u32[]{:S(2)}) %collective-permute-start.18) | collective-permute-done | bytes 262176 | tf_op jit(solution)/shard_map/ppermute | solution.py:32
  97.7 1.5 %collective-permute-done.19.refs_3_ = bf16[256,512]{1,0:T(8,128)(2,1)S(1)} collective-permute-done((bf16[256,512]{1,0:T(8,128)(2,1)S(1)}, bf16[256,512]{1,0:T(8,128)(2,1)S(1)}, u32[]{:S(2)}, u32[]{:S(2)}) %collective-permute-start.19) | collective-permute-done | bytes 262176 | tf_op jit(solution)/shard_map/ppermute | solution.py:32
  99.2 0.1 shard_map.122
  99.5 1.0 collective-permute-start.20
  100.4 1.8 %collective-permute-start.21 = (bf16[512,512]{1,0:T(8,128)(2,1)S(1)}, bf16[512,512]{1,0:T(8,128)(2,1)S(1)}, u32[]{:S(2)}, u32[]{:S(2)}) collective-permute-start(bf16[512,512]{1,0:T(8,128)(2,1)S(1)} %get-tuple-element.70), channel_id=1, source_target_pairs={{0,24},{32,38},{64,88},{96,102},{1,25},{33,39},{65,89},{97,103},{8... | collective-permute-start | bytes 1572872 | tf_op jit(solution)/shard_map/ppermute | solution.py:32
  102.2 2.7 %collective-permute-start.26 = (bf16[512,512]{1,0:T(8,128)(2,1)S(1)}, bf16[512,512]{1,0:T(8,128)(2,1)S(1)}, u32[]{:S(2)}, u32[]{:S(2)}) collective-permute-start(bf16[512,512]{1,0:T(8,128)(2,1)S(1)} %get-tuple-element.69), channel_id=1, source_target_pairs={{0,24},{32,38},{64,88},{96,102},{1,25},{33,39},{65,89},{97,103},{8... | collective-permute-start | bytes 1572872 | tf_op jit(solution)/shard_map/ppermute | solution.py:32
  104.9 2.5 %shard_map.123.refs_1_ = f32[1024,512]{1,0:T(8,128)S(1)} custom-call(bf16[1024,8192]{1,0:T(8,128)(2,1)S(1)} %shard_map.117.held, bf16[1024,512]{1,0:T(8,128)(2,1)S(1)} %get-tuple-element.72.refs_0_, bf16[1024,512]{1,0:T(8,128)(2,1)S(1)} %collective-permute-done.22.refs_1_), custom_call_target="tpu_custom_call" | custom-call | flops 1 | bytes 1 | tf_op jit(solution)/shard_map/pallas_call | solution.py:319
  107.4 1.7 %collective-permute-done.20.left = bf16[512,512]{1,0:T(8,128)(2,1)S(1)} collective-permute-done((bf16[512,512]{1,0:T(8,128)(2,1)S(1)}, bf16[512,512]{1,0:T(8,128)(2,1)S(1)}, u32[]{:S(2)}, u32[]{:S(2)}) %collective-permute-start.20) | collective-permute-done | bytes 524320 | tf_op jit(solution)/shard_map/ppermute | solution.py:32
  109.1 0.6 collective-permute-start.23
  109.7 2.0 %collective-permute-start.24 = (bf16[512,512]{1,0:T(8,128)(2,1)S(1)}, bf16[512,512]{1,0:T(8,128)(2,1)S(1)}, u32[]{:S(2)}, u32[]{:S(2)}) collective-permute-start(bf16[512,512]{1,0:T(8,128)(2,1)S(1)} %collective-permute-done.21.right), channel_id=1, source_target_pairs={{0,24},{32,38},{64,88},{96,102},{1,25},{33,39},{65,89},{97,103},{8... | collective-permute-start | bytes 1572872 | tf_op jit(solution)/shard_map/ppermute | solution.py:32
  111.7 1.8 %collective-permute-start.27 = (f32[256,256]{1,0:T(8,128)S(1)}, f32[256,256]{1,0:T(8,128)S(1)}, u32[]{:S(2)}, u32[]{:S(2)}) collective-permute-start(f32[256,256]{1,0:T(8,128)S(1)} %get-tuple-element.77.mine), channel_id=1, source_target_pairs={{0,32},{32,0},{64,96},{96,64},{1,33},{33,1},{65,97},{97,65},{8,40}... | collective-permute-start | bytes 786440 | tf_op jit(solution)/shard_map/ppermute | solution.py:32
  113.6 1.1 collective-permute-done.25.left
  114.8 1.4 %collective-permute-start.29 = (bf16[1024,512]{1,0:T(8,128)(2,1)S(1)}, bf16[1024,512]{1,0:T(8,128)(2,1)S(1)}, u32[]{:S(2)}, u32[]{:S(2)}) collective-permute-start(bf16[1024,512]{1,0:T(8,128)(2,1)S(1)} %shard_map.124.refs_0_), channel_id=1, source_target_pairs={{0,32},{32,0},{64,96},{96,64},{1,33},{33,1},{65,97},{97,65},{8,40}... | collective-permute-start | bytes 3145736 | tf_op jit(solution)/shard_map/ppermute | solution.py:32
  116.2 1.3 %shard_map.126.refs_1_ = f32[1024,512]{1,0:T(8,128)S(1)} custom-call(bf16[1024,8192]{1,0:T(8,128)(2,1)S(1)} %shard_map.117.held, bf16[1024,512]{1,0:T(8,128)(2,1)S(1)} %shard_map.125.refs_0_, f32[1024,512]{1,0:T(8,128)S(1)} %shard_map.123.refs_1_), custom_call_target="tpu_custom_call" | custom-call | flops 1 | bytes 1 | tf_op jit(solution)/shard_map/pallas_call | solution.py:319
  117.6 1.3 %shard_map.127.refs_1_ = f32[1024,512]{1,0:T(8,128)S(1)} custom-call(bf16[1024,8192]{1,0:T(8,128)(2,1)S(1)} %shard_map.117.held, bf16[1024,512]{1,0:T(8,128)(2,1)S(1)} %shard_map.124.refs_0_, f32[1024,512]{1,0:T(8,128)S(1)} %shard_map.126.refs_1_), custom_call_target="tpu_custom_call" | custom-call | flops 1 | bytes 1 | tf_op jit(solution)/shard_map/pallas_call | solution.py:319
  119.0 1.1 shard_map.128
  120.1 0.2 collective-permute-done.23.left
  120.4 1.6 %collective-permute-start.28 = (bf16[1024,512]{1,0:T(8,128)(2,1)S(1)}, bf16[1024,512]{1,0:T(8,128)(2,1)S(1)}, u32[]{:S(2)}, u32[]{:S(2)}) collective-permute-start(bf16[1024,512]{1,0:T(8,128)(2,1)S(1)} %shard_map.129.refs_0_), channel_id=1, source_target_pairs={{0,32},{32,0},{64,96},{96,64},{1,33},{33,1},{65,97},{97,65},{8,40}... | collective-permute-start | bytes 3145736 | tf_op jit(solution)/shard_map/ppermute | solution.py:32
  122.0 1.3 %shard_map.130.refs_1_ = f32[1024,512]{1,0:T(8,128)S(1)} custom-call(bf16[1024,8192]{1,0:T(8,128)(2,1)S(1)} %shard_map.117.held, bf16[1024,512]{1,0:T(8,128)(2,1)S(1)} %shard_map.129.refs_0_, f32[1024,512]{1,0:T(8,128)S(1)} %shard_map.127.refs_1_), custom_call_target="tpu_custom_call" | custom-call | flops 1 | bytes 1 | tf_op jit(solution)/shard_map/pallas_call | solution.py:319
  123.3 1.3 %shard_map.131.refs_1_ = f32[1024,512]{1,0:T(8,128)S(1)} custom-call(bf16[1024,8192]{1,0:T(8,128)(2,1)S(1)} %shard_map.117.held, bf16[1024,512]{1,0:T(8,128)(2,1)S(1)} %collective-permute-done.30.refs_0_, f32[1024,512]{1,0:T(8,128)S(1)} %shard_map.130.refs_1_), custom_call_target="tpu_custom_call" | custom-call | flops 1 | bytes 1 | tf_op jit(solution)/shard_map/pallas_call | solution.py:319
  124.6 1.3 %shard_map.132.refs_1_ = f32[1024,512]{1,0:T(8,128)S(1)} custom-call(bf16[1024,8192]{1,0:T(8,128)(2,1)S(1)} %shard_map.117.held, bf16[1024,512]{1,0:T(8,128)(2,1)S(1)} %collective-permute-done.29.refs_0_, f32[1024,512]{1,0:T(8,128)S(1)} %shard_map.131.refs_1_), custom_call_target="tpu_custom_call" | custom-call | flops 1 | bytes 1 | tf_op jit(solution)/shard_map/pallas_call | solution.py:319
  126.0 2.3 %shard_map.133 = bf16[1024,512]{1,0:T(8,128)(2,1)} custom-call(bf16[1024,8192]{1,0:T(8,128)(2,1)S(1)} %shard_map.117.held, bf16[1024,512]{1,0:T(8,128)(2,1)S(1)} %collective-permute-done.28.refs_0_, f32[1024,512]{1,0:T(8,128)S(1)} %shard_map.132.refs_1_), custom_call_target="tpu_custom_call" | custom-call | flops 1 | bytes 1 | tf_op jit(solution)/shard_map/pallas_call | solution.py:319
  (36 shorter events, 0.6 us)
Async XLA Ops:
  0.6 1.2 copy-start
  6.2 16.1 %collective-permute-start.2 = (bf16[1024,512]{1,0:T(8,128)(2,1)S(1)}, bf16[1024,512]{1,0:T(8,128)(2,1)S(1)}, u32[]{:S(2)}, u32[]{:S(2)}) collective-permute-start(bf16[1024,512]{1,0:T(8,128)(2,1)S(1)} %get-tuple-element.49), channel_id=1, source_target_pairs={{0,2},{32,40},{64,66},{96,104},{1,3},{33,41},{65,67},{97,105},{8,1... | collective-permute-start | bytes 3145736 | tf_op jit(solution)/shard_map/ppermute | solution.py:32
  8.4 13.9 %copy-start.1 = (bf16[1024,512]{1,0:T(8,128)(2,1)S(1)}, bf16[1024,512]{1,0:T(8,128)(2,1)}, u32[]{:S(2)}) copy-start(bf16[1024,512]{1,0:T(8,128)(2,1)} %grad_ref.7) | copy-start | bytes 3145732
  8.4 13.9 %collective-permute-start.3 = (bf16[1024,512]{1,0:T(8,128)(2,1)S(1)}, bf16[1024,512]{1,0:T(8,128)(2,1)S(1)}, u32[]{:S(2)}, u32[]{:S(2)}) collective-permute-start(bf16[1024,512]{1,0:T(8,128)(2,1)S(1)} %get-tuple-element.50), channel_id=1, source_target_pairs={{0,6},{32,56},{64,70},{96,120},{1,7},{33,57},{65,71},{97,121},{8,1... | collective-permute-start | bytes 3145736 | tf_op jit(solution)/shard_map/ppermute | solution.py:32
  14.3 19.3 %collective-permute-start = (bf16[1024,512]{1,0:T(8,128)(2,1)S(1)}, bf16[1024,512]{1,0:T(8,128)(2,1)S(1)}, u32[]{:S(2)}, u32[]{:S(2)}) collective-permute-start(bf16[1024,512]{1,0:T(8,128)(2,1)S(1)} %get-tuple-element.45), channel_id=1, source_target_pairs={{0,6},{32,56},{64,70},{96,120},{1,7},{33,57},{65,71},{97,121},{8,1... | collective-permute-start | bytes 3145736 | tf_op jit(solution)/shard_map/ppermute | solution.py:32
  15.7 17.8 %collective-permute-start.1 = (bf16[1024,512]{1,0:T(8,128)(2,1)S(1)}, bf16[1024,512]{1,0:T(8,128)(2,1)S(1)}, u32[]{:S(2)}, u32[]{:S(2)}) collective-permute-start(bf16[1024,512]{1,0:T(8,128)(2,1)S(1)} %get-tuple-element.46), channel_id=1, source_target_pairs={{0,2},{32,40},{64,66},{96,104},{1,3},{33,41},{65,67},{97,105},{8,1... | collective-permute-start | bytes 3145736 | tf_op jit(solution)/shard_map/ppermute | solution.py:32
  26.7 18.1 %collective-permute-start.4 = (bf16[1024,512]{1,0:T(8,128)(2,1)S(1)}, bf16[1024,512]{1,0:T(8,128)(2,1)S(1)}, u32[]{:S(2)}, u32[]{:S(2)}) collective-permute-start(bf16[1024,512]{1,0:T(8,128)(2,1)S(1)} %get-tuple-element.51), channel_id=1, source_target_pairs={{0,2},{32,40},{64,66},{96,104},{1,3},{33,41},{65,67},{97,105},{8,1... | collective-permute-start | bytes 3145736 | tf_op jit(solution)/shard_map/ppermute | solution.py:32
  28.1 16.7 %collective-permute-start.5 = (bf16[1024,512]{1,0:T(8,128)(2,1)S(1)}, bf16[1024,512]{1,0:T(8,128)(2,1)S(1)}, u32[]{:S(2)}, u32[]{:S(2)}) collective-permute-start(bf16[1024,512]{1,0:T(8,128)(2,1)S(1)} %get-tuple-element.52), channel_id=1, source_target_pairs={{0,6},{32,56},{64,70},{96,120},{1,7},{33,57},{65,71},{97,121},{8,1... | collective-permute-start | bytes 3145736 | tf_op jit(solution)/shard_map/ppermute | solution.py:32
  45.2 6.8 %collective-permute-start.10 = (bf16[256,512]{1,0:T(8,128)(2,1)S(1)}, bf16[256,512]{1,0:T(8,128)(2,1)S(1)}, u32[]{:S(2)}, u32[]{:S(2)}) collective-permute-start(bf16[256,512]{1,0:T(8,128)(2,1)S(1)} %get-tuple-element.59), channel_id=1, source_target_pairs={{0,8},{32,34},{64,72},{96,98},{1,9},{33,35},{65,73},{97,99},{8,16}... | collective-permute-start | bytes 786440 | tf_op jit(solution)/shard_map/ppermute | solution.py:32
  46.4 7.1 %collective-permute-start.11 = (bf16[256,512]{1,0:T(8,128)(2,1)S(1)}, bf16[256,512]{1,0:T(8,128)(2,1)S(1)}, u32[]{:S(2)}, u32[]{:S(2)}) collective-permute-start(bf16[256,512]{1,0:T(8,128)(2,1)S(1)} %get-tuple-element.60), channel_id=1, source_target_pairs={{0,24},{32,38},{64,88},{96,102},{1,25},{33,39},{65,89},{97,103},{8... | collective-permute-start | bytes 786440 | tf_op jit(solution)/shard_map/ppermute | solution.py:32
  47.9 7.9 %collective-permute-start.9 = (bf16[256,512]{1,0:T(8,128)(2,1)S(1)}, bf16[256,512]{1,0:T(8,128)(2,1)S(1)}, u32[]{:S(2)}, u32[]{:S(2)}) collective-permute-start(bf16[256,512]{1,0:T(8,128)(2,1)S(1)} %get-tuple-element.58), channel_id=1, source_target_pairs={{0,16},{32,36},{64,80},{96,100},{1,17},{33,37},{65,81},{97,101},{8... | collective-permute-start | bytes 786440 | tf_op jit(solution)/shard_map/ppermute | solution.py:32
  49.4 16.5 %collective-permute-start.6 = (bf16[256,512]{1,0:T(8,128)(2,1)S(1)}, bf16[256,512]{1,0:T(8,128)(2,1)S(1)}, u32[]{:S(2)}, u32[]{:S(2)}) collective-permute-start(bf16[256,512]{1,0:T(8,128)(2,1)S(1)} %get-tuple-element.54), channel_id=1, source_target_pairs={{0,16},{32,36},{64,80},{96,100},{1,17},{33,37},{65,81},{97,101},{8... | collective-permute-start | bytes 786440 | tf_op jit(solution)/shard_map/ppermute | solution.py:32
  50.9 15.0 %collective-permute-start.7 = (bf16[256,512]{1,0:T(8,128)(2,1)S(1)}, bf16[256,512]{1,0:T(8,128)(2,1)S(1)}, u32[]{:S(2)}, u32[]{:S(2)}) collective-permute-start(bf16[256,512]{1,0:T(8,128)(2,1)S(1)} %get-tuple-element.55), channel_id=1, source_target_pairs={{0,8},{32,34},{64,72},{96,98},{1,9},{33,35},{65,73},{97,99},{8,16}... | collective-permute-start | bytes 786440 | tf_op jit(solution)/shard_map/ppermute | solution.py:32
  52.0 14.0 %collective-permute-start.8 = (bf16[256,512]{1,0:T(8,128)(2,1)S(1)}, bf16[256,512]{1,0:T(8,128)(2,1)S(1)}, u32[]{:S(2)}, u32[]{:S(2)}) collective-permute-start(bf16[256,512]{1,0:T(8,128)(2,1)S(1)} %get-tuple-element.56), channel_id=1, source_target_pairs={{0,24},{32,38},{64,88},{96,102},{1,25},{33,39},{65,89},{97,103},{8... | collective-permute-start | bytes 786440 | tf_op jit(solution)/shard_map/ppermute | solution.py:32
  55.9 10.2 %collective-permute-start.12 = (bf16[256,512]{1,0:T(8,128)(2,1)S(1)}, bf16[256,512]{1,0:T(8,128)(2,1)S(1)}, u32[]{:S(2)}, u32[]{:S(2)}) collective-permute-start(bf16[256,512]{1,0:T(8,128)(2,1)S(1)} %shard_map.116), channel_id=1, source_target_pairs={{0,1},{32,33},{64,65},{96,97},{1,0},{33,32},{65,64},{97,96},{8,9},... | collective-permute-start | bytes 786440 | tf_op jit(solution)/shard_map/ppermute | solution.py:32
  65.9 1.0 copy-start.4
  65.9 1.2 copy-start.5
  65.9 1.3 %copy-start.6 = (f32[1,256,512]{2,1,0:T(8,128)S(1)}, f32[1,256,512]{2,1,0:T(8,128)}, u32[]{:S(2)}) copy-start(f32[1,256,512]{2,1,0:T(8,128)} %param.11) | copy-start | bytes 1572868
  65.9 11.7 %copy-start.2 = (f32[256,512]{1,0:T(8,128)S(1)}, f32[256,512]{1,0:T(8,128)}, u32[]{:S(2)}) copy-start(f32[256,512]{1,0:T(8,128)} %weights_ref.3) | copy-start | bytes 1572868
  65.9 11.7 %copy-start.3 = (f32[256,512]{1,0:T(8,128)S(1)}, f32[256,512]{1,0:T(8,128)}, u32[]{:S(2)}) copy-start(f32[256,512]{1,0:T(8,128)} %momentum_ref.3) | copy-start | bytes 1572868
  68.5 4.3 %collective-permute-start.13 = (f32[256,256]{1,0:T(8,128)S(1)}, f32[256,256]{1,0:T(8,128)S(1)}, u32[]{:S(2)}, u32[]{:S(2)}) collective-permute-start(f32[256,256]{1,0:T(8,128)S(1)} %get-tuple-element.67), channel_id=1, source_target_pairs={{0,32},{32,0},{64,96},{96,64},{1,33},{33,1},{65,97},{97,65},{8,40}... | collective-permute-start | bytes 786440 | tf_op jit(solution)/shard_map/ppermute | solution.py:32
  72.8 4.8 %collective-permute-start.14 = (bf16[256,256]{1,0:T(8,128)(2,1)S(1)}, bf16[256,256]{1,0:T(8,128)(2,1)S(1)}, u32[]{:S(2)}, u32[]{:S(2)}) collective-permute-start(bf16[256,256]{1,0:T(8,128)(2,1)S(1)} %shard_map.119.left), channel_id=1, source_target_pairs={{0,64},{32,96},{64,0},{96,32},{1,65},{33,97},{65,1},{97,33},{8,72}... | collective-permute-start | bytes 393224 | tf_op jit(solution)/shard_map/ppermute | solution.py:32
  77.8 5.1 %collective-permute-start.15 = (bf16[256,256]{1,0:T(8,128)(2,1)S(1)}, bf16[256,256]{1,0:T(8,128)(2,1)S(1)}, u32[]{:S(2)}, u32[]{:S(2)}) collective-permute-start(bf16[256,256]{1,0:T(8,128)(2,1)S(1)} %get-tuple-element.68.mine), channel_id=1, source_target_pairs={{0,65},{32,0},{64,1},{96,64},{1,33},{33,96},{65,97},{97,32},{8,73}... | collective-permute-start | bytes 393224 | tf_op jit(solution)/shard_map/ppermute | solution.py:32
  79.1 7.5 %collective-permute-start.16 = (bf16[256,256]{1,0:T(8,128)(2,1)S(1)}, bf16[256,256]{1,0:T(8,128)(2,1)S(1)}, u32[]{:S(2)}, u32[]{:S(2)}) collective-permute-start(bf16[256,256]{1,0:T(8,128)(2,1)S(1)} %get-tuple-element.68.mine), channel_id=1, source_target_pairs={{32,65},{96,1},{1,96},{65,32},{40,73},{104,9},{9,104},{73,40},{48,... | collective-permute-start | bytes 393224 | tf_op jit(solution)/shard_map/ppermute | solution.py:32
  86.6 8.7 %collective-permute-start.17 = (bf16[256,512]{1,0:T(8,128)(2,1)S(1)}, bf16[256,512]{1,0:T(8,128)(2,1)S(1)}, u32[]{:S(2)}, u32[]{:S(2)}) collective-permute-start(bf16[256,512]{1,0:T(8,128)(2,1)S(1)} %shard_map.121.refs_0_), channel_id=1, source_target_pairs={{0,2},{32,40},{64,66},{96,104},{1,3},{33,41},{65,67},{97,105},{8,1... | collective-permute-start | bytes 786440 | tf_op jit(solution)/shard_map/ppermute | solution.py:32
  87.9 9.8 %collective-permute-start.18 = (bf16[256,512]{1,0:T(8,128)(2,1)S(1)}, bf16[256,512]{1,0:T(8,128)(2,1)S(1)}, u32[]{:S(2)}, u32[]{:S(2)}) collective-permute-start(bf16[256,512]{1,0:T(8,128)(2,1)S(1)} %shard_map.121.refs_0_), channel_id=1, source_target_pairs={{0,6},{32,56},{64,70},{96,120},{1,7},{33,57},{65,71},{97,121},{8,1... | collective-permute-start | bytes 786440 | tf_op jit(solution)/shard_map/ppermute | solution.py:32
  91.6 7.7 %collective-permute-start.19 = (bf16[256,512]{1,0:T(8,128)(2,1)S(1)}, bf16[256,512]{1,0:T(8,128)(2,1)S(1)}, u32[]{:S(2)}, u32[]{:S(2)}) collective-permute-start(bf16[256,512]{1,0:T(8,128)(2,1)S(1)} %shard_map.121.refs_0_), channel_id=1, source_target_pairs={{0,4},{32,48},{64,68},{96,112},{1,5},{33,49},{65,69},{97,113},{8,1... | collective-permute-start | bytes 786440 | tf_op jit(solution)/shard_map/ppermute | solution.py:32
  99.4 5.5 %collective-permute-start.22 = (bf16[1024,512]{1,0:T(8,128)(2,1)S(1)}, bf16[1024,512]{1,0:T(8,128)(2,1)S(1)}, u32[]{:S(2)}, u32[]{:S(2)}) collective-permute-start(bf16[1024,512]{1,0:T(8,128)(2,1)S(1)} %get-tuple-element.72.refs_0_), channel_id=1, source_target_pairs={{0,32},{32,0},{64,96},{96,64},{1,33},{33,1},{65,97},{97,65},{8,40}... | collective-permute-start | bytes 3145736 | tf_op jit(solution)/shard_map/ppermute | solution.py:32
  99.5 9.6 %collective-permute-start.20 = (bf16[512,512]{1,0:T(8,128)(2,1)S(1)}, bf16[512,512]{1,0:T(8,128)(2,1)S(1)}, u32[]{:S(2)}, u32[]{:S(2)}) collective-permute-start(bf16[512,512]{1,0:T(8,128)(2,1)S(1)} %get-tuple-element.69), channel_id=1, source_target_pairs={{0,8},{32,34},{64,72},{96,98},{1,9},{33,35},{65,73},{97,99},{8,16}... | collective-permute-start | bytes 1572872 | tf_op jit(solution)/shard_map/ppermute | solution.py:32
  100.4 8.6 %collective-permute-start.21 = (bf16[512,512]{1,0:T(8,128)(2,1)S(1)}, bf16[512,512]{1,0:T(8,128)(2,1)S(1)}, u32[]{:S(2)}, u32[]{:S(2)}) collective-permute-start(bf16[512,512]{1,0:T(8,128)(2,1)S(1)} %get-tuple-element.70), channel_id=1, source_target_pairs={{0,24},{32,38},{64,88},{96,102},{1,25},{33,39},{65,89},{97,103},{8... | collective-permute-start | bytes 1572872 | tf_op jit(solution)/shard_map/ppermute | solution.py:32
  102.2 12.5 %collective-permute-start.25 = (bf16[512,512]{1,0:T(8,128)(2,1)S(1)}, bf16[512,512]{1,0:T(8,128)(2,1)S(1)}, u32[]{:S(2)}, u32[]{:S(2)}) collective-permute-start(bf16[512,512]{1,0:T(8,128)(2,1)S(1)} %get-tuple-element.70), channel_id=1, source_target_pairs={{0,8},{32,34},{64,72},{96,98},{1,9},{33,35},{65,73},{97,99},{8,16}... | collective-permute-start | bytes 1572872 | tf_op jit(solution)/shard_map/ppermute | solution.py:32
  102.2 12.5 %collective-permute-start.26 = (bf16[512,512]{1,0:T(8,128)(2,1)S(1)}, bf16[512,512]{1,0:T(8,128)(2,1)S(1)}, u32[]{:S(2)}, u32[]{:S(2)}) collective-permute-start(bf16[512,512]{1,0:T(8,128)(2,1)S(1)} %get-tuple-element.69), channel_id=1, source_target_pairs={{0,24},{32,38},{64,88},{96,102},{1,25},{33,39},{65,89},{97,103},{8... | collective-permute-start | bytes 1572872 | tf_op jit(solution)/shard_map/ppermute | solution.py:32
  109.1 11.2 %collective-permute-start.23 = (bf16[512,512]{1,0:T(8,128)(2,1)S(1)}, bf16[512,512]{1,0:T(8,128)(2,1)S(1)}, u32[]{:S(2)}, u32[]{:S(2)}) collective-permute-start(bf16[512,512]{1,0:T(8,128)(2,1)S(1)} %collective-permute-done.20.left), channel_id=1, source_target_pairs={{0,8},{32,34},{64,72},{96,98},{1,9},{33,35},{65,73},{97,99},{8,16}... | collective-permute-start | bytes 1572872 | tf_op jit(solution)/shard_map/ppermute | solution.py:32
  109.7 10.6 %collective-permute-start.24 = (bf16[512,512]{1,0:T(8,128)(2,1)S(1)}, bf16[512,512]{1,0:T(8,128)(2,1)S(1)}, u32[]{:S(2)}, u32[]{:S(2)}) collective-permute-start(bf16[512,512]{1,0:T(8,128)(2,1)S(1)} %collective-permute-done.21.right), channel_id=1, source_target_pairs={{0,24},{32,38},{64,88},{96,102},{1,25},{33,39},{65,89},{97,103},{8... | collective-permute-start | bytes 1572872 | tf_op jit(solution)/shard_map/ppermute | solution.py:32
  111.7 7.2 %collective-permute-start.27 = (f32[256,256]{1,0:T(8,128)S(1)}, f32[256,256]{1,0:T(8,128)S(1)}, u32[]{:S(2)}, u32[]{:S(2)}) collective-permute-start(f32[256,256]{1,0:T(8,128)S(1)} %get-tuple-element.77.mine), channel_id=1, source_target_pairs={{0,32},{32,0},{64,96},{96,64},{1,33},{33,1},{65,97},{97,65},{8,40}... | collective-permute-start | bytes 786440 | tf_op jit(solution)/shard_map/ppermute | solution.py:32
  114.8 9.9 %collective-permute-start.29 = (bf16[1024,512]{1,0:T(8,128)(2,1)S(1)}, bf16[1024,512]{1,0:T(8,128)(2,1)S(1)}, u32[]{:S(2)}, u32[]{:S(2)}) collective-permute-start(bf16[1024,512]{1,0:T(8,128)(2,1)S(1)} %shard_map.124.refs_0_), channel_id=1, source_target_pairs={{0,32},{32,0},{64,96},{96,64},{1,33},{33,1},{65,97},{97,65},{8,40}... | collective-permute-start | bytes 3145736 | tf_op jit(solution)/shard_map/ppermute | solution.py:32
  117.5 5.8 %collective-permute-start.30 = (bf16[1024,512]{1,0:T(8,128)(2,1)S(1)}, bf16[1024,512]{1,0:T(8,128)(2,1)S(1)}, u32[]{:S(2)}, u32[]{:S(2)}) collective-permute-start(bf16[1024,512]{1,0:T(8,128)(2,1)S(1)} %shard_map.125.refs_0_), channel_id=1, source_target_pairs={{0,32},{32,0},{64,96},{96,64},{1,33},{33,1},{65,97},{97,65},{8,40}... | collective-permute-start | bytes 3145736 | tf_op jit(solution)/shard_map/ppermute | solution.py:32
  120.4 5.6 %collective-permute-start.28 = (bf16[1024,512]{1,0:T(8,128)(2,1)S(1)}, bf16[1024,512]{1,0:T(8,128)(2,1)S(1)}, u32[]{:S(2)}, u32[]{:S(2)}) collective-permute-start(bf16[1024,512]{1,0:T(8,128)(2,1)S(1)} %shard_map.129.refs_0_), channel_id=1, source_target_pairs={{0,32},{32,0},{64,96},{96,64},{1,33},{33,1},{65,97},{97,65},{8,40}... | collective-permute-start | bytes 3145736 | tf_op jit(solution)/shard_map/ppermute | solution.py:32

commit v6 on v5

--- a/solution.py
+++ b/solution.py
@@ -341,15 +341,14 @@
     return both
 
 
+NEAR = [(0, 0), (3, 0), (1, 0), (2, 0)]
+WAVES = [(0, 3), (3, 3), (1, 1), (2, 1), (1, 3), (2, 3), (0, 1), (3, 1)]
+FAR = [(0, 2), (3, 2), (1, 2), (2, 2)]
 ORDER = [
     (partner, place)
-    for part in (
-        [(0, 0), (3, 0), (1, 0), (2, 0)],
-        [(0, 3), (3, 3), (1, 1), (2, 1)],
-        [(1, 3), (2, 3), (0, 1), (3, 1)],
-        [(0, 2), (3, 2), (1, 2), (2, 2)],
-    )
-    for partner in range(2)
+    for partner, part in (
+        (0, NEAR), (1, NEAR), (0, WAVES), (1, WAVES), (0, FAR), (1, FAR)
+    )
     for place in part
 ]
 
@@ -372,18 +371,15 @@
     low_up, high_down, acc = lax.optimization_barrier((low_up, high_down, acc))
     far_low, far_high = permute(low_up, second(1)), permute(high_down, second(-1))
     wave_one = join(low_up, high_down)
-    acc = project(held, 2048, [wave_one], acc, None)
     wave_two = join(high_up, low_down)
-    acc = project(held, 4096, [wave_two], acc, None)
+    acc = project(held, 2048, [wave_one, wave_two], acc, None)
     far_low, far_high, acc, new_global, new_momentum = lax.optimization_barrier(
         (far_low, far_high, acc, *finished)
     )
     wave = join(far_low, far_high)
     waves = [permute(array, other_core) for array in (wave_one, wave_two)]
     theirs = permute(wave, other_core)
-    acc = project(held, 6144, [wave], acc, None)
-    acc = project(held, 3072, waves[:1], acc, None)
-    acc = project(held, 5120, waves[1:], acc, None)
+    acc = project(held, 4096, [*waves, wave], acc, None)
     return project(held, 7168, [theirs], acc, scale), new_global, new_momentum
 
 

time: 129 us -> 128 us (level)
    pallas_call x7 -> x4, Pallas kernels: 11.4 us -> 10.9 us  [project(): pl.pallas_call(functools.partial(project_kernel, start, bool(carried), sc...]
where the time goes in v6:
time: 128 us
  starting transfers between devices  45.7 us (36%)
  waiting for transfers between devices  40.8 us (32%)
  Pallas kernels  38.1 us (30%)
  local copies, waits for them, and re-layouts  2.4 us (2%)
    ppermute x31, starting transfers between devices, permute(): return lax.ppermute(array, BOTH, pairs)  45.7 us
    ppermute x31, waiting for transfers between devices, permute(): return lax.ppermute(array, BOTH, pairs)  40.8 us
    pallas_call x4, Pallas kernels, grad_blocks(): pl.pallas_call(functools.partial(grad_kernel, names, len(recv)), in_specs...  17.4 us
    pallas_call x4, Pallas kernels, project(): pl.pallas_call(functools.partial(project_kernel, start, bool(carried), sc...  10.9 us
    pallas_call x1, Pallas kernels, arrange(): pl.pallas_call(functools.partial(arrange_kernel, places), in_specs=[ANY],...  6.31 us
    pallas_call x12, Pallas kernels, local(): pl.pallas_call(kernel, in_specs=[VMEM] * len(arrays), out_specs=[VMEM] *...  3.52 us
  transfers between devices with their start and end apart: 31, of which 15 were waited for; matrix products, arithmetic and copies ran while one was open for 0% of the time, Pallas kernels for 23%

profile of v6, /device:TPU:1, one launch (start us, length us, event | category | flops | bytes accessed | tf_op | source)
XLA Modules:
  0.0 128.1 jit_solution(10453909728259888565)
XLA Ops:
  0.6 1.2 copy-done
  1.9 4.3 %shard_map.112 = (bf16[1024,512]{1,0:T(8,128)(2,1)S(1)}, bf16[1024,512]{1,0:T(8,128)(2,1)S(1)}) custom-call(bf16[1024,8192]{1,0:T(8,128)(2,1)} %tok_ref.8, bf16[1024,512]{1,0:T(8,128)(2,1)S(1)} %copy-done), custom_call_target="tpu_custom_call" | custom-call | flops 2147483648 | bytes 4194304 | tf_op jit(solution)/shard_map/pallas_call | solution.py:138
  6.2 2.2 %collective-permute-start.2 = (bf16[1024,512]{1,0:T(8,128)(2,1)S(1)}, bf16[1024,512]{1,0:T(8,128)(2,1)S(1)}, u32[]{:S(2)}, u32[]{:S(2)}) collective-permute-start(bf16[1024,512]{1,0:T(8,128)(2,1)S(1)} %get-tuple-element.49), channel_id=1, source_target_pairs={{0,2},{32,40},{64,66},{96,104},{1,3},{33,41},{65,67},{97,105},{8,1... | collective-permute-start | bytes 3145736 | tf_op jit(solution)/shard_map/ppermute | solution.py:32
  8.4 1.5 %collective-permute-start.3 = (bf16[1024,512]{1,0:T(8,128)(2,1)S(1)}, bf16[1024,512]{1,0:T(8,128)(2,1)S(1)}, u32[]{:S(2)}, u32[]{:S(2)}) collective-permute-start(bf16[1024,512]{1,0:T(8,128)(2,1)S(1)} %get-tuple-element.50), channel_id=1, source_target_pairs={{0,6},{32,56},{64,70},{96,120},{1,7},{33,57},{65,71},{97,121},{8,1... | collective-permute-start | bytes 3145736 | tf_op jit(solution)/shard_map/ppermute | solution.py:32
  9.9 4.3 %shard_map.110 = (bf16[1024,512]{1,0:T(8,128)(2,1)S(1)}, bf16[1024,512]{1,0:T(8,128)(2,1)S(1)}) custom-call(bf16[1024,8192]{1,0:T(8,128)(2,1)} %tok_ref.8, bf16[1024,512]{1,0:T(8,128)(2,1)S(1)} %copy-done), custom_call_target="tpu_custom_call" | custom-call | flops 2147483648 | bytes 4194304 | tf_op jit(solution)/shard_map/pallas_call | solution.py:138
  14.3 1.5 %collective-permute-start = (bf16[1024,512]{1,0:T(8,128)(2,1)S(1)}, bf16[1024,512]{1,0:T(8,128)(2,1)S(1)}, u32[]{:S(2)}, u32[]{:S(2)}) collective-permute-start(bf16[1024,512]{1,0:T(8,128)(2,1)S(1)} %get-tuple-element.45), channel_id=1, source_target_pairs={{0,6},{32,56},{64,70},{96,120},{1,7},{33,57},{65,71},{97,121},{8,1... | collective-permute-start | bytes 3145736 | tf_op jit(solution)/shard_map/ppermute | solution.py:32
  15.7 0.1 collective-permute-start.1
  15.8 6.5 %collective-permute-done.2.refs_0_ = bf16[1024,512]{1,0:T(8,128)(2,1)S(1)} collective-permute-done((bf16[1024,512]{1,0:T(8,128)(2,1)S(1)}, bf16[1024,512]{1,0:T(8,128)(2,1)S(1)}, u32[]{:S(2)}, u32[]{:S(2)}) %collective-permute-start.2) | collective-permute-done | bytes 1048608 | tf_op jit(solution)/shard_map/ppermute | solution.py:32
  22.4 4.4 %shard_map.113 = (bf16[1024,512]{1,0:T(8,128)(2,1)S(1)}, bf16[1024,512]{1,0:T(8,128)(2,1)S(1)}) custom-call(bf16[1024,8192]{1,0:T(8,128)(2,1)} %tok_ref.8, bf16[1024,512]{1,0:T(8,128)(2,1)S(1)} %copy-done.1, bf16[1024,512]{1,0:T(8,128)(2,1)S(1)} %collective-permute-done.2.refs_0_, bf16[1024,512]{1,0:T(8,128)(2,1)S(1)} %collective-permute-done.3.refs_1_), custom_call_target="tpu_custom_call" | custom-call | flops 2147483648 | bytes 4194304 | tf_op jit(solution)/shard_map/pallas_call | solution.py:138
  26.7 1.4 %collective-permute-start.4 = (bf16[1024,512]{1,0:T(8,128)(2,1)S(1)}, bf16[1024,512]{1,0:T(8,128)(2,1)S(1)}, u32[]{:S(2)}, u32[]{:S(2)}) collective-permute-start(bf16[1024,512]{1,0:T(8,128)(2,1)S(1)} %get-tuple-element.51), channel_id=1, source_target_pairs={{0,2},{32,40},{64,66},{96,104},{1,3},{33,41},{65,67},{97,105},{8,1... | collective-permute-start | bytes 3145736 | tf_op jit(solution)/shard_map/ppermute | solution.py:32
  28.1 1.5 %collective-permute-start.5 = (bf16[1024,512]{1,0:T(8,128)(2,1)S(1)}, bf16[1024,512]{1,0:T(8,128)(2,1)S(1)}, u32[]{:S(2)}, u32[]{:S(2)}) collective-permute-start(bf16[1024,512]{1,0:T(8,128)(2,1)S(1)} %get-tuple-element.52), channel_id=1, source_target_pairs={{0,6},{32,56},{64,70},{96,120},{1,7},{33,57},{65,71},{97,121},{8,1... | collective-permute-start | bytes 3145736 | tf_op jit(solution)/shard_map/ppermute | solution.py:32
  29.6 4.0 %collective-permute-done.refs_0_ = bf16[1024,512]{1,0:T(8,128)(2,1)S(1)} collective-permute-done((bf16[1024,512]{1,0:T(8,128)(2,1)S(1)}, bf16[1024,512]{1,0:T(8,128)(2,1)S(1)}, u32[]{:S(2)}, u32[]{:S(2)}) %collective-permute-start) | collective-permute-done | bytes 1048608 | tf_op jit(solution)/shard_map/ppermute | solution.py:32
  33.6 4.3 %shard_map.111 = (f32[1024,512]{1,0:T(8,128)S(1)}, f32[1024,512]{1,0:T(8,128)S(1)}) custom-call(bf16[1024,8192]{1,0:T(8,128)(2,1)} %tok_ref.8, bf16[1024,512]{1,0:T(8,128)(2,1)S(1)} %copy-done.1, bf16[1024,512]{1,0:T(8,128)(2,1)S(1)} %collective-permute-done.refs_0_, bf16[1024,512]{1,0:T(8,128)(2,1)S(1)} %collective-permute-done.1.refs_1_), custom_call_target="tpu_custom_call" | custom-call | flops 2147483648 | bytes 4194304 | tf_op jit(solution)/shard_map/pallas_call | solution.py:138
  37.9 6.9 %collective-permute-done.4.got1 = bf16[1024,512]{1,0:T(8,128)(2,1)S(1)} collective-permute-done((bf16[1024,512]{1,0:T(8,128)(2,1)S(1)}, bf16[1024,512]{1,0:T(8,128)(2,1)S(1)}, u32[]{:S(2)}, u32[]{:S(2)}) %collective-permute-start.4) | collective-permute-done | bytes 1048608 | tf_op jit(solution)/shard_map/ppermute | solution.py:32
  44.8 0.3 shard_map.114
  45.2 1.3 collective-permute-start.10
  46.4 1.5 %collective-permute-start.11 = (bf16[256,512]{1,0:T(8,128)(2,1)S(1)}, bf16[256,512]{1,0:T(8,128)(2,1)S(1)}, u32[]{:S(2)}, u32[]{:S(2)}) collective-permute-start(bf16[256,512]{1,0:T(8,128)(2,1)S(1)} %get-tuple-element.60), channel_id=1, source_target_pairs={{0,24},{32,38},{64,88},{96,102},{1,25},{33,39},{65,89},{97,103},{8... | collective-permute-start | bytes 786440 | tf_op jit(solution)/shard_map/ppermute | solution.py:32
  47.9 1.5 %collective-permute-start.9 = (bf16[256,512]{1,0:T(8,128)(2,1)S(1)}, bf16[256,512]{1,0:T(8,128)(2,1)S(1)}, u32[]{:S(2)}, u32[]{:S(2)}) collective-permute-start(bf16[256,512]{1,0:T(8,128)(2,1)S(1)} %get-tuple-element.58), channel_id=1, source_target_pairs={{0,16},{32,36},{64,80},{96,100},{1,17},{33,37},{65,81},{97,101},{8... | collective-permute-start | bytes 786440 | tf_op jit(solution)/shard_map/ppermute | solution.py:32
  49.4 1.4 %collective-permute-start.6 = (bf16[256,512]{1,0:T(8,128)(2,1)S(1)}, bf16[256,512]{1,0:T(8,128)(2,1)S(1)}, u32[]{:S(2)}, u32[]{:S(2)}) collective-permute-start(bf16[256,512]{1,0:T(8,128)(2,1)S(1)} %get-tuple-element.54), channel_id=1, source_target_pairs={{0,16},{32,36},{64,80},{96,100},{1,17},{33,37},{65,81},{97,101},{8... | collective-permute-start | bytes 786440 | tf_op jit(solution)/shard_map/ppermute | solution.py:32
  50.9 1.1 collective-permute-done.10.refs_1_
  52.0 1.6 %collective-permute-start.8 = (bf16[256,512]{1,0:T(8,128)(2,1)S(1)}, bf16[256,512]{1,0:T(8,128)(2,1)S(1)}, u32[]{:S(2)}, u32[]{:S(2)}) collective-permute-start(bf16[256,512]{1,0:T(8,128)(2,1)S(1)} %get-tuple-element.56), channel_id=1, source_target_pairs={{0,24},{32,38},{64,88},{96,102},{1,25},{33,39},{65,89},{97,103},{8... | collective-permute-start | bytes 786440 | tf_op jit(solution)/shard_map/ppermute | solution.py:32
  53.6 2.2 %collective-permute-done.9.refs_0_ = bf16[256,512]{1,0:T(8,128)(2,1)S(1)} collective-permute-done((bf16[256,512]{1,0:T(8,128)(2,1)S(1)}, bf16[256,512]{1,0:T(8,128)(2,1)S(1)}, u32[]{:S(2)}, u32[]{:S(2)}) %collective-permute-start.9) | collective-permute-done | bytes 262176 | tf_op jit(solution)/shard_map/ppermute | solution.py:32
  55.8 0.1 shard_map.116
  55.9 3.7 %collective-permute-start.12 = (bf16[256,512]{1,0:T(8,128)(2,1)S(1)}, bf16[256,512]{1,0:T(8,128)(2,1)S(1)}, u32[]{:S(2)}, u32[]{:S(2)}) collective-permute-start(bf16[256,512]{1,0:T(8,128)(2,1)S(1)} %shard_map.116), channel_id=1, source_target_pairs={{0,1},{32,33},{64,65},{96,97},{1,0},{33,32},{65,64},{97,96},{8,9},... | collective-permute-start | bytes 786440 | tf_op jit(solution)/shard_map/ppermute | solution.py:32
  59.5 6.3 %shard_map.117.held = bf16[1024,8192]{1,0:T(8,128)(2,1)S(1)} custom-call(bf16[1024,8192]{1,0:T(8,128)(2,1)} %tok_ref.8), custom_call_target="tpu_custom_call" | custom-call | flops 1 | bytes 1 | tf_op jit(solution)/shard_map/pallas_call | solution.py:288
  66.0 0.1 shard_map.115.keep
  66.1 0.8 copy-done.4
  66.9 0.2 copy-done.5
  67.1 0.2 copy-done.6
  67.2 1.3 %shard_map.118 = (f32[256,512]{1,0:T(8,128)}, f32[256,512]{1,0:T(8,128)}, f32[256,256]{1,0:T(8,128)S(1)}, f32[256,256]{1,0:T(8,128)S(1)}) custom-call(f32[256,512]{1,0:T(8,128)S(1)} %shard_map.115.keep, bf16[256,512]{1,0:T(8,128)(2,1)S(1)} %collective-permute-done.12.got, f32[256,512]{1,0:T(8,128)S(1)} %bitcast.5, f32[256,512]{1,0:T(8,128)S(1)} %bitcast.6, ...), custom_call_target="tpu_custom_call" | custom-call | tf_op jit(solution)/shard_map/pallas_call | solution.py:79
  68.5 3.1 %collective-permute-start.13 = (f32[256,256]{1,0:T(8,128)S(1)}, f32[256,256]{1,0:T(8,128)S(1)}, u32[]{:S(2)}, u32[]{:S(2)}) collective-permute-start(f32[256,256]{1,0:T(8,128)S(1)} %get-tuple-element.67), channel_id=1, source_target_pairs={{0,32},{32,0},{64,96},{96,64},{1,33},{33,1},{65,97},{97,65},{8,40}... | collective-permute-start | bytes 786440 | tf_op jit(solution)/shard_map/ppermute | solution.py:32
  71.7 1.2 collective-permute-done.13.right
  72.8 0.8 collective-permute-start.14
  73.7 4.0 %collective-permute-done.14.right = bf16[256,256]{1,0:T(8,128)(2,1)S(1)} collective-permute-done((bf16[256,256]{1,0:T(8,128)(2,1)S(1)}, bf16[256,256]{1,0:T(8,128)(2,1)S(1)}, u32[]{:S(2)}, u32[]{:S(2)}) %collective-permute-start.14) | collective-permute-done | bytes 131104 | tf_op jit(solution)/shard_map/ppermute | solution.py:32
  77.6 0.1 shard_map.120
  77.8 1.3 collective-permute-start.15
  79.1 2.2 %collective-permute-start.16 = (bf16[256,256]{1,0:T(8,128)(2,1)S(1)}, bf16[256,256]{1,0:T(8,128)(2,1)S(1)}, u32[]{:S(2)}, u32[]{:S(2)}) collective-permute-start(bf16[256,256]{1,0:T(8,128)(2,1)S(1)} %get-tuple-element.68.mine), channel_id=1, source_target_pairs={{32,65},{96,1},{1,96},{65,32},{40,73},{104,9},{9,104},{73,40},{48,... | collective-permute-start | bytes 393224 | tf_op jit(solution)/shard_map/ppermute | solution.py:32
  81.3 1.6 %collective-permute-done.15.one = bf16[256,256]{1,0:T(8,128)(2,1)S(1)} collective-permute-done((bf16[256,256]{1,0:T(8,128)(2,1)S(1)}, bf16[256,256]{1,0:T(8,128)(2,1)S(1)}, u32[]{:S(2)}, u32[]{:S(2)}) %collective-permute-start.15) | collective-permute-done | bytes 131104 | tf_op jit(solution)/shard_map/ppermute | solution.py:32
  82.9 3.7 %collective-permute-done.16.two = bf16[256,256]{1,0:T(8,128)(2,1)S(1)} collective-permute-done((bf16[256,256]{1,0:T(8,128)(2,1)S(1)}, bf16[256,256]{1,0:T(8,128)(2,1)S(1)}, u32[]{:S(2)}, u32[]{:S(2)}) %collective-permute-start.16) | collective-permute-done | bytes 131104 | tf_op jit(solution)/shard_map/ppermute | solution.py:32
  86.6 1.3 %collective-permute-start.17 = (bf16[256,512]{1,0:T(8,128)(2,1)S(1)}, bf16[256,512]{1,0:T(8,128)(2,1)S(1)}, u32[]{:S(2)}, u32[]{:S(2)}) collective-permute-start(bf16[256,512]{1,0:T(8,128)(2,1)S(1)} %shard_map.121.refs_0_), channel_id=1, source_target_pairs={{0,2},{32,40},{64,66},{96,104},{1,3},{33,41},{65,67},{97,105},{8,1... | collective-permute-start | bytes 786440 | tf_op jit(solution)/shard_map/ppermute | solution.py:32
  87.9 3.7 %collective-permute-start.18 = (bf16[256,512]{1,0:T(8,128)(2,1)S(1)}, bf16[256,512]{1,0:T(8,128)(2,1)S(1)}, u32[]{:S(2)}, u32[]{:S(2)}) collective-permute-start(bf16[256,512]{1,0:T(8,128)(2,1)S(1)} %shard_map.121.refs_0_), channel_id=1, source_target_pairs={{0,6},{32,56},{64,70},{96,120},{1,7},{33,57},{65,71},{97,121},{8,1... | collective-permute-start | bytes 786440 | tf_op jit(solution)/shard_map/ppermute | solution.py:32
  91.6 1.1 collective-permute-start.19
  92.7 2.6 %collective-permute-done.17.refs_1_ = bf16[256,512]{1,0:T(8,128)(2,1)S(1)} collective-permute-done((bf16[256,512]{1,0:T(8,128)(2,1)S(1)}, bf16[256,512]{1,0:T(8,128)(2,1)S(1)}, u32[]{:S(2)}, u32[]{:S(2)}) %collective-permute-start.17) | collective-permute-done | bytes 262176 | tf_op jit(solution)/shard_map/ppermute | solution.py:32
  95.2 2.4 %collective-permute-done.18.refs_2_ = bf16[256,512]{1,0:T(8,128)(2,1)S(1)} collective-permute-done((bf16[256,512]{1,0:T(8,128)(2,1)S(1)}, bf16[256,512]{1,0:T(8,128)(2,1)S(1)}, u32[]{:S(2)}, u32[]{:S(2)}) %collective-permute-start.18) | collective-permute-done | bytes 262176 | tf_op jit(solution)/shard_map/ppermute | solution.py:32
  97.7 1.5 %collective-permute-done.19.refs_3_ = bf16[256,512]{1,0:T(8,128)(2,1)S(1)} collective-permute-done((bf16[256,512]{1,0:T(8,128)(2,1)S(1)}, bf16[256,512]{1,0:T(8,128)(2,1)S(1)}, u32[]{:S(2)}, u32[]{:S(2)}) %collective-permute-start.19) | collective-permute-done | bytes 262176 | tf_op jit(solution)/shard_map/ppermute | solution.py:32
  99.2 0.1 shard_map.122
  99.4 0.1 collective-permute-start.22
  99.5 1.0 collective-permute-start.20
  100.4 1.8 %collective-permute-start.21 = (bf16[512,512]{1,0:T(8,128)(2,1)S(1)}, bf16[512,512]{1,0:T(8,128)(2,1)S(1)}, u32[]{:S(2)}, u32[]{:S(2)}) collective-permute-start(bf16[512,512]{1,0:T(8,128)(2,1)S(1)} %get-tuple-element.70), channel_id=1, source_target_pairs={{0,24},{32,38},{64,88},{96,102},{1,25},{33,39},{65,89},{97,103},{8... | collective-permute-start | bytes 1572872 | tf_op jit(solution)/shard_map/ppermute | solution.py:32
  102.2 2.7 %collective-permute-start.26 = (bf16[512,512]{1,0:T(8,128)(2,1)S(1)}, bf16[512,512]{1,0:T(8,128)(2,1)S(1)}, u32[]{:S(2)}, u32[]{:S(2)}) collective-permute-start(bf16[512,512]{1,0:T(8,128)(2,1)S(1)} %get-tuple-element.69), channel_id=1, source_target_pairs={{0,24},{32,38},{64,88},{96,102},{1,25},{33,39},{65,89},{97,103},{8... | collective-permute-start | bytes 1572872 | tf_op jit(solution)/shard_map/ppermute | solution.py:32
  104.9 2.5 %shard_map.123.refs_2_ = f32[1024,512]{1,0:T(8,128)S(1)} custom-call(bf16[1024,8192]{1,0:T(8,128)(2,1)S(1)} %shard_map.117.held, bf16[1024,512]{1,0:T(8,128)(2,1)S(1)} %get-tuple-element.72.refs_0_, bf16[1024,512]{1,0:T(8,128)(2,1)S(1)} %collective-permute-done.22.refs_1_), custom_call_target="tpu_custom_call" | custom-call | flops 1 | bytes 1 | tf_op jit(solution)/shard_map/pallas_call | solution.py:319
  107.4 1.7 %collective-permute-done.20.left = bf16[512,512]{1,0:T(8,128)(2,1)S(1)} collective-permute-done((bf16[512,512]{1,0:T(8,128)(2,1)S(1)}, bf16[512,512]{1,0:T(8,128)(2,1)S(1)}, u32[]{:S(2)}, u32[]{:S(2)}) %collective-permute-start.20) | collective-permute-done | bytes 524320 | tf_op jit(solution)/shard_map/ppermute | solution.py:32
  109.1 0.6 collective-permute-start.23
  109.7 2.0 %collective-permute-start.24 = (bf16[512,512]{1,0:T(8,128)(2,1)S(1)}, bf16[512,512]{1,0:T(8,128)(2,1)S(1)}, u32[]{:S(2)}, u32[]{:S(2)}) collective-permute-start(bf16[512,512]{1,0:T(8,128)(2,1)S(1)} %collective-permute-done.21.right), channel_id=1, source_target_pairs={{0,24},{32,38},{64,88},{96,102},{1,25},{33,39},{65,89},{97,103},{8... | collective-permute-start | bytes 1572872 | tf_op jit(solution)/shard_map/ppermute | solution.py:32
  111.7 1.8 %collective-permute-start.27 = (f32[256,256]{1,0:T(8,128)S(1)}, f32[256,256]{1,0:T(8,128)S(1)}, u32[]{:S(2)}, u32[]{:S(2)}) collective-permute-start(f32[256,256]{1,0:T(8,128)S(1)} %get-tuple-element.77.mine), channel_id=1, source_target_pairs={{0,32},{32,0},{64,96},{96,64},{1,33},{33,1},{65,97},{97,65},{8,40}... | collective-permute-start | bytes 786440 | tf_op jit(solution)/shard_map/ppermute | solution.py:32
  113.6 1.1 collective-permute-done.25.left
  114.8 1.4 %collective-permute-start.30 = (bf16[1024,512]{1,0:T(8,128)(2,1)S(1)}, bf16[1024,512]{1,0:T(8,128)(2,1)S(1)}, u32[]{:S(2)}, u32[]{:S(2)}) collective-permute-start(bf16[1024,512]{1,0:T(8,128)(2,1)S(1)} %shard_map.125.refs_1_), channel_id=1, source_target_pairs={{0,32},{32,0},{64,96},{96,64},{1,33},{33,1},{65,97},{97,65},{8,40}... | collective-permute-start | bytes 3145736 | tf_op jit(solution)/shard_map/ppermute | solution.py:32
  116.2 0.1 collective-permute-start.29
  116.3 2.5 %shard_map.126.refs_3_ = f32[1024,512]{1,0:T(8,128)S(1)} custom-call(bf16[1024,8192]{1,0:T(8,128)(2,1)S(1)} %shard_map.117.held, bf16[1024,512]{1,0:T(8,128)(2,1)S(1)} %shard_map.124.refs_0_, bf16[1024,512]{1,0:T(8,128)(2,1)S(1)} %shard_map.125.refs_1_, f32[1024,512]{1,0:T(8,128)S(1)} %shard_map.123.refs_2_), custom_call_target="tpu_custom_call" | custom-call | flops 1 | bytes 1 | tf_op jit(solution)/shard_map/pallas_call | solution.py:319
  118.8 1.1 shard_map.127
  119.9 0.4 collective-permute-done.23.left
  120.4 1.6 %collective-permute-start.28 = (bf16[1024,512]{1,0:T(8,128)(2,1)S(1)}, bf16[1024,512]{1,0:T(8,128)(2,1)S(1)}, u32[]{:S(2)}, u32[]{:S(2)}) collective-permute-start(bf16[1024,512]{1,0:T(8,128)(2,1)S(1)} %shard_map.128.refs_2_), channel_id=1, source_target_pairs={{0,32},{32,0},{64,96},{96,64},{1,33},{33,1},{65,97},{97,65},{8,40}... | collective-permute-start | bytes 3145736 | tf_op jit(solution)/shard_map/ppermute | solution.py:32
  122.0 3.6 %shard_map.129.refs_1_ = f32[1024,512]{1,0:T(8,128)S(1)} custom-call(bf16[1024,8192]{1,0:T(8,128)(2,1)S(1)} %shard_map.117.held, bf16[1024,512]{1,0:T(8,128)(2,1)S(1)} %collective-permute-done.29.refs_0_, bf16[1024,512]{1,0:T(8,128)(2,1)S(1)} %collective-permute-done.30.refs_1_, bf16[1024,512]{1,0:T(8,128)(2,1)S(1)} %shard_map.128.refs_2_, ...), custom_call_target="tpu_custom_call" | custom-call | flops 1 | bytes 1 | tf_op jit(solution)/shard_map/pallas_call | solution.py:319
  125.6 2.3 %shard_map.130 = bf16[1024,512]{1,0:T(8,128)(2,1)} custom-call(bf16[1024,8192]{1,0:T(8,128)(2,1)S(1)} %shard_map.117.held, bf16[1024,512]{1,0:T(8,128)(2,1)S(1)} %collective-permute-done.28.refs_0_, f32[1024,512]{1,0:T(8,128)S(1)} %shard_map.129.refs_1_), custom_call_target="tpu_custom_call" | custom-call | flops 1 | bytes 1 | tf_op jit(solution)/shard_map/pallas_call | solution.py:319
  (33 shorter events, 0.4 us)
Async XLA Ops:
  0.6 1.2 copy-start
  6.2 16.1 %collective-permute-start.2 = (bf16[1024,512]{1,0:T(8,128)(2,1)S(1)}, bf16[1024,512]{1,0:T(8,128)(2,1)S(1)}, u32[]{:S(2)}, u32[]{:S(2)}) collective-permute-start(bf16[1024,512]{1,0:T(8,128)(2,1)S(1)} %get-tuple-element.49), channel_id=1, source_target_pairs={{0,2},{32,40},{64,66},{96,104},{1,3},{33,41},{65,67},{97,105},{8,1... | collective-permute-start | bytes 3145736 | tf_op jit(solution)/shard_map/ppermute | solution.py:32
  8.4 13.9 %copy-start.1 = (bf16[1024,512]{1,0:T(8,128)(2,1)S(1)}, bf16[1024,512]{1,0:T(8,128)(2,1)}, u32[]{:S(2)}) copy-start(bf16[1024,512]{1,0:T(8,128)(2,1)} %grad_ref.7) | copy-start | bytes 3145732
  8.4 13.9 %collective-permute-start.3 = (bf16[1024,512]{1,0:T(8,128)(2,1)S(1)}, bf16[1024,512]{1,0:T(8,128)(2,1)S(1)}, u32[]{:S(2)}, u32[]{:S(2)}) collective-permute-start(bf16[1024,512]{1,0:T(8,128)(2,1)S(1)} %get-tuple-element.50), channel_id=1, source_target_pairs={{0,6},{32,56},{64,70},{96,120},{1,7},{33,57},{65,71},{97,121},{8,1... | collective-permute-start | bytes 3145736 | tf_op jit(solution)/shard_map/ppermute | solution.py:32
  14.3 19.3 %collective-permute-start = (bf16[1024,512]{1,0:T(8,128)(2,1)S(1)}, bf16[1024,512]{1,0:T(8,128)(2,1)S(1)}, u32[]{:S(2)}, u32[]{:S(2)}) collective-permute-start(bf16[1024,512]{1,0:T(8,128)(2,1)S(1)} %get-tuple-element.45), channel_id=1, source_target_pairs={{0,6},{32,56},{64,70},{96,120},{1,7},{33,57},{65,71},{97,121},{8,1... | collective-permute-start | bytes 3145736 | tf_op jit(solution)/shard_map/ppermute | solution.py:32
  15.7 17.8 %collective-permute-start.1 = (bf16[1024,512]{1,0:T(8,128)(2,1)S(1)}, bf16[1024,512]{1,0:T(8,128)(2,1)S(1)}, u32[]{:S(2)}, u32[]{:S(2)}) collective-permute-start(bf16[1024,512]{1,0:T(8,128)(2,1)S(1)} %get-tuple-element.46), channel_id=1, source_target_pairs={{0,2},{32,40},{64,66},{96,104},{1,3},{33,41},{65,67},{97,105},{8,1... | collective-permute-start | bytes 3145736 | tf_op jit(solution)/shard_map/ppermute | solution.py:32
  26.7 18.1 %collective-permute-start.4 = (bf16[1024,512]{1,0:T(8,128)(2,1)S(1)}, bf16[1024,512]{1,0:T(8,128)(2,1)S(1)}, u32[]{:S(2)}, u32[]{:S(2)}) collective-permute-start(bf16[1024,512]{1,0:T(8,128)(2,1)S(1)} %get-tuple-element.51), channel_id=1, source_target_pairs={{0,2},{32,40},{64,66},{96,104},{1,3},{33,41},{65,67},{97,105},{8,1... | collective-permute-start | bytes 3145736 | tf_op jit(solution)/shard_map/ppermute | solution.py:32
  28.1 16.7 %collective-permute-start.5 = (bf16[1024,512]{1,0:T(8,128)(2,1)S(1)}, bf16[1024,512]{1,0:T(8,128)(2,1)S(1)}, u32[]{:S(2)}, u32[]{:S(2)}) collective-permute-start(bf16[1024,512]{1,0:T(8,128)(2,1)S(1)} %get-tuple-element.52), channel_id=1, source_target_pairs={{0,6},{32,56},{64,70},{96,120},{1,7},{33,57},{65,71},{97,121},{8,1... | collective-permute-start | bytes 3145736 | tf_op jit(solution)/shard_map/ppermute | solution.py:32
  45.2 6.8 %collective-permute-start.10 = (bf16[256,512]{1,0:T(8,128)(2,1)S(1)}, bf16[256,512]{1,0:T(8,128)(2,1)S(1)}, u32[]{:S(2)}, u32[]{:S(2)}) collective-permute-start(bf16[256,512]{1,0:T(8,128)(2,1)S(1)} %get-tuple-element.59), channel_id=1, source_target_pairs={{0,8},{32,34},{64,72},{96,98},{1,9},{33,35},{65,73},{97,99},{8,16}... | collective-permute-start | bytes 786440 | tf_op jit(solution)/shard_map/ppermute | solution.py:32
  46.4 7.1 %collective-permute-start.11 = (bf16[256,512]{1,0:T(8,128)(2,1)S(1)}, bf16[256,512]{1,0:T(8,128)(2,1)S(1)}, u32[]{:S(2)}, u32[]{:S(2)}) collective-permute-start(bf16[256,512]{1,0:T(8,128)(2,1)S(1)} %get-tuple-element.60), channel_id=1, source_target_pairs={{0,24},{32,38},{64,88},{96,102},{1,25},{33,39},{65,89},{97,103},{8... | collective-permute-start | bytes 786440 | tf_op jit(solution)/shard_map/ppermute | solution.py:32
  47.9 7.9 %collective-permute-start.9 = (bf16[256,512]{1,0:T(8,128)(2,1)S(1)}, bf16[256,512]{1,0:T(8,128)(2,1)S(1)}, u32[]{:S(2)}, u32[]{:S(2)}) collective-permute-start(bf16[256,512]{1,0:T(8,128)(2,1)S(1)} %get-tuple-element.58), channel_id=1, source_target_pairs={{0,16},{32,36},{64,80},{96,100},{1,17},{33,37},{65,81},{97,101},{8... | collective-permute-start | bytes 786440 | tf_op jit(solution)/shard_map/ppermute | solution.py:32
  49.4 16.5 %collective-permute-start.6 = (bf16[256,512]{1,0:T(8,128)(2,1)S(1)}, bf16[256,512]{1,0:T(8,128)(2,1)S(1)}, u32[]{:S(2)}, u32[]{:S(2)}) collective-permute-start(bf16[256,512]{1,0:T(8,128)(2,1)S(1)} %get-tuple-element.54), channel_id=1, source_target_pairs={{0,16},{32,36},{64,80},{96,100},{1,17},{33,37},{65,81},{97,101},{8... | collective-permute-start | bytes 786440 | tf_op jit(solution)/shard_map/ppermute | solution.py:32
  50.9 15.0 %collective-permute-start.7 = (bf16[256,512]{1,0:T(8,128)(2,1)S(1)}, bf16[256,512]{1,0:T(8,128)(2,1)S(1)}, u32[]{:S(2)}, u32[]{:S(2)}) collective-permute-start(bf16[256,512]{1,0:T(8,128)(2,1)S(1)} %get-tuple-element.55), channel_id=1, source_target_pairs={{0,8},{32,34},{64,72},{96,98},{1,9},{33,35},{65,73},{97,99},{8,16}... | collective-permute-start | bytes 786440 | tf_op jit(solution)/shard_map/ppermute | solution.py:32
  52.0 14.0 %collective-permute-start.8 = (bf16[256,512]{1,0:T(8,128)(2,1)S(1)}, bf16[256,512]{1,0:T(8,128)(2,1)S(1)}, u32[]{:S(2)}, u32[]{:S(2)}) collective-permute-start(bf16[256,512]{1,0:T(8,128)(2,1)S(1)} %get-tuple-element.56), channel_id=1, source_target_pairs={{0,24},{32,38},{64,88},{96,102},{1,25},{33,39},{65,89},{97,103},{8... | collective-permute-start | bytes 786440 | tf_op jit(solution)/shard_map/ppermute | solution.py:32
  55.9 10.2 %collective-permute-start.12 = (bf16[256,512]{1,0:T(8,128)(2,1)S(1)}, bf16[256,512]{1,0:T(8,128)(2,1)S(1)}, u32[]{:S(2)}, u32[]{:S(2)}) collective-permute-start(bf16[256,512]{1,0:T(8,128)(2,1)S(1)} %shard_map.116), channel_id=1, source_target_pairs={{0,1},{32,33},{64,65},{96,97},{1,0},{33,32},{65,64},{97,96},{8,9},... | collective-permute-start | bytes 786440 | tf_op jit(solution)/shard_map/ppermute | solution.py:32
  65.9 1.0 copy-start.4
  65.9 1.2 copy-start.5
  65.9 1.3 %copy-start.6 = (f32[1,256,512]{2,1,0:T(8,128)S(1)}, f32[1,256,512]{2,1,0:T(8,128)}, u32[]{:S(2)}) copy-start(f32[1,256,512]{2,1,0:T(8,128)} %param.11) | copy-start | bytes 1572868
  65.9 11.7 %copy-start.2 = (f32[256,512]{1,0:T(8,128)S(1)}, f32[256,512]{1,0:T(8,128)}, u32[]{:S(2)}) copy-start(f32[256,512]{1,0:T(8,128)} %weights_ref.3) | copy-start | bytes 1572868
  65.9 11.7 %copy-start.3 = (f32[256,512]{1,0:T(8,128)S(1)}, f32[256,512]{1,0:T(8,128)}, u32[]{:S(2)}) copy-start(f32[256,512]{1,0:T(8,128)} %momentum_ref.3) | copy-start | bytes 1572868
  68.5 4.3 %collective-permute-start.13 = (f32[256,256]{1,0:T(8,128)S(1)}, f32[256,256]{1,0:T(8,128)S(1)}, u32[]{:S(2)}, u32[]{:S(2)}) collective-permute-start(f32[256,256]{1,0:T(8,128)S(1)} %get-tuple-element.67), channel_id=1, source_target_pairs={{0,32},{32,0},{64,96},{96,64},{1,33},{33,1},{65,97},{97,65},{8,40}... | collective-permute-start | bytes 786440 | tf_op jit(solution)/shard_map/ppermute | solution.py:32
  72.8 4.8 %collective-permute-start.14 = (bf16[256,256]{1,0:T(8,128)(2,1)S(1)}, bf16[256,256]{1,0:T(8,128)(2,1)S(1)}, u32[]{:S(2)}, u32[]{:S(2)}) collective-permute-start(bf16[256,256]{1,0:T(8,128)(2,1)S(1)} %shard_map.119.left), channel_id=1, source_target_pairs={{0,64},{32,96},{64,0},{96,32},{1,65},{33,97},{65,1},{97,33},{8,72}... | collective-permute-start | bytes 393224 | tf_op jit(solution)/shard_map/ppermute | solution.py:32
  77.8 5.1 %collective-permute-start.15 = (bf16[256,256]{1,0:T(8,128)(2,1)S(1)}, bf16[256,256]{1,0:T(8,128)(2,1)S(1)}, u32[]{:S(2)}, u32[]{:S(2)}) collective-permute-start(bf16[256,256]{1,0:T(8,128)(2,1)S(1)} %get-tuple-element.68.mine), channel_id=1, source_target_pairs={{0,65},{32,0},{64,1},{96,64},{1,33},{33,96},{65,97},{97,32},{8,73}... | collective-permute-start | bytes 393224 | tf_op jit(solution)/shard_map/ppermute | solution.py:32
  79.1 7.5 %collective-permute-start.16 = (bf16[256,256]{1,0:T(8,128)(2,1)S(1)}, bf16[256,256]{1,0:T(8,128)(2,1)S(1)}, u32[]{:S(2)}, u32[]{:S(2)}) collective-permute-start(bf16[256,256]{1,0:T(8,128)(2,1)S(1)} %get-tuple-element.68.mine), channel_id=1, source_target_pairs={{32,65},{96,1},{1,96},{65,32},{40,73},{104,9},{9,104},{73,40},{48,... | collective-permute-start | bytes 393224 | tf_op jit(solution)/shard_map/ppermute | solution.py:32
  86.6 8.7 %collective-permute-start.17 = (bf16[256,512]{1,0:T(8,128)(2,1)S(1)}, bf16[256,512]{1,0:T(8,128)(2,1)S(1)}, u32[]{:S(2)}, u32[]{:S(2)}) collective-permute-start(bf16[256,512]{1,0:T(8,128)(2,1)S(1)} %shard_map.121.refs_0_), channel_id=1, source_target_pairs={{0,2},{32,40},{64,66},{96,104},{1,3},{33,41},{65,67},{97,105},{8,1... | collective-permute-start | bytes 786440 | tf_op jit(solution)/shard_map/ppermute | solution.py:32
  87.9 9.8 %collective-permute-start.18 = (bf16[256,512]{1,0:T(8,128)(2,1)S(1)}, bf16[256,512]{1,0:T(8,128)(2,1)S(1)}, u32[]{:S(2)}, u32[]{:S(2)}) collective-permute-start(bf16[256,512]{1,0:T(8,128)(2,1)S(1)} %shard_map.121.refs_0_), channel_id=1, source_target_pairs={{0,6},{32,56},{64,70},{96,120},{1,7},{33,57},{65,71},{97,121},{8,1... | collective-permute-start | bytes 786440 | tf_op jit(solution)/shard_map/ppermute | solution.py:32
  91.6 7.7 %collective-permute-start.19 = (bf16[256,512]{1,0:T(8,128)(2,1)S(1)}, bf16[256,512]{1,0:T(8,128)(2,1)S(1)}, u32[]{:S(2)}, u32[]{:S(2)}) collective-permute-start(bf16[256,512]{1,0:T(8,128)(2,1)S(1)} %shard_map.121.refs_0_), channel_id=1, source_target_pairs={{0,4},{32,48},{64,68},{96,112},{1,5},{33,49},{65,69},{97,113},{8,1... | collective-permute-start | bytes 786440 | tf_op jit(solution)/shard_map/ppermute | solution.py:32
  99.4 5.5 %collective-permute-start.22 = (bf16[1024,512]{1,0:T(8,128)(2,1)S(1)}, bf16[1024,512]{1,0:T(8,128)(2,1)S(1)}, u32[]{:S(2)}, u32[]{:S(2)}) collective-permute-start(bf16[1024,512]{1,0:T(8,128)(2,1)S(1)} %get-tuple-element.72.refs_0_), channel_id=1, source_target_pairs={{0,32},{32,0},{64,96},{96,64},{1,33},{33,1},{65,97},{97,65},{8,40}... | collective-permute-start | bytes 3145736 | tf_op jit(solution)/shard_map/ppermute | solution.py:32
  99.5 9.6 %collective-permute-start.20 = (bf16[512,512]{1,0:T(8,128)(2,1)S(1)}, bf16[512,512]{1,0:T(8,128)(2,1)S(1)}, u32[]{:S(2)}, u32[]{:S(2)}) collective-permute-start(bf16[512,512]{1,0:T(8,128)(2,1)S(1)} %get-tuple-element.69), channel_id=1, source_target_pairs={{0,8},{32,34},{64,72},{96,98},{1,9},{33,35},{65,73},{97,99},{8,16}... | collective-permute-start | bytes 1572872 | tf_op jit(solution)/shard_map/ppermute | solution.py:32
  100.4 8.6 %collective-permute-start.21 = (bf16[512,512]{1,0:T(8,128)(2,1)S(1)}, bf16[512,512]{1,0:T(8,128)(2,1)S(1)}, u32[]{:S(2)}, u32[]{:S(2)}) collective-permute-start(bf16[512,512]{1,0:T(8,128)(2,1)S(1)} %get-tuple-element.70), channel_id=1, source_target_pairs={{0,24},{32,38},{64,88},{96,102},{1,25},{33,39},{65,89},{97,103},{8... | collective-permute-start | bytes 1572872 | tf_op jit(solution)/shard_map/ppermute | solution.py:32
  102.2 12.5 %collective-permute-start.25 = (bf16[512,512]{1,0:T(8,128)(2,1)S(1)}, bf16[512,512]{1,0:T(8,128)(2,1)S(1)}, u32[]{:S(2)}, u32[]{:S(2)}) collective-permute-start(bf16[512,512]{1,0:T(8,128)(2,1)S(1)} %get-tuple-element.70), channel_id=1, source_target_pairs={{0,8},{32,34},{64,72},{96,98},{1,9},{33,35},{65,73},{97,99},{8,16}... | collective-permute-start | bytes 1572872 | tf_op jit(solution)/shard_map/ppermute | solution.py:32
  102.2 12.5 %collective-permute-start.26 = (bf16[512,512]{1,0:T(8,128)(2,1)S(1)}, bf16[512,512]{1,0:T(8,128)(2,1)S(1)}, u32[]{:S(2)}, u32[]{:S(2)}) collective-permute-start(bf16[512,512]{1,0:T(8,128)(2,1)S(1)} %get-tuple-element.69), channel_id=1, source_target_pairs={{0,24},{32,38},{64,88},{96,102},{1,25},{33,39},{65,89},{97,103},{8... | collective-permute-start | bytes 1572872 | tf_op jit(solution)/shard_map/ppermute | solution.py:32
  109.1 11.2 %collective-permute-start.23 = (bf16[512,512]{1,0:T(8,128)(2,1)S(1)}, bf16[512,512]{1,0:T(8,128)(2,1)S(1)}, u32[]{:S(2)}, u32[]{:S(2)}) collective-permute-start(bf16[512,512]{1,0:T(8,128)(2,1)S(1)} %collective-permute-done.20.left), channel_id=1, source_target_pairs={{0,8},{32,34},{64,72},{96,98},{1,9},{33,35},{65,73},{97,99},{8,16}... | collective-permute-start | bytes 1572872 | tf_op jit(solution)/shard_map/ppermute | solution.py:32
  109.7 10.6 %collective-permute-start.24 = (bf16[512,512]{1,0:T(8,128)(2,1)S(1)}, bf16[512,512]{1,0:T(8,128)(2,1)S(1)}, u32[]{:S(2)}, u32[]{:S(2)}) collective-permute-start(bf16[512,512]{1,0:T(8,128)(2,1)S(1)} %collective-permute-done.21.right), channel_id=1, source_target_pairs={{0,24},{32,38},{64,88},{96,102},{1,25},{33,39},{65,89},{97,103},{8... | collective-permute-start | bytes 1572872 | tf_op jit(solution)/shard_map/ppermute | solution.py:32
  111.7 7.0 %collective-permute-start.27 = (f32[256,256]{1,0:T(8,128)S(1)}, f32[256,256]{1,0:T(8,128)S(1)}, u32[]{:S(2)}, u32[]{:S(2)}) collective-permute-start(f32[256,256]{1,0:T(8,128)S(1)} %get-tuple-element.77.mine), channel_id=1, source_target_pairs={{0,32},{32,0},{64,96},{96,64},{1,33},{33,1},{65,97},{97,65},{8,40}... | collective-permute-start | bytes 786440 | tf_op jit(solution)/shard_map/ppermute | solution.py:32
  114.8 7.2 %collective-permute-start.30 = (bf16[1024,512]{1,0:T(8,128)(2,1)S(1)}, bf16[1024,512]{1,0:T(8,128)(2,1)S(1)}, u32[]{:S(2)}, u32[]{:S(2)}) collective-permute-start(bf16[1024,512]{1,0:T(8,128)(2,1)S(1)} %shard_map.125.refs_1_), channel_id=1, source_target_pairs={{0,32},{32,0},{64,96},{96,64},{1,33},{33,1},{65,97},{97,65},{8,40}... | collective-permute-start | bytes 3145736 | tf_op jit(solution)/shard_map/ppermute | solution.py:32
  116.2 5.8 %collective-permute-start.29 = (bf16[1024,512]{1,0:T(8,128)(2,1)S(1)}, bf16[1024,512]{1,0:T(8,128)(2,1)S(1)}, u32[]{:S(2)}, u32[]{:S(2)}) collective-permute-start(bf16[1024,512]{1,0:T(8,128)(2,1)S(1)} %shard_map.124.refs_0_), channel_id=1, source_target_pairs={{0,32},{32,0},{64,96},{96,64},{1,33},{33,1},{65,97},{97,65},{8,40}... | collective-permute-start | bytes 3145736 | tf_op jit(solution)/shard_map/ppermute | solution.py:32
  120.4 5.2 %collective-permute-start.28 = (bf16[1024,512]{1,0:T(8,128)(2,1)S(1)}, bf16[1024,512]{1,0:T(8,128)(2,1)S(1)}, u32[]{:S(2)}, u32[]{:S(2)}) collective-permute-start(bf16[1024,512]{1,0:T(8,128)(2,1)S(1)} %shard_map.128.refs_2_), channel_id=1, source_target_pairs={{0,32},{32,0},{64,96},{96,64},{1,33},{33,1},{65,97},{97,65},{8,40}... | collective-permute-start | bytes 3145736 | tf_op jit(solution)/shard_map/ppermute | solution.py:32
